TPU v7x, 256 devices: a whole 4x4x8 slice. The times are simulated.
256 devices in a mesh: ctx: 64 (over z, y, core), head: 4 (over x).
Axes of the slice: x: 4, y: 4, z: 8, core: 2. Of those that a mesh axis runs over, the one named last changes fastest.
Arguments:
- queries: bfloat16 [24576, 4096], P(('ctx', 'head')), may hold values from -7 to 7
- keys: bfloat16 [24576, 1024], P(('ctx', 'head')), may hold values from -7 to 7
- values: bfloat16 [24576, 1024], P(('ctx', 'head')), may hold values from -6 to 6
- out_grad: bfloat16 [24576, 4096], P(('ctx', 'head')), may hold values from -6 to 6
- doc_ids: int32 [24576], P('ctx'), may hold values from 0 to 63, never falling along the last dimension, each value on 1 to 1152 neighbouring positions
Outputs:
- attention_out: bfloat16 [24576, 4096], P(('ctx', 'head'))
- query_grad: bfloat16 [24576, 4096], P(('ctx', 'head'))
- key_grad: bfloat16 [24576, 1024], P(('ctx', 'head'))
- value_grad: bfloat16 [24576, 1024], P(('ctx', 'head'))
Inputs may be any that keep to these rules, and one draw needn't show every extreme that they name: `doc_ids`: never falls along the batch; every document has 1 to 1152 tokens, and one has exactly 1152.
All inputs are finite; a program needn't handle non-finite values.
Results may differ from a plain program's by a relative error of at most 0.025.
Values may be sent and summed in bfloat16 or wider, within the bound.
No kernel may reach another device: no remote copies, remote signals or barrier semaphores. Data moves between devices by JAX's collectives and lax.ppermute only.
A program may use at most 128 MiB of HBM per device.

v0:
```python
import jax
import jax.numpy as jnp
from jax import lax
from jax.sharding import PartitionSpec as P

HDIM = 128
REACH = 3


masked_score = -1e30


def shifted(block, axis, distance):
    devices = range(lax.axis_size(axis))
    route = [(i - distance, i) for i in devices if i - distance in devices]
    return lax.ppermute(block, axis, route)


def piece_scores(query_rows, key_piece, allowed, score_scale):
    scores = (
        jnp.einsum("qgrd,kgd->grqk", query_rows, key_piece, preferred_element_type=jnp.float32)
        * score_scale
    )
    return jnp.where(allowed, scores, masked_score)


def piece_weights(scores, allowed, log_total):
    return jnp.where(allowed, jnp.exp(scores - log_total[..., None]), 0.0)


def piece_output(weights_full, value_piece):
    probs_low = weights_full.astype(jnp.bfloat16)
    return jnp.einsum("grqk,kgd->qgrd", probs_low, value_piece, preferred_element_type=jnp.float32)


def piece_grads(weights_full, query_rows, grad_rows, key_piece, value_piece, score_scale, row_dots):
    probs_low = weights_full.astype(jnp.bfloat16)
    value_term = jnp.einsum(
        "grqk,qgrd->kgd", probs_low, grad_rows, preferred_element_type=jnp.float32
    )
    grad_probs = jnp.einsum(
        "qgrd,kgd->grqk", grad_rows, value_piece, preferred_element_type=jnp.float32
    )
    grad_scores = (weights_full * (grad_probs - row_dots[..., None])).astype(jnp.bfloat16)
    query_term = (
        jnp.einsum("grqk,kgd->qgrd", grad_scores, key_piece, preferred_element_type=jnp.float32)
        * score_scale
    )
    key_term = (
        jnp.einsum("grqk,qgrd->kgd", grad_scores, query_rows, preferred_element_type=jnp.float32)
        * score_scale
    )
    return (query_term, key_term, value_term)


def local(queries, keys, values, out_grad, doc_ids):
    query_all, key_all, value_all, grad_all = (
        lax.all_to_all(queries, "head", split_axis=1, concat_axis=0, tiled=True),
        lax.all_to_all(keys, "head", split_axis=1, concat_axis=0, tiled=True),
        lax.all_to_all(values, "head", split_axis=1, concat_axis=0, tiled=True),
        lax.all_to_all(out_grad, "head", split_axis=1, concat_axis=0, tiled=True),
    )
    length = doc_ids.shape[0]
    kv_width = key_all.shape[1]
    kv_heads = kv_width // HDIM
    repeat = query_all.shape[1] // kv_width
    score_scale = HDIM ** (-0.5)
    query_rows = query_all.reshape(length, kv_heads, repeat, HDIM)
    grad_rows = grad_all.reshape(length, kv_heads, repeat, HDIM)
    position = jnp.arange(length)
    ctx_place = lax.axis_index("ctx")
    first_doc = doc_ids[0]
    own_allowed = (doc_ids[:, None] == doc_ids[None, :]) & (position[None, :] <= position[:, None])
    pieces = [
        (
            key_all.reshape(length, kv_heads, HDIM),
            value_all.reshape(length, kv_heads, HDIM),
            own_allowed,
            jnp.array(True),
        )
    ]
    fetched = [
        shifted((key_all, value_all, doc_ids), "ctx", distance) for distance in range(1, REACH + 1)
    ]
    for distance in range(REACH):
        remote_keys, remote_values, remote_docs = fetched[distance]
        present = ctx_place >= distance + 1
        allowed = (doc_ids[:, None] == remote_docs[None, :]) & present
        relevant = present & (remote_docs[length - 1] == first_doc)
        pieces.append(
            (
                remote_keys.reshape(length, kv_heads, HDIM),
                remote_values.reshape(length, kv_heads, HDIM),
                allowed,
                relevant,
            )
        )
    row_shape = (kv_heads, repeat, length)
    out_shape = (length, kv_heads, repeat, HDIM)
    stored_scores = []
    highest = jnp.full(row_shape, masked_score, jnp.float32)
    running_total = jnp.zeros(row_shape, jnp.float32)
    for key_piece, value_piece, allowed, relevant in pieces:
        scores = piece_scores(query_rows, key_piece, allowed, score_scale)
        stored_scores.append(scores)
        piece_high = jnp.max(scores, -1)
        piece_total = jnp.sum(jnp.exp(scores - piece_high[..., None]), -1)
        joined = jnp.maximum(highest, piece_high)
        running_total = running_total * jnp.exp(highest - joined) + piece_total * jnp.exp(
            piece_high - joined
        )
        highest = joined
    log_total = highest + jnp.log(running_total)
    stored_weights = []
    out_sum = jnp.zeros(out_shape, jnp.float32)
    for index in range(len(pieces)):
        key_piece, value_piece, allowed, relevant = pieces[index]
        weights_full = piece_weights(stored_scores[index], allowed, log_total)
        stored_weights.append(weights_full)
        out_sum = out_sum + piece_output(weights_full, value_piece)
    attention = out_sum.astype(jnp.bfloat16)
    row_dots = jnp.transpose(
        jnp.sum(grad_rows.astype(jnp.float32) * attention.astype(jnp.float32), -1), (1, 2, 0)
    )
    query_sum = jnp.zeros(out_shape, jnp.float32)
    key_terms = []
    value_terms = []
    for index in range(len(pieces)):
        key_piece, value_piece, allowed, relevant = pieces[index]
        query_term, key_term, value_term = piece_grads(
            stored_weights[index],
            query_rows,
            grad_rows,
            key_piece,
            value_piece,
            score_scale,
            row_dots,
        )
        query_sum = query_sum + query_term
        key_terms.append(key_term.reshape(length, kv_width))
        value_terms.append(value_term.reshape(length, kv_width))
    remote = [
        jnp.concatenate([key_terms[distance], value_terms[distance]], 1)
        for distance in range(1, REACH + 1)
    ]
    received = jnp.zeros((length, 2 * kv_width), jnp.float32)
    for distance in range(1, REACH + 1):
        received = received + shifted(remote[distance - 1], "ctx", -distance)
    key_total = (key_terms[0] + received[:, :kv_width]).astype(jnp.bfloat16)
    value_total = (value_terms[0] + received[:, kv_width:]).astype(jnp.bfloat16)
    query_total = query_sum.astype(jnp.bfloat16).reshape(length, repeat * kv_width)
    attention_rows = attention.reshape(length, repeat * kv_width)
    return (
        lax.all_to_all(attention_rows, "head", split_axis=0, concat_axis=1, tiled=True),
        lax.all_to_all(query_total, "head", split_axis=0, concat_axis=1, tiled=True),
        lax.all_to_all(key_total, "head", split_axis=0, concat_axis=1, tiled=True),
        lax.all_to_all(value_total, "head", split_axis=0, concat_axis=1, tiled=True),
    )


def solution(mesh):
    return jax.shard_map(
        local,
        mesh=mesh,
        in_specs=(
            P(("ctx", "head"), None),
            P(("ctx", "head"), None),
            P(("ctx", "head"), None),
            P(("ctx", "head"), None),
            P("ctx"),
        ),
        out_specs=(
            P(("ctx", "head"), None),
            P(("ctx", "head"), None),
            P(("ctx", "head"), None),
            P(("ctx", "head"), None),
        ),
        check_vma=False,
    )
```

profile of v0, /device:TPU:96, one launch (start us, length us, event | category | flops | bytes accessed | tf_op | source)
XLA Modules:
  0.0 212.9 jit_solution(7812730977379902750)
XLA Ops:
  2.3 4.3 %all-to-all-start = ((bf16[96,4,256]{2,0,1:T(8,128)(2,1)}), bf16[96,4,256]{2,0,1:T(8,128)(2,1)S(1)}, u32[]{:S(2)}, u32[]{:S(2)}) async-start(bf16[96,4,256]{2,0,1:T(8,128)(2,1)} %bitcast.257), calls=%async_computation | async-start | bytes 393216 | tf_op jit(solution)/shard_map/all_to_all | solution.py:59
  8.3 4.7 %all-to-all-done = bf16[96,4,256]{2,0,1:T(8,128)(2,1)S(1)} async-done(((bf16[96,4,256]{2,0,1:T(8,128)(2,1)}), bf16[96,4,256]{2,0,1:T(8,128)(2,1)S(1)}, u32[]{:S(2)}, u32[]{:S(2)}) %all-to-all-start) | async-done | bytes 196640 | tf_op jit(solution)/shard_map/all_to_all | solution.py:59
  13.0 3.4 %all-to-all-start.2 = ((bf16[96,4,256]{2,0,1:T(8,128)(2,1)}), bf16[96,4,256]{2,0,1:T(8,128)(2,1)S(1)}, u32[]{:S(2)}, u32[]{:S(2)}) async-start(bf16[96,4,256]{2,0,1:T(8,128)(2,1)} %bitcast.258), calls=%async_computation.2 | async-start | bytes 393216 | tf_op jit(solution)/shard_map/all_to_all | solution.py:60
  16.3 2.1 copy.333
  18.4 4.2 %all-to-all-done.2 = bf16[96,4,256]{2,0,1:T(8,128)(2,1)S(1)} async-done(((bf16[96,4,256]{2,0,1:T(8,128)(2,1)}), bf16[96,4,256]{2,0,1:T(8,128)(2,1)S(1)}, u32[]{:S(2)}, u32[]{:S(2)}) %all-to-all-start.2) | async-done | bytes 196640 | tf_op jit(solution)/shard_map/all_to_all | solution.py:60
  22.6 3.5 %all-to-all-start.1 = ((bf16[96,4,1024]{2,0,1:T(8,128)(2,1)}), bf16[96,4,1024]{2,0,1:T(8,128)(2,1)S(1)}, u32[]{:S(2)}, u32[]{:S(2)}) async-start(bf16[96,4,1024]{2,0,1:T(8,128)(2,1)} %bitcast.256), calls=%async_computation.1 | async-start | bytes 1572864 | tf_op jit(solution)/shard_map/all_to_all | solution.py:58
  28.1 5.2 %collective-permute-start = (s32[384]{0:T(512)S(1)}, s32[384]{0:T(512)S(1)}, u32[]{:S(2)}, u32[]{:S(2)}) collective-permute-start(s32[384]{0:T(512)S(1)} %copy-done.19), channel_id=1, source_target_pairs={{0,4},{4,8},{8,12},{12,16},{16,20},{20,24},{24,28},{28,32},{32,36}... | collective-permute-start | bytes 4616 | tf_op jit(solution)/shard_map/ppermute | solution.py:16
  33.3 2.6 %collective-permute-start.2 = (s32[384]{0:T(512)S(1)}, s32[384]{0:T(512)S(1)}, u32[]{:S(2)}, u32[]{:S(2)}) collective-permute-start(s32[384]{0:T(512)S(1)} %copy-done.19), channel_id=1, source_target_pairs={{0,8},{4,12},{8,16},{12,20},{16,24},{20,28},{24,32},{28,36},{32,40... | collective-permute-start | bytes 4616 | tf_op jit(solution)/shard_map/ppermute | solution.py:16
  35.9 3.4 %collective-permute-start.4 = (s32[384]{0:T(512)S(1)}, s32[384]{0:T(512)S(1)}, u32[]{:S(2)}, u32[]{:S(2)}) collective-permute-start(s32[384]{0:T(512)S(1)} %copy-done.19), channel_id=1, source_target_pairs={{0,12},{4,16},{8,20},{12,24},{16,28},{20,32},{24,36},{28,40},{32,4... | collective-permute-start | bytes 4616 | tf_op jit(solution)/shard_map/ppermute | solution.py:16
  40.3 4.1 %collective-permute-start.3 = (bf16[384,256]{1,0:T(8,128)(2,1)S(1)}, bf16[384,256]{1,0:T(8,128)(2,1)S(1)}, u32[]{:S(2)}, u32[]{:S(2)}) collective-permute-start(bf16[384,256]{1,0:T(8,128)(2,1)S(1)} %bitcast.290), channel_id=1, source_target_pairs={{0,8},{4,12},{8,16},{12,20},{16,24},{20,28},{24,32},{28,36},{32,40... | collective-permute-start | bytes 589832 | tf_op jit(solution)/shard_map/ppermute | solution.py:16
  44.4 4.0 %collective-permute-start.1 = (bf16[384,256]{1,0:T(8,128)(2,1)S(1)}, bf16[384,256]{1,0:T(8,128)(2,1)S(1)}, u32[]{:S(2)}, u32[]{:S(2)}) collective-permute-start(bf16[384,256]{1,0:T(8,128)(2,1)S(1)} %bitcast.291), channel_id=1, source_target_pairs={{0,4},{4,8},{8,12},{12,16},{16,20},{20,24},{24,28},{28,32},{32,36}... | collective-permute-start | bytes 589832 | tf_op jit(solution)/shard_map/ppermute | solution.py:16
  48.4 2.1 collective-permute-start.6
  50.5 2.6 %collective-permute-start.7 = (bf16[384,256]{1,0:T(8,128)(2,1)S(1)}, bf16[384,256]{1,0:T(8,128)(2,1)S(1)}, u32[]{:S(2)}, u32[]{:S(2)}) collective-permute-start(bf16[384,256]{1,0:T(8,128)(2,1)S(1)} %bitcast.286), channel_id=1, source_target_pairs={{0,8},{4,12},{8,16},{12,20},{16,24},{20,28},{24,32},{28,36},{32,40... | collective-permute-start | bytes 589832 | tf_op jit(solution)/shard_map/ppermute | solution.py:16
  53.1 4.0 %collective-permute-start.8 = (bf16[384,256]{1,0:T(8,128)(2,1)S(1)}, bf16[384,256]{1,0:T(8,128)(2,1)S(1)}, u32[]{:S(2)}, u32[]{:S(2)}) collective-permute-start(bf16[384,256]{1,0:T(8,128)(2,1)S(1)} %bitcast.287), channel_id=1, source_target_pairs={{0,12},{4,16},{8,20},{12,24},{16,28},{20,32},{24,36},{28,40},{32,4... | collective-permute-start | bytes 589832 | tf_op jit(solution)/shard_map/ppermute | solution.py:16
  65.0 5.2 %all-to-all-start.4 = ((bf16[96,4,1024]{2,0,1:T(8,128)(2,1)}), bf16[96,4,1024]{2,0,1:T(8,128)(2,1)S(1)}, u32[]{:S(2)}, u32[]{:S(2)}) async-start(bf16[96,4,1024]{2,0,1:T(8,128)(2,1)} %bitcast.255), calls=%async_computation.4 | async-start | bytes 1572864 | tf_op jit(solution)/shard_map/all_to_all | solution.py:61
  76.5 2.1 exponential_reduce_fusion
  78.6 2.1 exponential_reduce_fusion.2
  80.8 2.7 %fusion.60 = f32[2,4,384,128]{2,3,1,0:T(8,128)} fusion(bf16[384,2,128,1]{0,2,3,1:T(8,128)(2,1)S(1)} %bitcast.303, f32[2,384,384,4]{2,1,3,0:T(8,128)S(1)} %get-tuple-element.17, f32[2,4,384]{2,1,0:T(4,128)S(1)} %log_add_fusion, pred[384,384]{0,1:T(8,128)(4,1)S(1)} %get-tuple-element.6), kind=kOutput, calls=%fused_computation.98 | convolution fusion | flops 307888128 | bytes 6647808 | tf_op jit(solution)/shard_map/grqk,kgd->qgrd/dot_general | solution.py:33
  83.5 2.7 %fusion.64 = f32[2,4,384,128]{2,3,1,0:T(8,128)} fusion(bf16[384,2,128,1]{0,2,3,1:T(8,128)(2,1)S(1)} %copy-done.12, f32[2,384,384,4]{2,1,3,0:T(8,128)S(1)} %get-tuple-element.13, f32[2,4,384]{2,1,0:T(4,128)S(1)} %log_add_fusion, pred[384,384]{0,1:T(8,128)(4,1)S(1)} %get-tuple-element.9), kind=kOutput, calls=%fused_computation.100 | convolution fusion | flops 307888128 | bytes 6647808 | tf_op jit(solution)/shard_map/grqk,kgd->qgrd/dot_general | solution.py:33
  86.2 2.7 %fusion.56 = f32[2,4,384,128]{2,3,1,0:T(8,128)} fusion(bf16[384,2,128,1]{0,2,3,1:T(8,128)(2,1)S(1)} %bitcast.307, f32[2,384,384,4]{2,1,3,0:T(8,128)S(1)} %get-tuple-element.15, f32[2,4,384]{2,1,0:T(4,128)S(1)} %log_add_fusion, pred[384,384]{0,1:T(8,128)(4,1)S(1)} %get-tuple-element.7), kind=kOutput, calls=%fused_computation.96 | convolution fusion | flops 307888128 | bytes 6647808 | tf_op jit(solution)/shard_map/grqk,kgd->qgrd/dot_general | solution.py:33
  90.5 4.8 %fusion.54 = f32[2,384,128,1]{1,2,3,0:T(8,128)} fusion(bf16[384,2,4,128]{0,3,2,1:T(8,128)(2,1)S(1)} %copy.205, f32[2,384,384,4]{2,1,3,0:T(8,128)} %copy-done.3, f32[2,4,384]{2,1,0:T(4,128)S(1)} %log_add_fusion, pred[384,384]{0,1:T(8,128)(4,1)S(1)} %get-tuple-element.7), kind=kOutput, calls=%fused_computation.95 | convolution fusion | flops 307888128 | bytes 6057984 | tf_op jit(solution)/shard_map/grqk,qgrd->kgd/dot_general | solution.py:38
  95.3 6.4 %multiply_reduce_fusion = (f32[384,2,4]{0,2,1:T(4,128)S(1)}, bf16[384,2,4,128]{0,3,2,1:T(8,128)(2,1)}) fusion(bf16[384,2,4,128]{0,3,2,1:T(8,128)(2,1)S(1)} %copy.205, bf16[384,2,128,1]{0,2,3,1:T(8,128)(2,1)S(1)} %bitcast.305, f32[2,384,384,4]{2,1,3,0:T(8,128)} %copy-done.1, f32[2,4,384]{2,1,0:T(4,128)S(1)} %log_add_fusion, ...), kind=kOutput, calls=%fused_computation.33 | convolution fusion | flops 311030784 | bytes 11378688 | tf_op jit(solution)/shard_map/grqk,kgd->qgrd/dot_general | solution.py:33
  105.3 2.2 %fusion.58 = f32[2,384,128,1]{1,2,3,0:T(8,128)} fusion(bf16[384,2,4,128]{0,3,2,1:T(8,128)(2,1)S(1)} %copy.205, f32[2,384,384,4]{2,1,3,0:T(8,128)S(1)} %bitcast.264, f32[2,4,384]{2,1,0:T(4,128)S(1)} %log_add_fusion, pred[384,384]{0,1:T(8,128)(4,1)S(1)} %get-tuple-element.6), kind=kOutput, calls=%fused_computation.97 | convolution fusion | flops 307888128 | bytes 6057984 | tf_op jit(solution)/shard_map/grqk,qgrd->kgd/dot_general | solution.py:38
  107.5 3.2 %fusion.1 = bf16[2,4,384,384]{2,3,1,0:T(8,128)(2,1)} fusion(f32[2,384,384,4]{2,1,3,0:T(8,128)S(1)} %bitcast.262, f32[2,4,384]{2,1,0:T(4,128)S(1)} %bitcast.313, f32[2,4,384]{2,1,0:T(4,128)S(1)} %log_add_fusion, pred[384,384]{0,1:T(8,128)(4,1)S(1)} %get-tuple-element.8, bf16[384,2,128,1]{0,2,3,1:T(8,128)(2,1)S(1)} %bitcast.306, ...), kind=kOutput, calls=%fused_computation.2 | convolution fusion | flops 310247424 | bytes 8232960 | tf_op jit(solution)/shard_map/qgrd,kgd->grqk/dot_general | solution.py:41
  110.7 2.1 %fusion.48 = f32[2,384,128,1]{1,2,3,0:T(8,128)} fusion(bf16[384,2,4,128]{0,3,2,1:T(8,128)(2,1)S(1)} %copy.205, f32[2,384,384,4]{2,1,3,0:T(8,128)S(1)} %bitcast.262, f32[2,4,384]{2,1,0:T(4,128)S(1)} %log_add_fusion, pred[384,384]{0,1:T(8,128)(4,1)S(1)} %get-tuple-element.8), kind=kOutput, calls=%fused_computation.93 | convolution fusion | flops 307888128 | bytes 6057984 | tf_op jit(solution)/shard_map/grqk,qgrd->kgd/dot_general | solution.py:38
  112.8 3.1 %fusion.7 = bf16[2,4,384,384]{2,3,1,0:T(8,128)(2,1)S(1)} fusion(f32[2,384,384,4]{2,1,3,0:T(8,128)S(1)} %bitcast.260, f32[2,4,384]{2,1,0:T(4,128)S(1)} %bitcast.314, f32[2,4,384]{2,1,0:T(4,128)S(1)} %log_add_fusion, pred[384,384]{0,1:T(8,128)(4,1)S(1)} %get-tuple-element.9, bf16[384,2,128,1]{0,2,3,1:T(8,128)(2,1)S(1)} %copy-done.13, ...), kind=kOutput, calls=%fused_computation.11 | convolution fusion | flops 310247424 | bytes 8232960 | tf_op jit(solution)/shard_map/qgrd,kgd->grqk/dot_general | solution.py:41
  117.6 2.2 %fusion.66 = f32[2,4,384,128]{3,2,1,0:T(8,128)} fusion(bf16[2,4,384,384]{2,3,1,0:T(8,128)(2,1)S(1)} %fusion.5, bf16[384,2,128,1]{0,2,3,1:T(8,128)(2,1)S(1)} %bitcast.274), kind=kOutput, calls=%fused_computation.101 | convolution fusion | flops 301989888 | bytes 4128768 | tf_op jit(solution)/shard_map/grqk,kgd->qgrd/dot_general | solution.py:46
  121.4 2.2 %fusion.67 = f32[2,4,384,128]{3,2,1,0:T(8,128)} fusion(bf16[2,4,384,384]{2,3,1,0:T(8,128)(2,1)S(1)} %fusion.3, bf16[384,2,128,1]{0,2,3,1:T(8,128)(2,1)S(1)} %bitcast.272), kind=kOutput, calls=%fused_computation.102 | convolution fusion | flops 301989888 | bytes 4128768 | tf_op jit(solution)/shard_map/grqk,kgd->qgrd/dot_general | solution.py:46
  127.4 2.1 pad_maximum_fusion.1
  129.5 3.3 %collective-permute-start.10 = (f32[384,512]{1,0:T(8,128)}, f32[384,512]{1,0:T(8,128)}, u32[]{:S(2)}, u32[]{:S(2)}) collective-permute-start(f32[384,512]{1,0:T(8,128)} %pad_maximum_fusion.1), channel_id=1, source_target_pairs={{8,0},{12,4},{16,8},{20,12},{24,16},{28,20},{32,24},{36,28},{40,32... | collective-permute-start | bytes 2359304 | tf_op jit(solution)/shard_map/ppermute | solution.py:16
  136.6 2.1 pad_maximum_fusion
  138.7 2.9 %collective-permute-start.9 = (f32[384,512]{1,0:T(8,128)}, f32[384,512]{1,0:T(8,128)}, u32[]{:S(2)}, u32[]{:S(2)}) collective-permute-start(f32[384,512]{1,0:T(8,128)} %pad_maximum_fusion), channel_id=1, source_target_pairs={{4,0},{8,4},{12,8},{16,12},{20,16},{24,20},{28,24},{32,28},{36,32}... | collective-permute-start | bytes 2359304 | tf_op jit(solution)/shard_map/ppermute | solution.py:16
  141.6 3.2 %fusion.16 = f32[2,384,128]{1,2,0:T(8,128)} fusion(bf16[2,4,384,384]{2,3,1,0:T(8,128)(2,1)} %fusion.1, bf16[384,2,4,128]{0,3,2,1:T(8,128)(2,1)S(1)} %copy.223), kind=kOutput, calls=%fused_computation.36 | convolution fusion | flops 302088192 | bytes 3538944 | tf_op jit(solution)/shard_map/grqk,qgrd->kgd/dot_general | solution.py:50
  150.8 2.6 %fusion.21 = bf16[384,2,4,128]{3,0,2,1:T(8,128)(2,1)S(1)} fusion(f32[2,4,384,128]{3,2,1,0:T(8,128)} %fusion.67, f32[2,4,384,128]{3,2,1,0:T(8,128)S(1)} %fusion.25, f32[2,4,384,128]{3,2,1,0:T(8,128)S(1)} %copy-done.5, bf16[2,4,384,384]{2,3,1,0:T(8,128)(2,1)S(1)} %copy-done.4, bf16[384,2,128,1]{0,2,3,1:T(8,128)(2,1)} %bitcast.276), kind=kOutput, calls=%fused_computation.44 | convolution fusion | flops 303955968 | bytes 8060928 | tf_op jit(solution)/shard_map/grqk,kgd->qgrd/dot_general | solution.py:46
  154.9 2.4 %all_to_all.126 = bf16[4,96,1024]{2,1,0:T(8,128)(2,1)} reshape(bf16[384,2,4,128]{3,2,1,0:T(4,128)(2,1)} %copy.220) | data formatting | bytes 1572864 | tf_op jit(solution)/shard_map/all_to_all | solution.py:155
  157.2 4.5 %all-to-all-start.5 = ((bf16[4,96,1024]{2,1,0:T(8,128)(2,1)}), bf16[4,96,1024]{2,1,0:T(8,128)(2,1)}, u32[]{:S(2)}, u32[]{:S(2)}) async-start(bf16[4,96,1024]{2,1,0:T(8,128)(2,1)} %all_to_all.126), calls=%async_computation.5 | async-start | bytes 1572864 | tf_op jit(solution)/shard_map/all_to_all | solution.py:155
  161.8 2.1 pad_maximum_fusion.2
  163.8 2.7 %collective-permute-start.11 = (f32[384,512]{1,0:T(8,128)}, f32[384,512]{1,0:T(8,128)}, u32[]{:S(2)}, u32[]{:S(2)}) collective-permute-start(f32[384,512]{1,0:T(8,128)} %pad_maximum_fusion.2), channel_id=1, source_target_pairs={{12,0},{16,4},{20,8},{24,12},{28,16},{32,20},{36,24},{40,28},{44,3... | collective-permute-start | bytes 2359304 | tf_op jit(solution)/shard_map/ppermute | solution.py:16
  166.6 2.2 %copy.200 = bf16[384,2,4,128]{3,2,1,0:T(4,128)(2,1)} copy(bf16[384,2,4,128]{0,3,2,1:T(8,128)(2,1)} %get-tuple-element.19) | data formatting | bytes 1572864 | tf_op jit(solution)/shard_map/convert_element_type | solution.py:121
  168.8 2.3 %all_to_all.119 = bf16[4,96,1024]{2,1,0:T(8,128)(2,1)} reshape(bf16[384,2,4,128]{3,2,1,0:T(4,128)(2,1)} %copy.200) | data formatting | bytes 1572864 | tf_op jit(solution)/shard_map/all_to_all | solution.py:154
  171.1 4.7 %fusion.62 = f32[2,384,128,1]{1,2,3,0:T(8,128)} fusion(bf16[384,2,4,128]{0,3,2,1:T(8,128)(2,1)} %copy-done.11, f32[2,384,384,4]{2,1,3,0:T(8,128)} %copy-done, f32[2,4,384]{2,1,0:T(4,128)S(1)} %log_add_fusion, pred[384,384]{0,1:T(8,128)(4,1)S(1)} %get-tuple-element.9), kind=kOutput, calls=%fused_computation.99 | convolution fusion | flops 307888128 | bytes 6057984 | tf_op jit(solution)/shard_map/grqk,qgrd->kgd/dot_general | solution.py:38
  175.8 4.5 %all-to-all-start.3 = ((bf16[4,96,1024]{2,1,0:T(8,128)(2,1)}), bf16[4,96,1024]{2,1,0:T(8,128)(2,1)}, u32[]{:S(2)}, u32[]{:S(2)}) async-start(bf16[4,96,1024]{2,1,0:T(8,128)(2,1)} %all_to_all.119), calls=%async_computation.3 | async-start | bytes 1572864 | tf_op jit(solution)/shard_map/all_to_all | solution.py:154
  182.5 3.3 %collective-permute-done.11 = f32[384,512]{1,0:T(8,128)} collective-permute-done((f32[384,512]{1,0:T(8,128)}, f32[384,512]{1,0:T(8,128)}, u32[]{:S(2)}, u32[]{:S(2)}) %collective-permute-start.11) | collective-permute-done | bytes 786464 | tf_op jit(solution)/shard_map/ppermute | solution.py:16
  188.4 5.3 %all-to-all-done.3 = bf16[4,96,1024]{2,1,0:T(8,128)(2,1)} async-done(((bf16[4,96,1024]{2,1,0:T(8,128)(2,1)}), bf16[4,96,1024]{2,1,0:T(8,128)(2,1)}, u32[]{:S(2)}, u32[]{:S(2)}) %all-to-all-start.3) | async-done | bytes 786464 | tf_op jit(solution)/shard_map/all_to_all | solution.py:154
  193.6 8.7 %all_to_all.146 = bf16[4,96,256]{2,1,0:T(8,128)(2,1)S(1)} all-to-all(bf16[4,96,256]{2,1,0:T(8,128)(2,1)S(1)} %bitcast.296), channel_id=1, replica_groups=mesh['ctx'=64,'head'=4] {'head'}, dimensions={0} | all-to-all | bytes 393216 | tf_op jit(solution)/shard_map/all_to_all | solution.py:156
  202.3 3.4 %all-to-all-start.7 = ((bf16[4,96,256]{2,1,0:T(8,128)(2,1)}), bf16[4,96,256]{2,1,0:T(8,128)(2,1)S(1)}, u32[]{:S(2)}, u32[]{:S(2)}) async-start(bf16[4,96,256]{2,1,0:T(8,128)(2,1)} %bitcast.80), calls=%async_computation.7 | async-start | bytes 393216 | tf_op jit(solution)/shard_map/all_to_all | solution.py:157
  205.7 2.1 copy.319
  207.8 2.1 copy.318
  (117 shorter events, 51.2 us)
Async XLA Ops:
  0.6 27.4 %copy-start.19 = (s32[384]{0:T(512)S(1)}, s32[384]{0:T(512)}, u32[]{:S(2)}) copy-start(s32[384]{0:T(512)} %param.9) | copy-start | bytes 4612
  0.6 38.7 %copy-start.10 = (bf16[96,4096]{1,0:T(8,128)(2,1)S(1)}, bf16[96,4096]{1,0:T(8,128)(2,1)}, u32[]{:S(2)}) copy-start(bf16[96,4096]{1,0:T(8,128)(2,1)} %param.8) | copy-start | bytes 2359300
  2.3 10.6 %all-to-all-start = ((bf16[96,4,256]{2,0,1:T(8,128)(2,1)}), bf16[96,4,256]{2,0,1:T(8,128)(2,1)S(1)}, u32[]{:S(2)}, u32[]{:S(2)}) async-start(bf16[96,4,256]{2,0,1:T(8,128)(2,1)} %bitcast.257), calls=%async_computation | async-start | bytes 393216 | tf_op jit(solution)/shard_map/all_to_all | solution.py:59
  13.0 9.7 %all-to-all-start.2 = ((bf16[96,4,256]{2,0,1:T(8,128)(2,1)}), bf16[96,4,256]{2,0,1:T(8,128)(2,1)S(1)}, u32[]{:S(2)}, u32[]{:S(2)}) async-start(bf16[96,4,256]{2,0,1:T(8,128)(2,1)} %bitcast.258), calls=%async_computation.2 | async-start | bytes 393216 | tf_op jit(solution)/shard_map/all_to_all | solution.py:60
  22.6 42.4 %all-to-all-start.1 = ((bf16[96,4,1024]{2,0,1:T(8,128)(2,1)}), bf16[96,4,1024]{2,0,1:T(8,128)(2,1)S(1)}, u32[]{:S(2)}, u32[]{:S(2)}) async-start(bf16[96,4,1024]{2,0,1:T(8,128)(2,1)} %bitcast.256), calls=%async_computation.1 | async-start | bytes 1572864 | tf_op jit(solution)/shard_map/all_to_all | solution.py:58
  26.1 27.0 %collective-permute-start.5 = (bf16[384,256]{1,0:T(8,128)(2,1)S(1)}, bf16[384,256]{1,0:T(8,128)(2,1)S(1)}, u32[]{:S(2)}, u32[]{:S(2)}) collective-permute-start(bf16[384,256]{1,0:T(8,128)(2,1)S(1)} %bitcast.289), channel_id=1, source_target_pairs={{0,12},{4,16},{8,20},{12,24},{16,28},{20,32},{24,36},{28,40},{32,4... | collective-permute-start | bytes 589832 | tf_op jit(solution)/shard_map/ppermute | solution.py:16
  28.1 16.3 %collective-permute-start = (s32[384]{0:T(512)S(1)}, s32[384]{0:T(512)S(1)}, u32[]{:S(2)}, u32[]{:S(2)}) collective-permute-start(s32[384]{0:T(512)S(1)} %copy-done.19), channel_id=1, source_target_pairs={{0,4},{4,8},{8,12},{12,16},{16,20},{20,24},{24,28},{28,32},{32,36}... | collective-permute-start | bytes 4616 | tf_op jit(solution)/shard_map/ppermute | solution.py:16
  33.3 15.1 %collective-permute-start.2 = (s32[384]{0:T(512)S(1)}, s32[384]{0:T(512)S(1)}, u32[]{:S(2)}, u32[]{:S(2)}) collective-permute-start(s32[384]{0:T(512)S(1)} %copy-done.19), channel_id=1, source_target_pairs={{0,8},{4,12},{8,16},{12,20},{16,24},{20,28},{24,32},{28,36},{32,40... | collective-permute-start | bytes 4616 | tf_op jit(solution)/shard_map/ppermute | solution.py:16
  35.9 14.6 %collective-permute-start.4 = (s32[384]{0:T(512)S(1)}, s32[384]{0:T(512)S(1)}, u32[]{:S(2)}, u32[]{:S(2)}) collective-permute-start(s32[384]{0:T(512)S(1)} %copy-done.19), channel_id=1, source_target_pairs={{0,12},{4,16},{8,20},{12,24},{16,28},{20,32},{24,36},{28,40},{32,4... | collective-permute-start | bytes 4616 | tf_op jit(solution)/shard_map/ppermute | solution.py:16
  40.3 19.1 %collective-permute-start.3 = (bf16[384,256]{1,0:T(8,128)(2,1)S(1)}, bf16[384,256]{1,0:T(8,128)(2,1)S(1)}, u32[]{:S(2)}, u32[]{:S(2)}) collective-permute-start(bf16[384,256]{1,0:T(8,128)(2,1)S(1)} %bitcast.290), channel_id=1, source_target_pairs={{0,8},{4,12},{8,16},{12,20},{16,24},{20,28},{24,32},{28,36},{32,40... | collective-permute-start | bytes 589832 | tf_op jit(solution)/shard_map/ppermute | solution.py:16
  44.4 15.2 %collective-permute-start.1 = (bf16[384,256]{1,0:T(8,128)(2,1)S(1)}, bf16[384,256]{1,0:T(8,128)(2,1)S(1)}, u32[]{:S(2)}, u32[]{:S(2)}) collective-permute-start(bf16[384,256]{1,0:T(8,128)(2,1)S(1)} %bitcast.291), channel_id=1, source_target_pairs={{0,4},{4,8},{8,12},{12,16},{16,20},{20,24},{24,28},{28,32},{32,36}... | collective-permute-start | bytes 589832 | tf_op jit(solution)/shard_map/ppermute | solution.py:16
  48.4 12.0 %collective-permute-start.6 = (bf16[384,256]{1,0:T(8,128)(2,1)S(1)}, bf16[384,256]{1,0:T(8,128)(2,1)S(1)}, u32[]{:S(2)}, u32[]{:S(2)}) collective-permute-start(bf16[384,256]{1,0:T(8,128)(2,1)S(1)} %bitcast.285), channel_id=1, source_target_pairs={{0,4},{4,8},{8,12},{12,16},{16,20},{20,24},{24,28},{28,32},{32,36}... | collective-permute-start | bytes 589832 | tf_op jit(solution)/shard_map/ppermute | solution.py:16
  50.5 12.8 %collective-permute-start.7 = (bf16[384,256]{1,0:T(8,128)(2,1)S(1)}, bf16[384,256]{1,0:T(8,128)(2,1)S(1)}, u32[]{:S(2)}, u32[]{:S(2)}) collective-permute-start(bf16[384,256]{1,0:T(8,128)(2,1)S(1)} %bitcast.286), channel_id=1, source_target_pairs={{0,8},{4,12},{8,16},{12,20},{16,24},{20,28},{24,32},{28,36},{32,40... | collective-permute-start | bytes 589832 | tf_op jit(solution)/shard_map/ppermute | solution.py:16
  53.1 11.1 %collective-permute-start.8 = (bf16[384,256]{1,0:T(8,128)(2,1)S(1)}, bf16[384,256]{1,0:T(8,128)(2,1)S(1)}, u32[]{:S(2)}, u32[]{:S(2)}) collective-permute-start(bf16[384,256]{1,0:T(8,128)(2,1)S(1)} %bitcast.287), channel_id=1, source_target_pairs={{0,12},{4,16},{8,20},{12,24},{16,28},{20,32},{24,36},{28,40},{32,4... | collective-permute-start | bytes 589832 | tf_op jit(solution)/shard_map/ppermute | solution.py:16
  59.6 14.0 %copy-start.6 = (bf16[384,256]{0,1:T(8,128)(2,1)}, bf16[384,256]{0,1:T(8,128)(2,1)S(1)}, u32[]{:S(2)}) copy-start(bf16[384,256]{0,1:T(8,128)(2,1)S(1)} %copy.185) | copy-start | bytes 589828
  65.0 23.9 %all-to-all-start.4 = ((bf16[96,4,1024]{2,0,1:T(8,128)(2,1)}), bf16[96,4,1024]{2,0,1:T(8,128)(2,1)S(1)}, u32[]{:S(2)}, u32[]{:S(2)}) async-start(bf16[96,4,1024]{2,0,1:T(8,128)(2,1)} %bitcast.255), calls=%async_computation.4 | async-start | bytes 1572864 | tf_op jit(solution)/shard_map/all_to_all | solution.py:61
  71.6 2.9 %copy-start.8 = (bf16[384,256]{0,1:T(8,128)(2,1)S(1)}, bf16[384,256]{0,1:T(8,128)(2,1)}, u32[]{:S(2)}) copy-start(bf16[384,256]{0,1:T(8,128)(2,1)} %copy.182) | copy-start | bytes 589828
  73.6 2.9 %copy-start.1 = (f32[2,384,384,4]{2,1,3,0:T(8,128)}, f32[2,384,384,4]{2,1,3,0:T(8,128)S(1)}, u32[]{:S(2)}) copy-start(f32[2,384,384,4]{2,1,3,0:T(8,128)S(1)} %get-tuple-element.11) | copy-start | bytes 14155780
  74.6 11.6 %copy-start.3 = (f32[2,384,384,4]{2,1,3,0:T(8,128)}, f32[2,384,384,4]{2,1,3,0:T(8,128)S(1)}, u32[]{:S(2)}) copy-start(f32[2,384,384,4]{2,1,3,0:T(8,128)S(1)} %get-tuple-element.15) | copy-start | bytes 14155780
  75.6 5.2 %copy-start.2 = (f32[2,384,384,4]{2,1,3,0:T(8,128)}, f32[2,384,384,4]{2,1,3,0:T(8,128)S(1)}, u32[]{:S(2)}) copy-start(f32[2,384,384,4]{2,1,3,0:T(8,128)S(1)} %get-tuple-element.17) | copy-start | bytes 14155780
  76.5 7.0 %copy-start = (f32[2,384,384,4]{2,1,3,0:T(8,128)}, f32[2,384,384,4]{2,1,3,0:T(8,128)S(1)}, u32[]{:S(2)}) copy-start(f32[2,384,384,4]{2,1,3,0:T(8,128)S(1)} %get-tuple-element.13) | copy-start | bytes 14155780
  78.6 2.2 %copy-start.14 = (bf16[384,256]{0,1:T(8,128)(2,1)S(1)}, bf16[384,256]{0,1:T(8,128)(2,1)}, u32[]{:S(2)}) copy-start(bf16[384,256]{0,1:T(8,128)(2,1)} %copy.194) | copy-start | bytes 589828
  80.7 2.8 %copy-start.12 = (bf16[384,2,128,1]{0,2,3,1:T(8,128)(2,1)S(1)}, bf16[384,2,128,1]{0,2,3,1:T(8,128)(2,1)}, u32[]{:S(2)}) copy-start(bf16[384,2,128,1]{0,2,3,1:T(8,128)(2,1)} %copy.253) | copy-start | bytes 589828
  83.5 2.7 %copy-start.17 = (bf16[384,256]{0,1:T(8,128)(2,1)S(1)}, bf16[384,256]{0,1:T(8,128)(2,1)}, u32[]{:S(2)}) copy-start(bf16[384,256]{0,1:T(8,128)(2,1)} %copy.196) | copy-start | bytes 589828
  90.5 20.2 %copy-start.11 = (bf16[384,2,4,128]{0,3,2,1:T(8,128)(2,1)}, bf16[384,2,4,128]{0,3,2,1:T(8,128)(2,1)S(1)}, u32[]{:S(2)}) copy-start(bf16[384,2,4,128]{0,3,2,1:T(8,128)(2,1)S(1)} %copy.205) | copy-start | bytes 2359300
  90.5 4.9 %copy-start.16 = (bf16[384,256]{0,1:T(8,128)(2,1)S(1)}, bf16[384,256]{0,1:T(8,128)(2,1)}, u32[]{:S(2)}) copy-start(bf16[384,256]{0,1:T(8,128)(2,1)} %copy.198) | copy-start | bytes 589828
  90.5 11.2 %slice-start.6 = ((s8[4718592]{0:T(1024)(128)(4,1)}), s8[4194304]{0:T(1024)(128)(4,1)S(1)}, s32[]{:S(2)}) async-start(s8[4718592]{0:T(1024)(128)(4,1)} %bitcast.265), calls=%async_computation.14 | async-start | bytes 8388608
  90.5 13.0 %slice-start.4 = ((s8[4718592]{0:T(1024)(128)(4,1)}), s8[4194304]{0:T(1024)(128)(4,1)S(1)}, s32[]{:S(2)}) async-start(s8[4718592]{0:T(1024)(128)(4,1)} %bitcast.263), calls=%async_computation.12 | async-start | bytes 8388608
  95.3 6.4 %slice-start.7 = ((s8[4718592]{0:T(1024)(128)(4,1)}), s8[524288]{0:T(1024)(128)(4,1)S(1)}, s32[]{:S(2)}) async-start(s8[4718592]{0:T(1024)(128)(4,1)} %bitcast.265), calls=%async_computation.15 | async-start | bytes 1048576
  95.3 6.4 %copy-start.18 = (bf16[384,256]{0,1:T(8,128)(2,1)S(1)}, bf16[384,256]{0,1:T(8,128)(2,1)}, u32[]{:S(2)}) copy-start(bf16[384,256]{0,1:T(8,128)(2,1)} %copy.196) | copy-start | bytes 589828
  95.3 8.2 %slice-start.5 = ((s8[4718592]{0:T(1024)(128)(4,1)}), s8[524288]{0:T(1024)(128)(4,1)S(1)}, s32[]{:S(2)}) async-start(s8[4718592]{0:T(1024)(128)(4,1)} %bitcast.263), calls=%async_computation.13 | async-start | bytes 1048576
  101.7 1.8 copy-start.15
  101.7 5.7 %slice-start.2 = ((s8[4718592]{0:T(1024)(128)(4,1)}), s8[4194304]{0:T(1024)(128)(4,1)S(1)}, s32[]{:S(2)}) async-start(s8[4718592]{0:T(1024)(128)(4,1)} %bitcast.261), calls=%async_computation.10 | async-start | bytes 8388608
  103.5 3.9 %slice-start.3 = ((s8[4718592]{0:T(1024)(128)(4,1)}), s8[524288]{0:T(1024)(128)(4,1)S(1)}, s32[]{:S(2)}) async-start(s8[4718592]{0:T(1024)(128)(4,1)} %bitcast.261), calls=%async_computation.11 | async-start | bytes 1048576
  105.3 7.5 %slice-start = ((s8[4718592]{0:T(1024)(128)(4,1)}), s8[4194304]{0:T(1024)(128)(4,1)S(1)}, s32[]{:S(2)}) async-start(s8[4718592]{0:T(1024)(128)(4,1)} %bitcast.259), calls=%async_computation.8 | async-start | bytes 8388608
  107.5 5.4 %slice-start.1 = ((s8[4718592]{0:T(1024)(128)(4,1)}), s8[524288]{0:T(1024)(128)(4,1)S(1)}, s32[]{:S(2)}) async-start(s8[4718592]{0:T(1024)(128)(4,1)} %bitcast.259), calls=%async_computation.9 | async-start | bytes 1048576
  110.7 2.2 %copy-start.13 = (bf16[384,2,128,1]{0,2,3,1:T(8,128)(2,1)S(1)}, bf16[384,2,128,1]{0,2,3,1:T(8,128)(2,1)}, u32[]{:S(2)}) copy-start(bf16[384,2,128,1]{0,2,3,1:T(8,128)(2,1)} %copy.253) | copy-start | bytes 589828
  112.8 4.7 %copy-start.9 = (bf16[384,256]{0,1:T(8,128)(2,1)S(1)}, bf16[384,256]{0,1:T(8,128)(2,1)}, u32[]{:S(2)}) copy-start(bf16[384,256]{0,1:T(8,128)(2,1)} %copy.182) | copy-start | bytes 589828
  116.0 5.4 %copy-start.7 = (bf16[384,256]{0,1:T(8,128)(2,1)S(1)}, bf16[384,256]{0,1:T(8,128)(2,1)}, u32[]{:S(2)}) copy-start(bf16[384,256]{0,1:T(8,128)(2,1)} %copy-done.6) | copy-start | bytes 589828
  129.5 53.0 %collective-permute-start.10 = (f32[384,512]{1,0:T(8,128)}, f32[384,512]{1,0:T(8,128)}, u32[]{:S(2)}, u32[]{:S(2)}) collective-permute-start(f32[384,512]{1,0:T(8,128)} %pad_maximum_fusion.1), channel_id=1, source_target_pairs={{8,0},{12,4},{16,8},{20,12},{24,16},{28,20},{32,24},{36,28},{40,32... | collective-permute-start | bytes 2359304 | tf_op jit(solution)/shard_map/ppermute | solution.py:16
  138.7 43.8 %collective-permute-start.9 = (f32[384,512]{1,0:T(8,128)}, f32[384,512]{1,0:T(8,128)}, u32[]{:S(2)}, u32[]{:S(2)}) collective-permute-start(f32[384,512]{1,0:T(8,128)} %pad_maximum_fusion), channel_id=1, source_target_pairs={{4,0},{8,4},{12,8},{16,12},{20,16},{24,20},{28,24},{32,28},{36,32}... | collective-permute-start | bytes 2359304 | tf_op jit(solution)/shard_map/ppermute | solution.py:16
  148.7 1.7 copy-start.4
  148.7 2.1 copy-start.5
  157.2 18.6 %all-to-all-start.5 = ((bf16[4,96,1024]{2,1,0:T(8,128)(2,1)}), bf16[4,96,1024]{2,1,0:T(8,128)(2,1)}, u32[]{:S(2)}, u32[]{:S(2)}) async-start(bf16[4,96,1024]{2,1,0:T(8,128)(2,1)} %all_to_all.126), calls=%async_computation.5 | async-start | bytes 1572864 | tf_op jit(solution)/shard_map/all_to_all | solution.py:155
  163.8 21.9 %collective-permute-start.11 = (f32[384,512]{1,0:T(8,128)}, f32[384,512]{1,0:T(8,128)}, u32[]{:S(2)}, u32[]{:S(2)}) collective-permute-start(f32[384,512]{1,0:T(8,128)} %pad_maximum_fusion.2), channel_id=1, source_target_pairs={{12,0},{16,4},{20,8},{24,12},{28,16},{32,20},{36,24},{40,28},{44,3... | collective-permute-start | bytes 2359304 | tf_op jit(solution)/shard_map/ppermute | solution.py:16
  175.8 17.9 %all-to-all-start.3 = ((bf16[4,96,1024]{2,1,0:T(8,128)(2,1)}), bf16[4,96,1024]{2,1,0:T(8,128)(2,1)}, u32[]{:S(2)}, u32[]{:S(2)}) async-start(bf16[4,96,1024]{2,1,0:T(8,128)(2,1)} %all_to_all.119), calls=%async_computation.3 | async-start | bytes 1572864 | tf_op jit(solution)/shard_map/all_to_all | solution.py:154
  202.3 9.7 %all-to-all-start.7 = ((bf16[4,96,256]{2,1,0:T(8,128)(2,1)}), bf16[4,96,256]{2,1,0:T(8,128)(2,1)S(1)}, u32[]{:S(2)}, u32[]{:S(2)}) async-start(bf16[4,96,256]{2,1,0:T(8,128)(2,1)} %bitcast.80), calls=%async_computation.7 | async-start | bytes 393216 | tf_op jit(solution)/shard_map/all_to_all | solution.py:157
where the time goes:
time: 217 us; the launch traced here: 213 us
  starting transfers between devices  67.6 us (31%)
  matrix products  58 us (27%)
  local copies, waits for them, and re-layouts  42.4 us (20%)
  waiting for transfers between devices  21.1 us (10%)
  other arithmetic  13.6 us (6%)
  blocking collectives  8.68 us (4%)
    ppermute x12, starting transfers between devices, shifted(): return lax.ppermute(block, axis, route)  38.8 us
    dot_general x4, matrix products, piece_output(): jnp.einsum('grqk,kgd->qgrd', probs_low, value_piece, preferred_element_ty...  14.4 us
    dot_general x4, matrix products, piece_grads(): jnp.einsum('grqk,qgrd->kgd', probs_low, grad_rows, preferred_element_type...  13.8 us
    dot_general x4, matrix products, piece_grads(): jnp.einsum('qgrd,kgd->grqk', grad_rows, value_piece, preferred_element_ty...  9.79 us
    all_to_all x1, blocking collectives, local(): lax.all_to_all(key_total, 'head', split_axis=0, concat_axis=1, tiled=True)  8.68 us
    dot_general x4, matrix products, piece_grads(): jnp.einsum('grqk,kgd->qgrd', grad_scores, key_piece, preferred_element_ty...  8.01 us
    dot_general x4, matrix products, piece_grads(): jnp.einsum('grqk,qgrd->kgd', grad_scores, query_rows, preferred_element_t...  7.22 us
    reshape x4, local copies, waits for them, and re-layouts, local(): value_terms.append(value_term.reshape(length, kv_width))  6.89 us
  transfers between devices with their start and end apart: 19, of which 7 were waited for; matrix products, arithmetic and copies ran while one was open for 31% of the time, Pallas kernels for 0%

commit v1 on v0

v1 whole, which is shorter than its diff:
```python
import functools
import math

import jax
import jax.numpy as jnp
from jax import lax
from jax.experimental import pallas as pl
from jax.experimental.pallas import tpu as pltpu
from jax.sharding import Mesh, PartitionSpec as P

HDIM = 128
ROWS = 384
PART = 96
HEADS = 8
QW = HEADS * HDIM
KVW = 4 * HDIM
WINDOW = 4 * ROWS
TILE = 128
KT = 256
MASKED = -1e30
SCALE = HDIM**-0.5
EXP_SCALE = SCALE * math.log2(math.e)
ANY = pl.BlockSpec(memory_space=pl.ANY)
SMEM = pl.BlockSpec(memory_space=pltpu.SMEM)
VMEM = pl.BlockSpec(memory_space=pltpu.VMEM)
BF16, F32 = jnp.bfloat16, jnp.float32


def struct(shape, dtype):
    return jax.ShapeDtypeStruct(shape, dtype)


def run_copies(copies):
    for copy in copies:
        copy.start()
    for copy in copies:
        copy.wait()


def copier(sems):
    count = [0]

    def make(src, dst):
        count[0] += 1
        return pltpu.make_async_copy(src, dst, sems.at[count[0] - 1])

    return make


def pack_kernel(width, x_ref, a_ref, b_ref, *refs):
    outs, sems = refs[:3], refs[3]
    make = copier(sems)
    copies = []
    for p in range(1, 4):
        place = pl.multiple_of(lax.rem(x_ref[0] + p, 4) * width, width)
        for n, src in enumerate((a_ref, b_ref)):
            copies.append(make(src.at[:, pl.ds(place, width)], outs[p - 1].at[:, pl.ds(n * width, width)]))
    run_copies(copies)


def pack(x, a, b):
    width = a.shape[1] // 4
    piece = struct((PART, 2 * width), BF16)
    return pl.pallas_call(
        functools.partial(pack_kernel, width),
        in_specs=[SMEM, ANY, ANY],
        out_specs=[VMEM] * 3,
        out_shape=[piece] * 3,
        scratch_shapes=[pltpu.SemaphoreType.DMA((6,))],
        name="pack",
    )(x, a, b)


def unpack_kernel(width, x_ref, *refs):
    pieces, outs, sems = refs[:4], refs[4:6], refs[6]
    make = copier(sems)
    copies = []
    for p in range(4):
        place = pl.multiple_of(lax.rem(x_ref[0] + 4 - p, 4) * width, width)
        for n, out in enumerate(outs):
            copies.append(make(pieces[p].at[:, pl.ds(n * width, width)], out.at[:, pl.ds(place, width)]))
    run_copies(copies)


def unpack(x, pieces):
    width = pieces[0].shape[1] // 2
    whole = struct((PART, 4 * width), BF16)
    return pl.pallas_call(
        functools.partial(unpack_kernel, width),
        in_specs=[SMEM] + [ANY] * 4,
        out_specs=[VMEM] * 2,
        out_shape=[whole] * 2,
        scratch_shapes=[pltpu.SemaphoreType.DMA((8,))],
        name="unpack",
    )(x, *pieces)


def arrange_kernel(x_ref, k_ref, v_ref, r1, r2, r3, doc_ref, out_ref, sems):
    make = copier(sems)
    x = x_ref[0]
    half = KVW // 2
    own = pl.multiple_of(x * half, half)
    rows = pl.ds(pl.multiple_of(x * PART, PART), PART)
    copies = [
        make(k_ref.at[:, pl.ds(own, half)], out_ref.at[rows, pl.ds(0, half)]),
        make(v_ref.at[:, pl.ds(own, half)], out_ref.at[rows, pl.ds(half, half)]),
        make(doc_ref, out_ref.at[pl.ds(ROWS, 16)]),
    ]
    for p, ref in enumerate((r1, r2, r3)):
        place = pl.multiple_of(lax.rem(x + 3 - p, 4) * PART, PART)
        copies.append(make(ref, out_ref.at[pl.ds(place, PART)]))
    run_copies(copies)


def arrange(x, keys, values, received, docs):
    return pl.pallas_call(
        arrange_kernel,
        in_specs=[SMEM] + [ANY] * 6,
        out_specs=VMEM,
        out_shape=struct((ROWS + 16, KVW), BF16),
        scratch_shapes=[pltpu.SemaphoreType.DMA((6,))],
        name="arrange",
    )(x, keys, values, *received, docs)


def dot(a, b, contract):
    return lax.dot_general(a, b, ((contract[:1], contract[1:]), ((), ())), preferred_element_type=F32)


def attention_kernel(
    x_ref, q_ref, do_ref, q1, q2, q3, kv0, kv_b, kv_c, kv_a, docs_ref,
    o0, o1, o2, o3, own_ref, far_ref, swap_ref, next_ref,
    kv, docs_kv, qd, out, acc, s_scr, p_scr, kvt, doc_col, sems,
):
    make = copier(sems)
    x, core = x_ref[0], x_ref[1]
    slot_b, slot_a = jnp.where(core == 0, 0, 2), jnp.where(core == 0, 2, 0)
    copies = []
    for ref, slot in ((kv0, 3), (kv_c, 1), (kv_b, slot_b), (kv_a, slot_a)):
        copies.append(make(ref.at[pl.ds(0, ROWS)], kv.at[pl.ds(pl.multiple_of(slot * ROWS, ROWS), ROWS)]))
        copies.append(make(ref.at[pl.ds(ROWS, 16)], docs_kv.at[slot]))
    rows = pl.ds(pl.multiple_of(x * PART, PART), PART)
    own = pl.multiple_of(x * QW, QW)
    for n, ref in enumerate((q_ref, do_ref)):
        copies.append(make(ref.at[:, pl.ds(own, QW)], qd.at[rows, pl.ds(n * QW, QW)]))
    for p, ref in enumerate((q1, q2, q3)):
        place = pl.multiple_of(lax.rem(x + 3 - p, 4) * PART, PART)
        copies.append(make(ref, qd.at[pl.ds(place, PART)]))
    for copy in copies:
        copy.start()
    acc[...] = jnp.zeros_like(acc)
    for copy in copies:
        copy.wait()

    eye = (
        lax.broadcasted_iota(jnp.int32, (HDIM, HDIM), 0) == lax.broadcasted_iota(jnp.int32, (HDIM, HDIM), 1)
    ).astype(BF16)
    key_docs = jnp.concatenate([docs_kv[s][0:1, 0:ROWS] for s in range(4)], 1).astype(F32)
    row_docs = docs_ref[...]
    first_tile = []
    for i in range(ROWS // TILE):
        first = row_docs[0:1, i * TILE : i * TILE + 1]
        earlier = jnp.sum((key_docs < first).astype(F32)).astype(jnp.int32)
        first_tile.append(earlier // KT)
    column = jnp.transpose(jnp.broadcast_to(key_docs, (TILE, WINDOW)))
    for t in range(WINDOW // KT):

        @pl.when(t >= first_tile[0])
        def _():
            keys_at = pl.ds(t * KT, KT)
            for n in range(4):
                kvt[n, :, keys_at] = dot(eye, kv[keys_at, n * HDIM : (n + 1) * HDIM], (1, 1)).astype(BF16)

    doc_col[...] = column

    for g in range(2):
        k_cols = slice(g * HDIM, (g + 1) * HDIM)
        v_cols = slice((2 + g) * HDIM, (3 + g) * HDIM)
        for i in range(ROWS // TILE):
            tile_rows = slice(i * TILE, (i + 1) * TILE)
            heads = [(4 * g + r) * HDIM for r in range(4)]
            q = jnp.concatenate([qd[tile_rows, c : c + HDIM] for c in heads], 0)
            do = jnp.concatenate([qd[tile_rows, QW + c : QW + c + HDIM] for c in heads], 0)
            docs_row = row_docs[0:1, i * TILE : (i + 1) * TILE]
            last = (3 * ROWS + (i + 1) * TILE - 1) // KT
            lo, hi = first_tile[i], last + 1
            width = 4 * TILE

            def score(t, high):
                at = pl.ds(pl.multiple_of(t * KT, KT), KT)
                s = dot(kv[at, k_cols], q, (1, 1))
                key_at = lax.broadcasted_iota(jnp.int32, (KT, TILE), 0) + t * KT
                row_at = lax.broadcasted_iota(jnp.int32, (KT, TILE), 1) + (3 * ROWS + i * TILE)
                allowed = (doc_col[at, :] == docs_row) & (key_at <= row_at)
                s = jnp.concatenate(
                    [jnp.where(allowed, s[:, r * TILE : (r + 1) * TILE], MASKED) for r in range(4)], 1
                )
                s_scr[t] = s
                return jnp.maximum(high, jnp.max(s, 0, keepdims=True))

            high = lax.fori_loop(lo, hi, score, jnp.full((1, width), MASKED, F32))
            shift = high * EXP_SCALE

            def weigh(t, carry):
                total, o_t = carry
                at = pl.ds(pl.multiple_of(t * KT, KT), KT)
                e = jnp.exp2(s_scr[t] * EXP_SCALE - shift)
                low = e.astype(BF16)
                p_scr[t] = low
                o_t = o_t + dot(kvt[2 + g, :, at], low, (1, 0))
                return total + jnp.sum(e, 0, keepdims=True), o_t

            total, o_t = lax.fori_loop(
                lo, hi, weigh, (jnp.zeros((1, width), F32), jnp.zeros((HDIM, width), F32))
            )
            inverse = 1.0 / total
            o_t = (o_t * inverse).astype(BF16).astype(F32)
            do_t = dot(eye, do, (1, 1))
            dots = jnp.sum(do_t * o_t, 0, keepdims=True)

            def back(t, dq_t):
                at = pl.ds(pl.multiple_of(t * KT, KT), KT)
                probs = p_scr[t].astype(F32) * inverse
                dp = dot(kv[at, v_cols], do, (1, 1))
                ds = (probs * (dp - dots)).astype(BF16)
                acc[at, v_cols] += dot(probs.astype(BF16), do, (1, 0))
                acc[at, k_cols] += dot(ds, q, (1, 0))
                return dq_t + dot(kvt[g, :, at], ds, (1, 0))

            dq_t = lax.fori_loop(lo, hi, back, jnp.zeros((HDIM, width), F32)) * SCALE
            for r in range(4):
                lanes = slice(r * TILE, (r + 1) * TILE)
                out[tile_rows, heads[r] : heads[r] + HDIM] = jnp.transpose(o_t[:, lanes]).astype(BF16)
                out[tile_rows, QW + heads[r] : QW + heads[r] + HDIM] = jnp.transpose(dq_t[:, lanes]).astype(BF16)

    copies = []
    for p, ref in enumerate((o0, o1, o2, o3)):
        place = pl.multiple_of(lax.rem(x + p, 4) * PART, PART)
        copies.append(make(out.at[pl.ds(place, PART)], ref))
    for copy in copies:
        copy.start()
    half = KVW // 2

    def gradient(slot):
        part = acc[pl.ds(pl.multiple_of(slot * ROWS, ROWS), ROWS), :]
        return jnp.concatenate([part[:, :half] * SCALE, part[:, half:]], 1)

    own_ref[...] = gradient(3)
    next_ref[...] = gradient(1)
    far_ref[...] = gradient(slot_b).astype(BF16)
    swap_ref[...] = gradient(slot_a).astype(BF16)
    for copy in copies:
        copy.wait()


def attention(place, queries, out_grad, received, kv0, kv_b, kv_c, kv_a, docs):
    piece = struct((PART, 2 * QW), BF16)
    tiles = WINDOW // KT
    return pl.pallas_call(
        attention_kernel,
        in_specs=[SMEM] + [ANY] * 9 + [VMEM],
        out_specs=[ANY] * 4 + [VMEM] * 4,
        out_shape=[piece] * 4
        + [struct((ROWS, KVW), F32), struct((ROWS, KVW), BF16), struct((ROWS, KVW), BF16), struct((ROWS, KVW), F32)],
        scratch_shapes=[
            pltpu.VMEM((WINDOW, KVW), BF16),
            pltpu.VMEM((4, 16, KVW), BF16),
            pltpu.VMEM((ROWS, 2 * QW), BF16),
            pltpu.VMEM((ROWS, 2 * QW), BF16),
            pltpu.VMEM((WINDOW, KVW), F32),
            pltpu.VMEM((tiles, KT, 4 * TILE), F32),
            pltpu.VMEM((tiles, KT, 4 * TILE), BF16),
            pltpu.VMEM((4, HDIM, WINDOW), BF16),
            pltpu.VMEM((WINDOW, TILE), F32),
            pltpu.SemaphoreType.DMA((20,)),
        ],
        compiler_params=pltpu.CompilerParams(vmem_limit_bytes=40 * 1024 * 1024),
        cost_estimate=pl.CostEstimate(flops=8_000_000_000, bytes_accessed=8_000_000, transcendentals=4_000_000),
        name="attention",
    )(place, queries, out_grad, *received, kv0, kv_b, kv_c, kv_a, docs)


def around(block, distance):
    return lax.ppermute(block, "head", [(i, (i + distance) % 4) for i in range(4)])


def over_chips(block, routes):
    chips = lax.axis_size("chip")
    pairs = [
        (2 * c + k, 2 * (c + step) + to)
        for c in range(chips)
        for k, step, to in routes
        if 0 <= c + step < chips
    ]
    return lax.ppermute(block, ("chip", "core"), pairs)


def local(queries, keys, values, out_grad, doc_ids):
    x = lax.axis_index("head")
    place = jnp.stack([x, lax.axis_index("core")]).astype(jnp.int32)
    doc_number = doc_ids + 1
    docs_low = jnp.pad(doc_number.astype(BF16)[None, :], ((0, 15), (0, KVW - ROWS)))
    docs = jnp.broadcast_to(doc_number.astype(F32)[None, :], (8, ROWS))
    kv_pieces = pack(place, keys, values)
    kv_received = [around(piece, p + 1) for p, piece in enumerate(kv_pieces)]
    q_pieces = pack(place, queries, out_grad)
    q_received = [around(piece, p + 1) for p, piece in enumerate(q_pieces)]
    kv0 = arrange(place, keys, values, kv_received, docs_low)
    kv_c = over_chips(kv0, [(0, 1, 0), (1, 1, 1)])
    kv_b = over_chips(kv0, [(0, 0, 1), (1, 2, 0)])
    kv_a = over_chips(kv_c, [(0, 0, 1), (1, 0, 0)])
    o0, o1, o2, o3, own, far, swap, near = attention(
        place, queries, out_grad, q_received, kv0, kv_b, kv_c, kv_a, docs
    )
    back_a = over_chips(swap, [(0, 0, 1), (1, 0, 0)])
    near = (near + back_a.astype(F32)).astype(BF16)
    back_c = over_chips(near, [(0, -1, 0), (1, -1, 1)])
    back_b = over_chips(far, [(1, 0, 0), (0, -2, 1)])
    outs = [o0] + [around(piece, p) for p, piece in ((1, o1), (2, o2), (3, o3))]
    attention_out, query_grad = unpack(place, outs)
    total = (own + back_b.astype(F32) + back_c.astype(F32)).astype(BF16)
    parts = [lax.dynamic_slice_in_dim(total, (x + p) % 4 * PART, PART, 0) for p in range(4)]
    grads = [parts[0]] + [around(parts[p], p) for p in (1, 2, 3)]
    key_grad, value_grad = unpack(place, grads)
    return attention_out, query_grad, key_grad, value_grad


def solution(mesh):
    chips = mesh.devices.size // 8
    mesh = Mesh(mesh.devices.reshape(chips, 2, 4), ("chip", "core", "head"))
    rows = P(("chip", "core", "head"), None)
    return jax.shard_map(
        local,
        mesh=mesh,
        in_specs=(rows, rows, rows, rows, P(("chip", "core"))),
        out_specs=(rows, rows, rows, rows),
        check_vma=False,
    )
```

time: 217 us -> 134 us (0.62)
  the two profiles are of different devices: /device:TPU:96 before, /device:TPU:128 now
where the time goes in v1:
time: 134 us; the launch traced here: 133 us
  waiting for transfers between devices  46.6 us (35%)
  starting transfers between devices  40.1 us (30%)
  Pallas kernels  36.7 us (27%)
  local copies, waits for them, and re-layouts  7.54 us (6%)
    ppermute x12, waiting for transfers between devices, around(): lax.ppermute(block, 'head', [(i, (i + distance) % 4) for i in range(4)])  24.7 us
    pallas_call x1, Pallas kernels, attention(): pl.pallas_call(attention_kernel, in_specs=[SMEM] + [ANY] * 9 + [VMEM], ou...  22.9 us
    ppermute x6, waiting for transfers between devices, over_chips(): return lax.ppermute(block, ('chip', 'core'), pairs)  22 us
    ppermute x6, starting transfers between devices, over_chips(): return lax.ppermute(block, ('chip', 'core'), pairs)  20.8 us
    ppermute x12, starting transfers between devices, around(): lax.ppermute(block, 'head', [(i, (i + distance) % 4) for i in range(4)])  19.3 us
    unnamed x40, local copies, waits for them, and re-layouts  6.24 us
    pallas_call x2, Pallas kernels, unpack(): pl.pallas_call(functools.partial(unpack_kernel, width), in_specs=[SMEM] +...  5.78 us
    pallas_call x2, Pallas kernels, pack(): pl.pallas_call(functools.partial(pack_kernel, width), in_specs=[SMEM, ANY...  5.44 us
  transfers between devices with their start and end apart: 18, of which 7 were waited for; matrix products, arithmetic and copies ran while one was open for 1% of the time, Pallas kernels for 5%

profile of v1, /device:TPU:128, one launch (start us, length us, event | category | flops | bytes accessed | tf_op | source)
XLA Modules:
  0.0 133.0 jit_solution(119213238483648185)
XLA Ops:
  0.6 0.6 pad_add_fusion.x_ref
  1.2 2.3 %pack.3 = (bf16[96,512]{1,0:T(8,128)(2,1)}, bf16[96,512]{1,0:T(8,128)(2,1)}, bf16[96,512]{1,0:T(8,128)(2,1)}) custom-call(s32[2]{0:T(128)} %pad_add_fusion.x_ref, bf16[96,1024]{1,0:T(8,128)(2,1)} %k_ref.1, bf16[96,1024]{1,0:T(8,128)(2,1)} %v_ref.1), custom_call_target="tpu_custom_call" | custom-call | tf_op jit(solution)/shard_map/pack/pallas_call | solution.py:64
  3.6 0.0 copy-start.19
  3.6 1.6 %collective-permute-start.3 = (bf16[96,512]{1,0:T(8,128)(2,1)}, bf16[96,512]{1,0:T(8,128)(2,1)S(1)}, u32[]{:S(2)}, u32[]{:S(2)}) collective-permute-start(bf16[96,512]{1,0:T(8,128)(2,1)} %get-tuple-element.25), channel_id=1, source_target_pairs={{0,1},{1,2},{2,3},{3,0},{4,5},{5,6},{6,7},{7,4},{8,9},{9,10},{10,1... | collective-permute-start | bytes 294920 | tf_op jit(solution)/shard_map/ppermute | solution.py:284
  5.2 2.7 %collective-permute-start.4 = (bf16[96,512]{1,0:T(8,128)(2,1)}, bf16[96,512]{1,0:T(8,128)(2,1)S(1)}, u32[]{:S(2)}, u32[]{:S(2)}) collective-permute-start(bf16[96,512]{1,0:T(8,128)(2,1)} %get-tuple-element.26), channel_id=1, source_target_pairs={{0,2},{1,3},{2,0},{3,1},{4,6},{5,7},{6,4},{7,5},{8,10},{9,11},{10,... | collective-permute-start | bytes 294920 | tf_op jit(solution)/shard_map/ppermute | solution.py:284
  7.9 1.4 %collective-permute-start.5 = (bf16[96,512]{1,0:T(8,128)(2,1)}, bf16[96,512]{1,0:T(8,128)(2,1)S(1)}, u32[]{:S(2)}, u32[]{:S(2)}) collective-permute-start(bf16[96,512]{1,0:T(8,128)(2,1)} %get-tuple-element.27), channel_id=1, source_target_pairs={{0,3},{1,0},{2,1},{3,2},{4,7},{5,4},{6,5},{7,6},{8,11},{9,8},{10,9... | collective-permute-start | bytes 294920 | tf_op jit(solution)/shard_map/ppermute | solution.py:284
  9.3 0.6 pad.4.doc_ref
  9.9 2.8 %collective-permute-done.4.r2 = bf16[96,512]{1,0:T(8,128)(2,1)S(1)} collective-permute-done((bf16[96,512]{1,0:T(8,128)(2,1)}, bf16[96,512]{1,0:T(8,128)(2,1)S(1)}, u32[]{:S(2)}, u32[]{:S(2)}) %collective-permute-start.4) | collective-permute-done | bytes 98336 | tf_op jit(solution)/shard_map/ppermute | solution.py:284
  12.7 0.6 copy-done.17
  13.4 0.6 copy-done.18
  14.0 2.5 %arrange.1.kv0 = bf16[400,512]{1,0:T(8,128)(2,1)} custom-call(s32[2]{0:T(128)} %pad_add_fusion.x_ref, bf16[96,1024]{1,0:T(8,128)(2,1)} %k_ref.1, bf16[96,1024]{1,0:T(8,128)(2,1)} %v_ref.1, bf16[96,512]{1,0:T(8,128)(2,1)} %copy-done.16, bf16[96,512]{1,0:T(8,128)(2,1)} %copy-done.17, bf16[96,512]{1,0:T(8,128)(2,1)} %copy-done.18, bf16[16,512]{1,0:T(8,128)(2,1)} %pad.4.doc_ref), custom_call_target="tpu_custom_call" | custom-call | tf_op jit(solution)/shard_map/arrange/pallas_call | solution.py:116
  16.6 3.6 %collective-permute-start.7 = (bf16[400,512]{1,0:T(8,128)(2,1)}, bf16[400,512]{1,0:T(8,128)(2,1)S(1)}, u32[]{:S(2)}, u32[]{:S(2)}) collective-permute-start(bf16[400,512]{1,0:T(8,128)(2,1)} %arrange.1.kv0), channel_id=1, source_target_pairs={{0,8},{4,12},{8,16},{12,20},{16,24},{20,28},{24,32},{28,36},{32,40... | collective-permute-start | bytes 1228808 | tf_op jit(solution)/shard_map/ppermute | solution.py:295
  20.2 1.9 %collective-permute-start.6 = (bf16[400,512]{1,0:T(8,128)(2,1)}, bf16[400,512]{1,0:T(8,128)(2,1)S(1)}, u32[]{:S(2)}, u32[]{:S(2)}) collective-permute-start(bf16[400,512]{1,0:T(8,128)(2,1)} %arrange.1.kv0), channel_id=1, source_target_pairs={{0,4},{4,16},{8,12},{12,24},{16,20},{20,32},{24,28},{28,40},{32,36... | collective-permute-start | bytes 1228808 | tf_op jit(solution)/shard_map/ppermute | solution.py:295
  22.1 14.1 %collective-permute-done.7.kv_c = bf16[400,512]{1,0:T(8,128)(2,1)S(1)} collective-permute-done((bf16[400,512]{1,0:T(8,128)(2,1)}, bf16[400,512]{1,0:T(8,128)(2,1)S(1)}, u32[]{:S(2)}, u32[]{:S(2)}) %collective-permute-start.7) | collective-permute-done | bytes 409632 | tf_op jit(solution)/shard_map/ppermute | solution.py:295
  36.2 3.1 %pack.2 = (bf16[96,2048]{1,0:T(8,128)(2,1)}, bf16[96,2048]{1,0:T(8,128)(2,1)}, bf16[96,2048]{1,0:T(8,128)(2,1)}) custom-call(s32[2]{0:T(128)} %pad_add_fusion.x_ref, bf16[96,4096]{1,0:T(8,128)(2,1)} %q_ref.1, bf16[96,4096]{1,0:T(8,128)(2,1)} %do_ref.1), custom_call_target="tpu_custom_call" | custom-call | tf_op jit(solution)/shard_map/pack/pallas_call | solution.py:64
  39.3 0.1 collective-permute-start
  39.4 3.5 %collective-permute-start.1 = (bf16[96,2048]{1,0:T(8,128)(2,1)}, bf16[96,2048]{1,0:T(8,128)(2,1)S(1)}, u32[]{:S(2)}, u32[]{:S(2)}) collective-permute-start(bf16[96,2048]{1,0:T(8,128)(2,1)} %get-tuple-element.23), channel_id=1, source_target_pairs={{0,2},{1,3},{2,0},{3,1},{4,6},{5,7},{6,4},{7,5},{8,10},{9,11},{10,... | collective-permute-start | bytes 1179656 | tf_op jit(solution)/shard_map/ppermute | solution.py:284
  42.9 1.1 collective-permute-start.2
  44.0 8.4 %collective-permute-done.q1 = bf16[96,2048]{1,0:T(8,128)(2,1)S(1)} collective-permute-done((bf16[96,2048]{1,0:T(8,128)(2,1)}, bf16[96,2048]{1,0:T(8,128)(2,1)S(1)}, u32[]{:S(2)}, u32[]{:S(2)}) %collective-permute-start) | collective-permute-done | bytes 393248 | tf_op jit(solution)/shard_map/ppermute | solution.py:284
  52.4 8.6 %collective-permute-done.1.q2 = bf16[96,2048]{1,0:T(8,128)(2,1)S(1)} collective-permute-done((bf16[96,2048]{1,0:T(8,128)(2,1)}, bf16[96,2048]{1,0:T(8,128)(2,1)S(1)}, u32[]{:S(2)}, u32[]{:S(2)}) %collective-permute-start.1) | collective-permute-done | bytes 393248 | tf_op jit(solution)/shard_map/ppermute | solution.py:284
  61.0 0.3 collective-permute-done.2.q3
  61.4 0.7 copy-done.5
  62.1 0.6 copy-done.4
  62.7 1.0 copy-done.2
  63.7 1.0 copy-done.6
  64.7 22.9 %attention.1 = (bf16[96,2048]{1,0:T(8,128)(2,1)S(1)}, bf16[96,2048]{1,0:T(8,128)(2,1)S(1)}, bf16[96,2048]{1,0:T(8,128)(2,1)S(1)}, bf16[96,2048]{1,0:T(8,128)(2,1...) custom-call(s32[2]{0:T(128)S(1)} %copy-done.4, ...), custom_call_target="tpu_custom_call" | custom-call | flops 8000000000 | bytes 8000000 | tf_op jit(solution)/shard_map/attention/pallas_call | solution.py:259
  87.7 0.0 copy-start.7
  87.7 5.4 %collective-permute-start.13 = (bf16[384,512]{1,0:T(8,128)(2,1)S(1)}, bf16[384,512]{1,0:T(8,128)(2,1)S(1)}, u32[]{:S(2)}, u32[]{:S(2)}) collective-permute-start(bf16[384,512]{1,0:T(8,128)(2,1)S(1)} %get-tuple-element.37), channel_id=1, source_target_pairs={{0,4},{4,0},{8,12},{12,8},{16,20},{20,16},{24,28},{28,24},{32,36},... | collective-permute-start | bytes 1179656 | tf_op jit(solution)/shard_map/ppermute | solution.py:295
  93.1 1.9 %collective-permute-start.12 = (bf16[384,512]{1,0:T(8,128)(2,1)}, bf16[384,512]{1,0:T(8,128)(2,1)S(1)}, u32[]{:S(2)}, u32[]{:S(2)}) collective-permute-start(bf16[384,512]{1,0:T(8,128)(2,1)} %get-tuple-element.35), channel_id=1, source_target_pairs={{4,0},{12,8},{20,16},{16,4},{28,24},{24,12},{36,32},{32,20},{44,40... | collective-permute-start | bytes 1179656 | tf_op jit(solution)/shard_map/ppermute | solution.py:295
  95.0 0.1 add_convert_fusion.1
  95.2 8.0 %collective-permute-start.14 = (bf16[384,512]{1,0:T(8,128)(2,1)S(1)}, bf16[384,512]{1,0:T(8,128)(2,1)S(1)}, u32[]{:S(2)}, u32[]{:S(2)}) collective-permute-start(bf16[384,512]{1,0:T(8,128)(2,1)S(1)} %add_convert_fusion.1), channel_id=1, source_target_pairs={{8,0},{12,4},{16,8},{20,12},{24,16},{28,20},{32,24},{36,28},{40,32... | collective-permute-start | bytes 1179656 | tf_op jit(solution)/shard_map/ppermute | solution.py:295
  103.2 2.2 %collective-permute-start.10 = (bf16[96,2048]{1,0:T(8,128)(2,1)}, bf16[96,2048]{1,0:T(8,128)(2,1)S(1)}, u32[]{:S(2)}, u32[]{:S(2)}) collective-permute-start(bf16[96,2048]{1,0:T(8,128)(2,1)} %copy-done.9), channel_id=1, source_target_pairs={{0,2},{1,3},{2,0},{3,1},{4,6},{5,7},{6,4},{7,5},{8,10},{9,11},{10,... | collective-permute-start | bytes 1179656 | tf_op jit(solution)/shard_map/ppermute | solution.py:284
  105.4 2.0 %collective-permute-start.11 = (bf16[96,2048]{1,0:T(8,128)(2,1)}, bf16[96,2048]{1,0:T(8,128)(2,1)S(1)}, u32[]{:S(2)}, u32[]{:S(2)}) collective-permute-start(bf16[96,2048]{1,0:T(8,128)(2,1)} %copy-done.8), channel_id=1, source_target_pairs={{0,3},{1,0},{2,1},{3,2},{4,7},{5,4},{6,5},{7,6},{8,11},{9,8},{10,9... | collective-permute-start | bytes 1179656 | tf_op jit(solution)/shard_map/ppermute | solution.py:284
  107.4 0.0 collective-permute-start.9
  107.4 7.9 %collective-permute-done.14 = bf16[384,512]{1,0:T(8,128)(2,1)S(1)} collective-permute-done((bf16[384,512]{1,0:T(8,128)(2,1)S(1)}, bf16[384,512]{1,0:T(8,128)(2,1)S(1)}, u32[]{:S(2)}, u32[]{:S(2)}) %collective-permute-start.14) | collective-permute-done | bytes 393248 | tf_op jit(solution)/shard_map/ppermute | solution.py:295
  115.3 0.2 add_convert_fusion
  115.5 0.7 constant_dynamic-slice_fusion
  116.1 1.4 %collective-permute-start.15 = (bf16[96,512]{1,0:T(8,128)(2,1)S(1)}, bf16[96,512]{1,0:T(8,128)(2,1)S(1)}, u32[]{:S(2)}, u32[]{:S(2)}) collective-permute-start(bf16[96,512]{1,0:T(8,128)(2,1)S(1)} %get-tuple-element.42), channel_id=1, source_target_pairs={{0,1},{1,2},{2,3},{3,0},{4,5},{5,6},{6,7},{7,4},{8,9},{9,10},{10,1... | collective-permute-start | bytes 294920 | tf_op jit(solution)/shard_map/ppermute | solution.py:284
  117.5 2.7 %collective-permute-start.16 = (bf16[96,512]{1,0:T(8,128)(2,1)S(1)}, bf16[96,512]{1,0:T(8,128)(2,1)S(1)}, u32[]{:S(2)}, u32[]{:S(2)}) collective-permute-start(bf16[96,512]{1,0:T(8,128)(2,1)S(1)} %get-tuple-element.41), channel_id=1, source_target_pairs={{0,2},{1,3},{2,0},{3,1},{4,6},{5,7},{6,4},{7,5},{8,10},{9,11},{10,... | collective-permute-start | bytes 294920 | tf_op jit(solution)/shard_map/ppermute | solution.py:284
  120.2 0.6 collective-permute-start.17
  120.8 4.6 %collective-permute-done.11.refs_3_ = bf16[96,2048]{1,0:T(8,128)(2,1)S(1)} collective-permute-done((bf16[96,2048]{1,0:T(8,128)(2,1)}, bf16[96,2048]{1,0:T(8,128)(2,1)S(1)}, u32[]{:S(2)}, u32[]{:S(2)}) %collective-permute-start.11) | collective-permute-done | bytes 393248 | tf_op jit(solution)/shard_map/ppermute | solution.py:284
  125.4 0.8 copy-done.11
  126.2 0.1 copy-done.12
  126.3 3.3 %unpack.2 = (bf16[96,4096]{1,0:T(8,128)(2,1)}, bf16[96,4096]{1,0:T(8,128)(2,1)}) custom-call(s32[2]{0:T(128)} %pad_add_fusion.x_ref, bf16[96,2048]{1,0:T(8,128)(2,1)} %copy-done.3, bf16[96,2048]{1,0:T(8,128)(2,1)} %copy-done.12, bf16[96,2048]{1,0:T(8,128)(2,1)} %copy-done.10, bf16[96,2048]{1,0:T(8,128)(2,1)} %copy-done.11), custom_call_target="tpu_custom_call" | custom-call | tf_op jit(solution)/shard_map/unpack/pallas_call | solution.py:88
  129.7 0.6 copy-done.13
  130.3 0.1 copy-done.14
  130.4 0.0 copy-done.15
  130.4 2.4 %unpack.3 = (bf16[96,1024]{1,0:T(8,128)(2,1)}, bf16[96,1024]{1,0:T(8,128)(2,1)}) custom-call(s32[2]{0:T(128)} %pad_add_fusion.x_ref, bf16[96,512]{1,0:T(8,128)(2,1)} %get-tuple-element.43.refs_0_, bf16[96,512]{1,0:T(8,128)(2,1)} %copy-done.13, bf16[96,512]{1,0:T(8,128)(2,1)} %copy-done.14, bf16[96,512]{1,0:T(8,128)(2,1)} %copy-done.15), custom_call_target="tpu_custom_call" | custom-call | tf_op jit(solution)/shard_map/unpack/pallas_call | solution.py:88
  (42 shorter events, 0.1 us)
Async XLA Ops:
  3.6 5.7 %copy-start.19 = (s32[384]{0:T(512)S(1)}, s32[384]{0:T(512)}, u32[]{:S(2)}) copy-start(s32[384]{0:T(512)} %param.9) | copy-start | bytes 4612
  3.6 6.4 %collective-permute-start.3 = (bf16[96,512]{1,0:T(8,128)(2,1)}, bf16[96,512]{1,0:T(8,128)(2,1)S(1)}, u32[]{:S(2)}, u32[]{:S(2)}) collective-permute-start(bf16[96,512]{1,0:T(8,128)(2,1)} %get-tuple-element.25), channel_id=1, source_target_pairs={{0,1},{1,2},{2,3},{3,0},{4,5},{5,6},{6,7},{7,4},{8,9},{9,10},{10,1... | collective-permute-start | bytes 294920 | tf_op jit(solution)/shard_map/ppermute | solution.py:284
  5.2 7.6 %collective-permute-start.4 = (bf16[96,512]{1,0:T(8,128)(2,1)}, bf16[96,512]{1,0:T(8,128)(2,1)S(1)}, u32[]{:S(2)}, u32[]{:S(2)}) collective-permute-start(bf16[96,512]{1,0:T(8,128)(2,1)} %get-tuple-element.26), channel_id=1, source_target_pairs={{0,2},{1,3},{2,0},{3,1},{4,6},{5,7},{6,4},{7,5},{8,10},{9,11},{10,... | collective-permute-start | bytes 294920 | tf_op jit(solution)/shard_map/ppermute | solution.py:284
  7.9 4.8 %collective-permute-start.5 = (bf16[96,512]{1,0:T(8,128)(2,1)}, bf16[96,512]{1,0:T(8,128)(2,1)S(1)}, u32[]{:S(2)}, u32[]{:S(2)}) collective-permute-start(bf16[96,512]{1,0:T(8,128)(2,1)} %get-tuple-element.27), channel_id=1, source_target_pairs={{0,3},{1,0},{2,1},{3,2},{4,7},{5,4},{6,5},{7,6},{8,11},{9,8},{10,9... | collective-permute-start | bytes 294920 | tf_op jit(solution)/shard_map/ppermute | solution.py:284
  9.9 2.8 %copy-start.16 = (bf16[96,512]{1,0:T(8,128)(2,1)}, bf16[96,512]{1,0:T(8,128)(2,1)S(1)}, u32[]{:S(2)}) copy-start(bf16[96,512]{1,0:T(8,128)(2,1)S(1)} %collective-permute-done.3.r1) | copy-start | bytes 294916
  12.7 0.6 copy-start.17
  13.4 0.6 copy-start.18
  16.5 45.6 %copy-start = (bf16[96,4096]{1,0:T(8,128)(2,1)S(1)}, bf16[96,4096]{1,0:T(8,128)(2,1)}, u32[]{:S(2)}) copy-start(bf16[96,4096]{1,0:T(8,128)(2,1)} %q_ref.1) | copy-start | bytes 2359300
  16.5 45.6 %copy-start.1 = (bf16[96,4096]{1,0:T(8,128)(2,1)S(1)}, bf16[96,4096]{1,0:T(8,128)(2,1)}, u32[]{:S(2)}) copy-start(bf16[96,4096]{1,0:T(8,128)(2,1)} %do_ref.1) | copy-start | bytes 2359300
  16.6 19.6 %collective-permute-start.7 = (bf16[400,512]{1,0:T(8,128)(2,1)}, bf16[400,512]{1,0:T(8,128)(2,1)S(1)}, u32[]{:S(2)}, u32[]{:S(2)}) collective-permute-start(bf16[400,512]{1,0:T(8,128)(2,1)} %arrange.1.kv0), channel_id=1, source_target_pairs={{0,8},{4,12},{8,16},{12,20},{16,24},{20,28},{24,32},{28,36},{32,40... | collective-permute-start | bytes 1228808 | tf_op jit(solution)/shard_map/ppermute | solution.py:295
  20.2 41.2 %collective-permute-start.6 = (bf16[400,512]{1,0:T(8,128)(2,1)}, bf16[400,512]{1,0:T(8,128)(2,1)S(1)}, u32[]{:S(2)}, u32[]{:S(2)}) collective-permute-start(bf16[400,512]{1,0:T(8,128)(2,1)} %arrange.1.kv0), channel_id=1, source_target_pairs={{0,4},{4,16},{8,12},{12,24},{16,20},{20,32},{24,28},{28,40},{32,36... | collective-permute-start | bytes 1228808 | tf_op jit(solution)/shard_map/ppermute | solution.py:295
  36.2 25.2 %collective-permute-start.8 = (bf16[400,512]{1,0:T(8,128)(2,1)S(1)}, bf16[400,512]{1,0:T(8,128)(2,1)S(1)}, u32[]{:S(2)}, u32[]{:S(2)}) collective-permute-start(bf16[400,512]{1,0:T(8,128)(2,1)S(1)} %collective-permute-done.7.kv_c), channel_id=1, source_target_pairs={{0,4},{4,0},{8,12},{12,8},{16,20},{20,16},{24,28},{28,24},{32,36},... | collective-permute-start | bytes 1228808 | tf_op jit(solution)/shard_map/ppermute | solution.py:295
  39.3 13.1 %collective-permute-start = (bf16[96,2048]{1,0:T(8,128)(2,1)}, bf16[96,2048]{1,0:T(8,128)(2,1)S(1)}, u32[]{:S(2)}, u32[]{:S(2)}) collective-permute-start(bf16[96,2048]{1,0:T(8,128)(2,1)} %get-tuple-element.22), channel_id=1, source_target_pairs={{0,1},{1,2},{2,3},{3,0},{4,5},{5,6},{6,7},{7,4},{8,9},{9,10},{10,1... | collective-permute-start | bytes 1179656 | tf_op jit(solution)/shard_map/ppermute | solution.py:284
  39.4 21.6 %collective-permute-start.1 = (bf16[96,2048]{1,0:T(8,128)(2,1)}, bf16[96,2048]{1,0:T(8,128)(2,1)S(1)}, u32[]{:S(2)}, u32[]{:S(2)}) collective-permute-start(bf16[96,2048]{1,0:T(8,128)(2,1)} %get-tuple-element.23), channel_id=1, source_target_pairs={{0,2},{1,3},{2,0},{3,1},{4,6},{5,7},{6,4},{7,5},{8,10},{9,11},{10,... | collective-permute-start | bytes 1179656 | tf_op jit(solution)/shard_map/ppermute | solution.py:284
  42.9 18.5 %collective-permute-start.2 = (bf16[96,2048]{1,0:T(8,128)(2,1)}, bf16[96,2048]{1,0:T(8,128)(2,1)S(1)}, u32[]{:S(2)}, u32[]{:S(2)}) collective-permute-start(bf16[96,2048]{1,0:T(8,128)(2,1)} %get-tuple-element.24), channel_id=1, source_target_pairs={{0,3},{1,0},{2,1},{3,2},{4,7},{5,4},{6,5},{7,6},{8,11},{9,8},{10,9... | collective-permute-start | bytes 1179656 | tf_op jit(solution)/shard_map/ppermute | solution.py:284
  61.4 0.8 copy-start.5
  62.1 0.6 copy-start.4
  62.7 1.0 copy-start.2
  63.7 1.0 copy-start.6
  87.7 7.5 %copy-start.3 = (bf16[96,2048]{1,0:T(8,128)(2,1)}, bf16[96,2048]{1,0:T(8,128)(2,1)S(1)}, u32[]{:S(2)}) copy-start(bf16[96,2048]{1,0:T(8,128)(2,1)S(1)} %get-tuple-element.28.refs_0_) | copy-start | bytes 1179652
  87.7 7.5 %copy-start.7 = (bf16[96,2048]{1,0:T(8,128)(2,1)}, bf16[96,2048]{1,0:T(8,128)(2,1)S(1)}, u32[]{:S(2)}) copy-start(bf16[96,2048]{1,0:T(8,128)(2,1)S(1)} %get-tuple-element.29) | copy-start | bytes 1179652
  87.7 7.5 %copy-start.8 = (bf16[96,2048]{1,0:T(8,128)(2,1)}, bf16[96,2048]{1,0:T(8,128)(2,1)S(1)}, u32[]{:S(2)}) copy-start(bf16[96,2048]{1,0:T(8,128)(2,1)S(1)} %get-tuple-element.31) | copy-start | bytes 1179652
  87.7 7.5 %copy-start.9 = (bf16[96,2048]{1,0:T(8,128)(2,1)}, bf16[96,2048]{1,0:T(8,128)(2,1)S(1)}, u32[]{:S(2)}) copy-start(bf16[96,2048]{1,0:T(8,128)(2,1)S(1)} %get-tuple-element.30) | copy-start | bytes 1179652
  87.7 7.3 %collective-permute-start.13 = (bf16[384,512]{1,0:T(8,128)(2,1)S(1)}, bf16[384,512]{1,0:T(8,128)(2,1)S(1)}, u32[]{:S(2)}, u32[]{:S(2)}) collective-permute-start(bf16[384,512]{1,0:T(8,128)(2,1)S(1)} %get-tuple-element.37), channel_id=1, source_target_pairs={{0,4},{4,0},{8,12},{12,8},{16,20},{20,16},{24,28},{28,24},{32,36},... | collective-permute-start | bytes 1179656 | tf_op jit(solution)/shard_map/ppermute | solution.py:295
  93.1 14.3 %collective-permute-start.12 = (bf16[384,512]{1,0:T(8,128)(2,1)}, bf16[384,512]{1,0:T(8,128)(2,1)S(1)}, u32[]{:S(2)}, u32[]{:S(2)}) collective-permute-start(bf16[384,512]{1,0:T(8,128)(2,1)} %get-tuple-element.35), channel_id=1, source_target_pairs={{4,0},{12,8},{20,16},{16,4},{28,24},{24,12},{36,32},{32,20},{44,40... | collective-permute-start | bytes 1179656 | tf_op jit(solution)/shard_map/ppermute | solution.py:295
  95.2 20.1 %collective-permute-start.14 = (bf16[384,512]{1,0:T(8,128)(2,1)S(1)}, bf16[384,512]{1,0:T(8,128)(2,1)S(1)}, u32[]{:S(2)}, u32[]{:S(2)}) collective-permute-start(bf16[384,512]{1,0:T(8,128)(2,1)S(1)} %add_convert_fusion.1), channel_id=1, source_target_pairs={{8,0},{12,4},{16,8},{20,12},{24,16},{28,20},{32,24},{36,28},{40,32... | collective-permute-start | bytes 1179656 | tf_op jit(solution)/shard_map/ppermute | solution.py:295
  103.2 17.0 %collective-permute-start.10 = (bf16[96,2048]{1,0:T(8,128)(2,1)}, bf16[96,2048]{1,0:T(8,128)(2,1)S(1)}, u32[]{:S(2)}, u32[]{:S(2)}) collective-permute-start(bf16[96,2048]{1,0:T(8,128)(2,1)} %copy-done.9), channel_id=1, source_target_pairs={{0,2},{1,3},{2,0},{3,1},{4,6},{5,7},{6,4},{7,5},{8,10},{9,11},{10,... | collective-permute-start | bytes 1179656 | tf_op jit(solution)/shard_map/ppermute | solution.py:284
  105.4 20.0 %collective-permute-start.11 = (bf16[96,2048]{1,0:T(8,128)(2,1)}, bf16[96,2048]{1,0:T(8,128)(2,1)S(1)}, u32[]{:S(2)}, u32[]{:S(2)}) collective-permute-start(bf16[96,2048]{1,0:T(8,128)(2,1)} %copy-done.8), channel_id=1, source_target_pairs={{0,3},{1,0},{2,1},{3,2},{4,7},{5,4},{6,5},{7,6},{8,11},{9,8},{10,9... | collective-permute-start | bytes 1179656 | tf_op jit(solution)/shard_map/ppermute | solution.py:284
  107.4 18.0 %collective-permute-start.9 = (bf16[96,2048]{1,0:T(8,128)(2,1)}, bf16[96,2048]{1,0:T(8,128)(2,1)S(1)}, u32[]{:S(2)}, u32[]{:S(2)}) collective-permute-start(bf16[96,2048]{1,0:T(8,128)(2,1)} %copy-done.7), channel_id=1, source_target_pairs={{0,1},{1,2},{2,3},{3,0},{4,5},{5,6},{6,7},{7,4},{8,9},{9,10},{10,1... | collective-permute-start | bytes 1179656 | tf_op jit(solution)/shard_map/ppermute | solution.py:284
  116.1 13.5 %collective-permute-start.15 = (bf16[96,512]{1,0:T(8,128)(2,1)S(1)}, bf16[96,512]{1,0:T(8,128)(2,1)S(1)}, u32[]{:S(2)}, u32[]{:S(2)}) collective-permute-start(bf16[96,512]{1,0:T(8,128)(2,1)S(1)} %get-tuple-element.42), channel_id=1, source_target_pairs={{0,1},{1,2},{2,3},{3,0},{4,5},{5,6},{6,7},{7,4},{8,9},{9,10},{10,1... | collective-permute-start | bytes 294920 | tf_op jit(solution)/shard_map/ppermute | solution.py:284
  117.5 12.2 %collective-permute-start.16 = (bf16[96,512]{1,0:T(8,128)(2,1)S(1)}, bf16[96,512]{1,0:T(8,128)(2,1)S(1)}, u32[]{:S(2)}, u32[]{:S(2)}) collective-permute-start(bf16[96,512]{1,0:T(8,128)(2,1)S(1)} %get-tuple-element.41), channel_id=1, source_target_pairs={{0,2},{1,3},{2,0},{3,1},{4,6},{5,7},{6,4},{7,5},{8,10},{9,11},{10,... | collective-permute-start | bytes 294920 | tf_op jit(solution)/shard_map/ppermute | solution.py:284
  120.2 5.2 %copy-start.10 = (bf16[96,2048]{1,0:T(8,128)(2,1)}, bf16[96,2048]{1,0:T(8,128)(2,1)S(1)}, u32[]{:S(2)}) copy-start(bf16[96,2048]{1,0:T(8,128)(2,1)S(1)} %collective-permute-done.10.refs_2_) | copy-start | bytes 1179652
  120.2 9.5 %collective-permute-start.17 = (bf16[96,512]{1,0:T(8,128)(2,1)S(1)}, bf16[96,512]{1,0:T(8,128)(2,1)S(1)}, u32[]{:S(2)}, u32[]{:S(2)}) collective-permute-start(bf16[96,512]{1,0:T(8,128)(2,1)S(1)} %get-tuple-element.40), channel_id=1, source_target_pairs={{0,3},{1,0},{2,1},{3,2},{4,7},{5,4},{6,5},{7,6},{8,11},{9,8},{10,9... | collective-permute-start | bytes 294920 | tf_op jit(solution)/shard_map/ppermute | solution.py:284
  125.4 0.8 copy-start.11
  125.4 0.9 copy-start.12
  129.7 0.6 copy-start.13
  129.7 0.7 copy-start.14
  129.7 0.7 copy-start.15

commit v2 on v1

v2 whole, which is shorter than its diff:
```python
import functools
import math

import jax
import jax.numpy as jnp
from jax import lax
from jax.experimental import pallas as pl
from jax.experimental.pallas import tpu as pltpu
from jax.sharding import Mesh, PartitionSpec as P

HDIM = 128
ROWS = 384
PART = 96
KVW = 4 * HDIM
QW = 4 * HDIM
WINDOW = 4 * ROWS
TILE = 128
KT = 256
SPAN = 3 * ROWS + TILE
MASKED = -1e30
SCALE = HDIM**-0.5
EXP_SCALE = SCALE * math.log2(math.e)
ANY = pl.BlockSpec(memory_space=pl.ANY)
SMEM = pl.BlockSpec(memory_space=pltpu.SMEM)
VMEM = pl.BlockSpec(memory_space=pltpu.VMEM)
BF16, F32 = jnp.bfloat16, jnp.float32


def struct(shape, dtype):
    return jax.ShapeDtypeStruct(shape, dtype)


def run_copies(copies):
    for copy in copies:
        copy.start()
    for copy in copies:
        copy.wait()


def copier(sems):
    count = [0]

    def make(src, dst):
        count[0] += 1
        return pltpu.make_async_copy(src, dst, sems.at[count[0] - 1])

    return make


def pack_kernel(width, x_ref, a_ref, b_ref, *refs):
    outs, sems = refs[:-1], refs[-1]
    make = copier(sems)
    copies = []
    for p in range(1, 4):
        for g in range(2):
            place = pl.multiple_of(lax.rem(x_ref[0] + p, 4) * (2 * width) + g * width, width)
            for n, src in enumerate((a_ref, b_ref)):
                at = pl.ds((2 * g + n) * width, width)
                copies.append(make(src.at[:, pl.ds(place, width)], outs[p - 1].at[:, at]))
    run_copies(copies)


def pack(x, a, b):
    width = a.shape[1] // 8
    return pl.pallas_call(
        functools.partial(pack_kernel, width),
        in_specs=[SMEM, ANY, ANY],
        out_specs=[VMEM] * 3,
        out_shape=[struct((PART, 4 * width), BF16)] * 3,
        scratch_shapes=[pltpu.SemaphoreType.DMA((12,))],
        name="pack",
    )(x, a, b)


def unpack_kernel(width, x_ref, *refs):
    parts, outs, sems = refs[:4], refs[4:-1], refs[-1]
    make = copier(sems)
    copies = []
    for p in range(4):
        for g in range(2):
            place = pl.multiple_of(lax.rem(x_ref[0] + 4 - p, 4) * (2 * width) + g * width, width)
            for n, out in enumerate(outs):
                at = pl.ds((2 * g + n) * width, width)
                copies.append(make(parts[p].at[:, at], out.at[:, pl.ds(place, width)]))
    run_copies(copies)


def unpack(x, parts):
    width = parts[0].shape[1] // 4
    whole = struct((PART, 8 * width), BF16)
    return pl.pallas_call(
        functools.partial(unpack_kernel, width),
        in_specs=[SMEM] + [ANY] * 4,
        out_specs=[VMEM] * 2,
        out_shape=[whole] * 2,
        scratch_shapes=[pltpu.SemaphoreType.DMA((16,))],
        name="unpack",
    )(x, *parts)


def arrange_kernel(x_ref, k_ref, v_ref, r1, r2, r3, doc_ref, out_ref, sems):
    make = copier(sems)
    x = x_ref[0]
    rows = pl.ds(pl.multiple_of(x * PART, PART), PART)
    copies = [make(doc_ref, out_ref.at[pl.ds(ROWS, 16)])]
    for g in range(2):
        own = pl.multiple_of(x * (2 * HDIM) + g * HDIM, HDIM)
        for n, ref in enumerate((k_ref, v_ref)):
            copies.append(make(ref.at[:, pl.ds(own, HDIM)], out_ref.at[rows, pl.ds((2 * g + n) * HDIM, HDIM)]))
    for p, ref in enumerate((r1, r2, r3)):
        place = pl.multiple_of(lax.rem(x + 3 - p, 4) * PART, PART)
        copies.append(make(ref, out_ref.at[pl.ds(place, PART)]))
    run_copies(copies)


def arrange(x, keys, values, received, docs):
    return pl.pallas_call(
        arrange_kernel,
        in_specs=[SMEM] + [ANY] * 6,
        out_specs=VMEM,
        out_shape=struct((ROWS + 16, KVW), BF16),
        scratch_shapes=[pltpu.SemaphoreType.DMA((8,))],
        name="arrange",
    )(x, keys, values, *received, docs)


def dot(a, b, contract):
    return lax.dot_general(a, b, ((contract[:1], contract[1:]), ((), ())), preferred_element_type=F32)


def attention_kernel(
    x_ref, q_ref, do_ref, q1, q2, q3, kv0, kv_b, kv_c, kv_a, docs_ref,
    o0, o1, o2, o3, own_ref, far_ref, swap_ref, next_ref,
    kv, docs_kv, qd, out, acc, s_scr, p_scr, kvt, doc_col, qs, qt, sems,
):
    make = copier(sems)
    x, core = x_ref[0], x_ref[1]
    slot_b, slot_a = jnp.where(core == 0, 0, 2), jnp.where(core == 0, 2, 0)
    copies = []
    for ref, slot in ((kv0, 3), (kv_c, 1), (kv_b, slot_b), (kv_a, slot_a)):
        copies.append(make(ref.at[pl.ds(0, ROWS)], kv.at[pl.ds(pl.multiple_of(slot * ROWS, ROWS), ROWS)]))
        copies.append(make(ref.at[pl.ds(ROWS, 16)], docs_kv.at[slot]))
    kv_copies = len(copies)
    rows = pl.ds(pl.multiple_of(x * PART, PART), PART)
    for g in range(2):
        own = pl.multiple_of(x * (2 * QW) + g * QW, QW)
        for n, ref in enumerate((q_ref, do_ref)):
            copies.append(make(ref.at[:, pl.ds(own, QW)], qd.at[rows, pl.ds((2 * g + n) * QW, QW)]))
    for p, ref in enumerate((q1, q2, q3)):
        place = pl.multiple_of(lax.rem(x + 3 - p, 4) * PART, PART)
        copies.append(make(ref, qd.at[pl.ds(place, PART)]))
    for copy in copies:
        copy.start()
    acc[...] = jnp.zeros_like(acc)
    for copy in copies[:kv_copies]:
        copy.wait()

    eye = (
        lax.broadcasted_iota(jnp.int32, (HDIM, HDIM), 0) == lax.broadcasted_iota(jnp.int32, (HDIM, HDIM), 1)
    ).astype(BF16)
    key_docs = jnp.concatenate([docs_kv[s][0:1, 0:ROWS] for s in range(4)], 1)
    row_docs = docs_ref[...]
    doc_col[...] = jnp.transpose(jnp.broadcast_to(key_docs.astype(F32), (TILE, WINDOW)))
    for t in range(WINDOW // KT):
        at = slice(t * KT, (t + 1) * KT)
        for n in range(4):
            kvt[n, :, at] = dot(eye, kv[at, n * HDIM : (n + 1) * HDIM], (1, 1)).astype(BF16)
    for copy in copies[kv_copies:]:
        copy.wait()

    width = 4 * TILE
    chunks = range(SPAN // KT)
    units = range(2 * (ROWS // TILE))
    k_cols = [slice(2 * g * HDIM, (2 * g + 1) * HDIM) for g in range(2)]
    v_cols = [slice((2 * g + 1) * HDIM, (2 * g + 2) * HDIM) for g in range(2)]
    state = [{} for _ in units]

    def keys_of(u, c):
        first = u // 2 * TILE + c * KT
        return slice(first, first + KT)

    def rows_of(u):
        return slice(u // 2 * TILE, (u // 2 + 1) * TILE)

    def head_cols(u, n, r):
        first = (u % 2 * 2 + n) * QW + r * HDIM
        return slice(first, first + HDIM)

    def begin(u):
        q = jnp.concatenate([qd[rows_of(u), head_cols(u, 0, r)] for r in range(4)], 0)
        do = jnp.concatenate([qd[rows_of(u), head_cols(u, 1, r)] for r in range(4)], 0)
        qs[u, 0], qs[u, 1] = q, do
        qt[u, 0] = dot(eye, q, (1, 1)).astype(BF16)
        qt[u, 1] = dot(eye, do, (1, 1)).astype(BF16)
        state[u]["high"] = jnp.full((1, width), MASKED, F32)

    def score(u, c):
        at = keys_of(u, c)
        s = dot(kv[at, k_cols[u % 2]], qt[u, 0], (1, 0))
        docs_row = row_docs[0:1, rows_of(u)]
        allowed = doc_col[at, :] == docs_row
        if (c + 1) * KT > SPAN - TILE:
            key_at = lax.broadcasted_iota(jnp.int32, (KT, TILE), 0) + (u // 2 * TILE + c * KT)
            row_at = lax.broadcasted_iota(jnp.int32, (KT, TILE), 1) + (3 * ROWS + u // 2 * TILE)
            allowed = allowed & (key_at <= row_at)
        s = jnp.concatenate([jnp.where(allowed, s[:, r * TILE : (r + 1) * TILE], MASKED) for r in range(4)], 1)
        s_scr[u % 2, c] = s
        state[u]["high"] = jnp.maximum(state[u]["high"], jnp.max(s, 0, keepdims=True))

    def begin_weigh(u):
        state[u]["shift"] = state[u]["high"] * EXP_SCALE
        state[u]["total"] = jnp.zeros((1, width), F32)
        state[u]["o"] = jnp.zeros((HDIM, width), F32)

    def weigh(u, c):
        e = jnp.exp2(s_scr[u % 2, c] * EXP_SCALE - state[u]["shift"])
        low = e.astype(BF16)
        p_scr[u % 2, c] = low
        state[u]["total"] += jnp.sum(e, 0, keepdims=True)
        state[u]["o"] += dot(kvt[2 * (u % 2) + 1, :, keys_of(u, c)], low, (1, 0))

    def begin_back(u):
        inverse = 1.0 / state[u]["total"]
        o_t = (state[u]["o"] * inverse).astype(BF16).astype(F32)
        state[u]["inverse"] = inverse
        state[u]["dots"] = jnp.sum(qt[u, 1].astype(F32) * o_t, 0, keepdims=True)
        state[u]["dq"] = jnp.zeros((HDIM, width), F32)
        for r in range(4):
            lanes = slice(r * TILE, (r + 1) * TILE)
            out[rows_of(u), head_cols(u, 0, r)] = jnp.transpose(o_t[:, lanes]).astype(BF16)

    def back(u, c):
        at = keys_of(u, c)
        probs = p_scr[u % 2, c].astype(F32) * state[u]["inverse"]
        dp = dot(kv[at, v_cols[u % 2]], qt[u, 1], (1, 0))
        ds = (probs * (dp - state[u]["dots"])).astype(BF16)
        acc[at, v_cols[u % 2]] += dot(probs.astype(BF16), qs[u, 1], (1, 0))
        acc[at, k_cols[u % 2]] += dot(ds, qs[u, 0], (1, 0))
        state[u]["dq"] += dot(kvt[2 * (u % 2), :, at], ds, (1, 0))

    def end_back(u):
        for r in range(4):
            lanes = slice(r * TILE, (r + 1) * TILE)
            out[rows_of(u), head_cols(u, 1, r)] = jnp.transpose(state[u]["dq"][:, lanes] * SCALE).astype(BF16)

    for u in units:
        begin(u)
    for c in chunks:
        score(0, c)
    begin_weigh(0)
    for c in chunks:
        weigh(0, c)
    for u in units:
        begin_back(u)
        later = []
        if u + 1 < len(units):
            later = [functools.partial(score, u + 1, c) for c in chunks]
            later.append(functools.partial(begin_weigh, u + 1))
            later += [functools.partial(weigh, u + 1, c) for c in chunks]
        for c in chunks:
            back(u, c)
            for _ in range(3 if c == 0 else 2):
                if later:
                    later.pop(0)()
        end_back(u)

    copies = []
    for p, ref in enumerate((o0, o1, o2, o3)):
        place = pl.multiple_of(lax.rem(x + p, 4) * PART, PART)
        copies.append(make(out.at[pl.ds(place, PART)], ref))
    for copy in copies:
        copy.start()

    def gradient(slot):
        part = acc[pl.ds(pl.multiple_of(slot * ROWS, ROWS), ROWS), :]
        scales = (SCALE, 1.0, SCALE, 1.0)
        return jnp.concatenate([part[:, n * HDIM : (n + 1) * HDIM] * scales[n] for n in range(4)], 1)

    own_ref[...] = gradient(3)
    next_ref[...] = gradient(1)
    far_ref[...] = gradient(slot_b).astype(BF16)
    swap_ref[...] = gradient(slot_a).astype(BF16)
    for copy in copies:
        copy.wait()


def attention(place, queries, out_grad, received, kv0, kv_b, kv_c, kv_a, docs):
    piece = struct((PART, 4 * QW), BF16)
    grad, low_grad = struct((ROWS, KVW), F32), struct((ROWS, KVW), BF16)
    units, chunks, width = 2 * (ROWS // TILE), SPAN // KT, 4 * TILE
    return pl.pallas_call(
        attention_kernel,
        in_specs=[SMEM] + [ANY] * 9 + [VMEM],
        out_specs=[ANY] * 4 + [VMEM] * 4,
        out_shape=[piece] * 4 + [grad, low_grad, low_grad, grad],
        scratch_shapes=[
            pltpu.VMEM((WINDOW, KVW), BF16),
            pltpu.VMEM((4, 16, KVW), BF16),
            pltpu.VMEM((ROWS, 4 * QW), BF16),
            pltpu.VMEM((ROWS, 4 * QW), BF16),
            pltpu.VMEM((WINDOW, KVW), F32),
            pltpu.VMEM((2, chunks, KT, width), F32),
            pltpu.VMEM((2, chunks, KT, width), BF16),
            pltpu.VMEM((4, HDIM, WINDOW), BF16),
            pltpu.VMEM((WINDOW, TILE), F32),
            pltpu.VMEM((units, 2, width, HDIM), BF16),
            pltpu.VMEM((units, 2, HDIM, width), BF16),
            pltpu.SemaphoreType.DMA((20,)),
        ],
        compiler_params=pltpu.CompilerParams(vmem_limit_bytes=40 * 1024 * 1024),
        cost_estimate=pl.CostEstimate(flops=8_000_000_000, bytes_accessed=8_000_000, transcendentals=4_000_000),
        name="attention",
    )(place, queries, out_grad, *received, kv0, kv_b, kv_c, kv_a, docs)


def around(block, distance):
    return lax.ppermute(block, "head", [(i, (i + distance) % 4) for i in range(4)])


def over_chips(block, routes):
    chips = lax.axis_size("chip")
    pairs = [
        (2 * c + k, 2 * (c + step) + to)
        for c in range(chips)
        for k, step, to in routes
        if 0 <= c + step < chips
    ]
    return lax.ppermute(block, ("chip", "core"), pairs)


def local(queries, keys, values, out_grad, doc_ids):
    x = lax.axis_index("head")
    place = jnp.stack([x, lax.axis_index("core")]).astype(jnp.int32)
    doc_number = doc_ids + 1
    docs_low = jnp.pad(doc_number.astype(BF16)[None, :], ((0, 15), (0, KVW - ROWS)))
    docs = jnp.broadcast_to(doc_number.astype(F32)[None, :], (8, ROWS))
    kv_received = [around(piece, p + 1) for p, piece in enumerate(pack(place, keys, values))]
    q_pieces = pack(place, queries, out_grad)
    kv_received, q_pieces = lax.optimization_barrier((kv_received, q_pieces))
    q_received = [around(piece, p + 1) for p, piece in enumerate(q_pieces)]
    kv0 = arrange(place, keys, values, kv_received, docs_low)
    kv_c = over_chips(kv0, [(0, 1, 0), (1, 1, 1)])
    kv_b = over_chips(kv0, [(0, 0, 1), (1, 2, 0)])
    kv_c, q_received = lax.optimization_barrier((kv_c, q_received))
    kv_a = over_chips(kv_c, [(0, 0, 1), (1, 0, 0)])
    o0, o1, o2, o3, own, far, swap, near = attention(
        place, queries, out_grad, q_received, kv0, kv_b, kv_c, kv_a, docs
    )
    back_a = over_chips(swap, [(0, 0, 1), (1, 0, 0)])
    near = (near + back_a.astype(F32)).astype(BF16)
    back_c = over_chips(near, [(0, -1, 0), (1, -1, 1)])
    back_b = over_chips(far, [(1, 0, 0), (0, -2, 1)])
    outs = [o0] + [around(piece, p) for p, piece in ((1, o1), (2, o2), (3, o3))]
    attention_out, query_grad = unpack(place, outs)
    total = (own + back_b.astype(F32) + back_c.astype(F32)).astype(BF16)
    parts = [lax.dynamic_slice_in_dim(total, (x + p) % 4 * PART, PART, 0) for p in range(4)]
    grads = [parts[0]] + [around(parts[p], p) for p in (1, 2, 3)]
    key_grad, value_grad = unpack(place, grads)
    return attention_out, query_grad, key_grad, value_grad


def solution(mesh):
    chips = mesh.devices.size // 8
    mesh = Mesh(mesh.devices.reshape(chips, 2, 4), ("chip", "core", "head"))
    rows = P(("chip", "core", "head"), None)
    return jax.shard_map(
        local,
        mesh=mesh,
        in_specs=(rows, rows, rows, rows, P(("chip", "core"))),
        out_specs=(rows, rows, rows, rows),
        check_vma=False,
    )
```

time: 134 us -> 100 us (0.75)
  waiting for transfers between devices: 46.6 us -> 27.1 us
  starting transfers between devices: 40.1 us -> 32 us
  Pallas kernels: 36.7 us -> 32.2 us
  local copies, waits for them, and re-layouts: 7.54 us -> 5.13 us
    ppermute x6, waiting for transfers between devices: 22 us -> 9.95 us  [over_chips(): return lax.ppermute(block, ('chip', 'core'), pairs)]
    ppermute x6, starting transfers between devices: 20.8 us -> 13.2 us  [over_chips(): return lax.ppermute(block, ('chip', 'core'), pairs)]
    ppermute x12, waiting for transfers between devices: 24.7 us -> 17.1 us  [around(): lax.ppermute(block, 'head', [(i, (i + distance) % 4) for i in range(4)])]
    pallas_call x1, Pallas kernels: 22.9 us -> 18 us  [attention(): pl.pallas_call(attention_kernel, in_specs=[SMEM] + [ANY] * 9 + [VMEM], ou...]
    unnamed x40 -> x30, local copies, waits for them, and re-layouts: 6.24 us -> 3.84 us
  transfers between devices with their start and end apart: 18 -> 18, of which waited for: 7 -> 6; matrix products, arithmetic and copies ran while one was open for 1% -> 3% of each run, Pallas kernels for 5% -> 7%
where the time goes in v2:
time: 100 us; the launch traced here: 99.5 us
  Pallas kernels  32.2 us (32%)
  starting transfers between devices  32 us (32%)
  waiting for transfers between devices  27.1 us (27%)
  local copies, waits for them, and re-layouts  5.13 us (5%)
  other arithmetic  2.01 us (2%)
  between operations  1.11 us (1%)
    ppermute x12, starting transfers between devices, around(): lax.ppermute(block, 'head', [(i, (i + distance) % 4) for i in range(4)])  18.8 us
    pallas_call x1, Pallas kernels, attention(): pl.pallas_call(attention_kernel, in_specs=[SMEM] + [ANY] * 9 + [VMEM], ou...  18 us
    ppermute x12, waiting for transfers between devices, around(): lax.ppermute(block, 'head', [(i, (i + distance) % 4) for i in range(4)])  17.1 us
    ppermute x6, starting transfers between devices, over_chips(): return lax.ppermute(block, ('chip', 'core'), pairs)  13.2 us
    ppermute x6, waiting for transfers between devices, over_chips(): return lax.ppermute(block, ('chip', 'core'), pairs)  9.95 us
    pallas_call x2, Pallas kernels, unpack(): pl.pallas_call(functools.partial(unpack_kernel, width), in_specs=[SMEM] +...  5.92 us
    pallas_call x2, Pallas kernels, pack(): pl.pallas_call(functools.partial(pack_kernel, width), in_specs=[SMEM, ANY...  5.65 us
    unnamed x30, local copies, waits for them, and re-layouts  3.84 us
  transfers between devices with their start and end apart: 18, of which 6 were waited for; matrix products, arithmetic and copies ran while one was open for 3% of the time, Pallas kernels for 7%

profile of v2, /device:TPU:128, one launch (start us, length us, event | category | flops | bytes accessed | tf_op | source)
XLA Modules:
  0.0 99.5 jit_solution(5869662303982960285)
XLA Ops:
  0.6 0.6 pad_add_fusion.x_ref
  1.2 2.4 %pack.2 = (bf16[96,512]{1,0:T(8,128)(2,1)}, bf16[96,512]{1,0:T(8,128)(2,1)}, bf16[96,512]{1,0:T(8,128)(2,1)}) custom-call(s32[2]{0:T(128)} %pad_add_fusion.x_ref, bf16[96,1024]{1,0:T(8,128)(2,1)} %k_ref.1, bf16[96,1024]{1,0:T(8,128)(2,1)} %v_ref.1), custom_call_target="tpu_custom_call" | custom-call | tf_op jit(solution)/shard_map/pack/pallas_call | solution.py:65
  3.6 0.0 copy-start.14
  3.7 1.6 %collective-permute-start = (bf16[96,512]{1,0:T(8,128)(2,1)}, bf16[96,512]{1,0:T(8,128)(2,1)S(1)}, u32[]{:S(2)}, u32[]{:S(2)}) collective-permute-start(bf16[96,512]{1,0:T(8,128)(2,1)} %get-tuple-element.32), channel_id=1, source_target_pairs={{0,1},{1,2},{2,3},{3,0},{4,5},{5,6},{6,7},{7,4},{8,9},{9,10},{10,1... | collective-permute-start | bytes 294920 | tf_op jit(solution)/shard_map/ppermute | solution.py:317
  5.2 2.7 %collective-permute-start.1 = (bf16[96,512]{1,0:T(8,128)(2,1)}, bf16[96,512]{1,0:T(8,128)(2,1)S(1)}, u32[]{:S(2)}, u32[]{:S(2)}) collective-permute-start(bf16[96,512]{1,0:T(8,128)(2,1)} %get-tuple-element.33), channel_id=1, source_target_pairs={{0,2},{1,3},{2,0},{3,1},{4,6},{5,7},{6,4},{7,5},{8,10},{9,11},{10,... | collective-permute-start | bytes 294920 | tf_op jit(solution)/shard_map/ppermute | solution.py:317
  8.0 1.4 %collective-permute-start.2 = (bf16[96,512]{1,0:T(8,128)(2,1)}, bf16[96,512]{1,0:T(8,128)(2,1)S(1)}, u32[]{:S(2)}, u32[]{:S(2)}) collective-permute-start(bf16[96,512]{1,0:T(8,128)(2,1)} %get-tuple-element.34), channel_id=1, source_target_pairs={{0,3},{1,0},{2,1},{3,2},{4,7},{5,4},{6,5},{7,6},{8,11},{9,8},{10,9... | collective-permute-start | bytes 294920 | tf_op jit(solution)/shard_map/ppermute | solution.py:317
  9.4 3.3 %pack.3 = (bf16[96,2048]{1,0:T(8,128)(2,1)}, bf16[96,2048]{1,0:T(8,128)(2,1)}, bf16[96,2048]{1,0:T(8,128)(2,1)}) custom-call(s32[2]{0:T(128)} %pad_add_fusion.x_ref, bf16[96,4096]{1,0:T(8,128)(2,1)} %q_ref.1, bf16[96,4096]{1,0:T(8,128)(2,1)} %do_ref.1), custom_call_target="tpu_custom_call" | custom-call | tf_op jit(solution)/shard_map/pack/pallas_call | solution.py:65
  12.7 0.0 copy-start
  12.7 0.6 pad.4.doc_ref
  13.3 0.0 collective-permute-done.r1
  13.3 0.0 copy-start.12
  13.3 0.0 collective-permute-done.2.r3
  13.3 0.6 copy-done.11
  13.9 0.0 copy-done.12
  14.0 0.0 copy-done.13
  14.0 2.6 %arrange.1.kv0 = bf16[400,512]{1,0:T(8,128)(2,1)} custom-call(s32[2]{0:T(128)} %pad_add_fusion.x_ref, bf16[96,1024]{1,0:T(8,128)(2,1)} %k_ref.1, bf16[96,1024]{1,0:T(8,128)(2,1)} %v_ref.1, bf16[96,512]{1,0:T(8,128)(2,1)} %copy-done.11, bf16[96,512]{1,0:T(8,128)(2,1)} %copy-done.12, bf16[96,512]{1,0:T(8,128)(2,1)} %copy-done.13, bf16[16,512]{1,0:T(8,128)(2,1)} %pad.4.doc_ref), custom_call_target="tpu_custom_call" | custom-call | tf_op jit(solution)/shard_map/arrange/pallas_call | solution.py:117
  16.6 3.5 %collective-permute-start.3 = (bf16[400,512]{1,0:T(8,128)(2,1)}, bf16[400,512]{1,0:T(8,128)(2,1)S(1)}, u32[]{:S(2)}, u32[]{:S(2)}) collective-permute-start(bf16[400,512]{1,0:T(8,128)(2,1)} %arrange.1.kv0), channel_id=1, source_target_pairs={{0,8},{4,12},{8,16},{12,20},{16,24},{20,28},{24,32},{28,36},{32,40... | collective-permute-start | bytes 1228808 | tf_op jit(solution)/shard_map/ppermute | solution.py:328
  20.1 0.8 collective-permute-start.4
  20.9 2.8 %collective-permute-start.5 = (bf16[96,2048]{1,0:T(8,128)(2,1)}, bf16[96,2048]{1,0:T(8,128)(2,1)S(1)}, u32[]{:S(2)}, u32[]{:S(2)}) collective-permute-start(bf16[96,2048]{1,0:T(8,128)(2,1)} %get-tuple-element.42), channel_id=1, source_target_pairs={{0,2},{1,3},{2,0},{3,1},{4,6},{5,7},{6,4},{7,5},{8,10},{9,11},{10,... | collective-permute-start | bytes 1179656 | tf_op jit(solution)/shard_map/ppermute | solution.py:317
  23.7 1.2 %collective-permute-start.6 = (bf16[96,2048]{1,0:T(8,128)(2,1)}, bf16[96,2048]{1,0:T(8,128)(2,1)S(1)}, u32[]{:S(2)}, u32[]{:S(2)}) collective-permute-start(bf16[96,2048]{1,0:T(8,128)(2,1)} %get-tuple-element.43), channel_id=1, source_target_pairs={{0,3},{1,0},{2,1},{3,2},{4,7},{5,4},{6,5},{7,6},{8,11},{9,8},{10,9... | collective-permute-start | bytes 1179656 | tf_op jit(solution)/shard_map/ppermute | solution.py:317
  24.9 1.9 %collective-permute-start.7 = (bf16[400,512]{1,0:T(8,128)(2,1)}, bf16[400,512]{1,0:T(8,128)(2,1)S(1)}, u32[]{:S(2)}, u32[]{:S(2)}) collective-permute-start(bf16[400,512]{1,0:T(8,128)(2,1)} %arrange.1.kv0), channel_id=1, source_target_pairs={{0,4},{4,16},{8,12},{12,24},{16,20},{20,32},{24,28},{28,40},{32,36... | collective-permute-start | bytes 1228808 | tf_op jit(solution)/shard_map/ppermute | solution.py:328
  26.8 7.0 %collective-permute-done.4.q1 = bf16[96,2048]{1,0:T(8,128)(2,1)S(1)} collective-permute-done((bf16[96,2048]{1,0:T(8,128)(2,1)}, bf16[96,2048]{1,0:T(8,128)(2,1)S(1)}, u32[]{:S(2)}, u32[]{:S(2)}) %collective-permute-start.4) | collective-permute-done | bytes 393248 | tf_op jit(solution)/shard_map/ppermute | solution.py:317
  33.8 5.9 %collective-permute-done.5.q2 = bf16[96,2048]{1,0:T(8,128)(2,1)S(1)} collective-permute-done((bf16[96,2048]{1,0:T(8,128)(2,1)}, bf16[96,2048]{1,0:T(8,128)(2,1)S(1)}, u32[]{:S(2)}, u32[]{:S(2)}) %collective-permute-start.5) | collective-permute-done | bytes 393248 | tf_op jit(solution)/shard_map/ppermute | solution.py:317
  39.8 0.6 collective-permute-done.6.q3
  40.4 1.7 %collective-permute-done.8.kv_a = bf16[400,512]{1,0:T(8,128)(2,1)S(1)} collective-permute-done((bf16[400,512]{1,0:T(8,128)(2,1)S(1)}, bf16[400,512]{1,0:T(8,128)(2,1)S(1)}, u32[]{:S(2)}, u32[]{:S(2)}) %collective-permute-start.8) | collective-permute-done | bytes 409632 | tf_op jit(solution)/shard_map/ppermute | solution.py:328
  42.1 0.6 copy-done.4
  42.7 1.0 %copy-done.2 = bf16[400,512]{1,0:T(8,128)(2,1)S(1)} copy-done((bf16[400,512]{1,0:T(8,128)(2,1)S(1)}, bf16[400,512]{1,0:T(8,128)(2,1)}, u32[]{:S(2)}) %copy-start.2) | copy-done | bytes 409624
  43.7 18.0 %attention.1 = (bf16[96,2048]{1,0:T(8,128)(2,1)S(1)}, bf16[96,2048]{1,0:T(8,128)(2,1)S(1)}, bf16[96,2048]{1,0:T(8,128)(2,1)S(1)}, bf16[96,2048]{1,0:T(8,128)(2,1...) custom-call(s32[2]{0:T(128)S(1)} %copy-done.4, ...), custom_call_target="tpu_custom_call" | custom-call | flops 8000000000 | bytes 8000000 | tf_op jit(solution)/shard_map/attention/pallas_call | solution.py:291
  61.8 0.2 collective-permute-start.13
  62.0 4.3 %collective-permute-start.12 = (bf16[384,512]{1,0:T(8,128)(2,1)}, bf16[384,512]{1,0:T(8,128)(2,1)}, u32[]{:S(2)}, u32[]{:S(2)}) collective-permute-start(bf16[384,512]{1,0:T(8,128)(2,1)} %get-tuple-element.55), channel_id=1, source_target_pairs={{4,0},{12,8},{20,16},{16,4},{28,24},{24,12},{36,32},{32,20},{44,40... | collective-permute-start | bytes 1179656 | tf_op jit(solution)/shard_map/ppermute | solution.py:328
  66.3 0.1 add_convert_fusion.1
  66.5 3.3 %collective-permute-start.14 = (bf16[384,512]{1,0:T(8,128)(2,1)S(1)}, bf16[384,512]{1,0:T(8,128)(2,1)}, u32[]{:S(2)}, u32[]{:S(2)}) collective-permute-start(bf16[384,512]{1,0:T(8,128)(2,1)S(1)} %add_convert_fusion.1), channel_id=1, source_target_pairs={{8,0},{12,4},{16,8},{20,12},{24,16},{28,20},{32,24},{36,28},{40,32... | collective-permute-start | bytes 1179656 | tf_op jit(solution)/shard_map/ppermute | solution.py:328
  69.8 1.8 %collective-permute-start.10 = (bf16[96,2048]{1,0:T(8,128)(2,1)S(1)}, bf16[96,2048]{1,0:T(8,128)(2,1)S(1)}, u32[]{:S(2)}, u32[]{:S(2)}) collective-permute-start(bf16[96,2048]{1,0:T(8,128)(2,1)S(1)} %get-tuple-element.50), channel_id=1, source_target_pairs={{0,2},{1,3},{2,0},{3,1},{4,6},{5,7},{6,4},{7,5},{8,10},{9,11},{10,... | collective-permute-start | bytes 1179656 | tf_op jit(solution)/shard_map/ppermute | solution.py:317
  71.7 2.0 %collective-permute-start.11 = (bf16[96,2048]{1,0:T(8,128)(2,1)S(1)}, bf16[96,2048]{1,0:T(8,128)(2,1)S(1)}, u32[]{:S(2)}, u32[]{:S(2)}) collective-permute-start(bf16[96,2048]{1,0:T(8,128)(2,1)S(1)} %get-tuple-element.51), channel_id=1, source_target_pairs={{0,3},{1,0},{2,1},{3,2},{4,7},{5,4},{6,5},{7,6},{8,11},{9,8},{10,9... | collective-permute-start | bytes 1179656 | tf_op jit(solution)/shard_map/ppermute | solution.py:317
  73.7 8.2 %collective-permute-done.14 = bf16[384,512]{1,0:T(8,128)(2,1)} collective-permute-done((bf16[384,512]{1,0:T(8,128)(2,1)S(1)}, bf16[384,512]{1,0:T(8,128)(2,1)}, u32[]{:S(2)}, u32[]{:S(2)}) %collective-permute-start.14) | collective-permute-done | bytes 393248 | tf_op jit(solution)/shard_map/ppermute | solution.py:328
  81.9 1.3 %add_convert_fusion = bf16[384,512]{1,0:T(8,128)(2,1)S(1)} fusion(bf16[384,512]{1,0:T(8,128)(2,1)} %collective-permute-done.14, f32[384,512]{1,0:T(8,128)S(1)} %get-tuple-element.54, bf16[384,512]{1,0:T(8,128)(2,1)} %collective-permute-done.12), kind=kLoop, calls=%fused_computation | loop fusion | flops 983040 | bytes 1966080 | tf_op jit(solution)/shard_map/convert_element_type | solution.py:355
  83.2 0.7 constant_dynamic-slice_fusion
  83.9 1.1 %collective-permute-start.15 = (bf16[96,512]{1,0:T(8,128)(2,1)S(1)}, bf16[96,512]{1,0:T(8,128)(2,1)S(1)}, u32[]{:S(2)}, u32[]{:S(2)}) collective-permute-start(bf16[96,512]{1,0:T(8,128)(2,1)S(1)} %get-tuple-element.62), channel_id=1, source_target_pairs={{0,1},{1,2},{2,3},{3,0},{4,5},{5,6},{6,7},{7,4},{8,9},{9,10},{10,1... | collective-permute-start | bytes 294920 | tf_op jit(solution)/shard_map/ppermute | solution.py:317
  85.0 3.0 %collective-permute-start.16 = (bf16[96,512]{1,0:T(8,128)(2,1)S(1)}, bf16[96,512]{1,0:T(8,128)(2,1)S(1)}, u32[]{:S(2)}, u32[]{:S(2)}) collective-permute-start(bf16[96,512]{1,0:T(8,128)(2,1)S(1)} %get-tuple-element.61), channel_id=1, source_target_pairs={{0,2},{1,3},{2,0},{3,1},{4,6},{5,7},{6,4},{7,5},{8,10},{9,11},{10,... | collective-permute-start | bytes 294920 | tf_op jit(solution)/shard_map/ppermute | solution.py:317
  88.0 0.3 collective-permute-start.17
  88.3 3.5 %collective-permute-done.11.refs_3_ = bf16[96,2048]{1,0:T(8,128)(2,1)S(1)} collective-permute-done((bf16[96,2048]{1,0:T(8,128)(2,1)S(1)}, bf16[96,2048]{1,0:T(8,128)(2,1)S(1)}, u32[]{:S(2)}, u32[]{:S(2)}) %collective-permute-start.11) | collective-permute-done | bytes 393248 | tf_op jit(solution)/shard_map/ppermute | solution.py:317
  91.8 0.7 copy-done.6
  92.5 0.1 copy-done.7
  92.7 3.4 %unpack.2 = (bf16[96,4096]{1,0:T(8,128)(2,1)}, bf16[96,4096]{1,0:T(8,128)(2,1)}) custom-call(s32[2]{0:T(128)} %pad_add_fusion.x_ref, bf16[96,2048]{1,0:T(8,128)(2,1)} %copy-done.3, bf16[96,2048]{1,0:T(8,128)(2,1)} %copy-done.7, bf16[96,2048]{1,0:T(8,128)(2,1)} %copy-done.5, bf16[96,2048]{1,0:T(8,128)(2,1)} %copy-done.6), custom_call_target="tpu_custom_call" | custom-call | tf_op jit(solution)/shard_map/unpack/pallas_call | solution.py:91
  96.1 0.6 copy-done.8
  96.7 0.0 copy-done.9
  96.8 0.0 copy-done.10
  96.8 2.5 %unpack.3 = (bf16[96,1024]{1,0:T(8,128)(2,1)}, bf16[96,1024]{1,0:T(8,128)(2,1)}) custom-call(s32[2]{0:T(128)} %pad_add_fusion.x_ref, bf16[96,512]{1,0:T(8,128)(2,1)} %get-tuple-element.63.refs_0_, bf16[96,512]{1,0:T(8,128)(2,1)} %copy-done.8, bf16[96,512]{1,0:T(8,128)(2,1)} %copy-done.9, bf16[96,512]{1,0:T(8,128)(2,1)} %copy-done.10), custom_call_target="tpu_custom_call" | custom-call | tf_op jit(solution)/shard_map/unpack/pallas_call | solution.py:91
  (32 shorter events, 0.1 us)
Async XLA Ops:
  3.6 5.7 %copy-start.14 = (s32[384]{0:T(512)S(1)}, s32[384]{0:T(512)}, u32[]{:S(2)}) copy-start(s32[384]{0:T(512)} %param.9) | copy-start | bytes 4612
  3.7 9.6 %collective-permute-start = (bf16[96,512]{1,0:T(8,128)(2,1)}, bf16[96,512]{1,0:T(8,128)(2,1)S(1)}, u32[]{:S(2)}, u32[]{:S(2)}) collective-permute-start(bf16[96,512]{1,0:T(8,128)(2,1)} %get-tuple-element.32), channel_id=1, source_target_pairs={{0,1},{1,2},{2,3},{3,0},{4,5},{5,6},{6,7},{7,4},{8,9},{9,10},{10,1... | collective-permute-start | bytes 294920 | tf_op jit(solution)/shard_map/ppermute | solution.py:317
  5.2 8.1 %collective-permute-start.1 = (bf16[96,512]{1,0:T(8,128)(2,1)}, bf16[96,512]{1,0:T(8,128)(2,1)S(1)}, u32[]{:S(2)}, u32[]{:S(2)}) collective-permute-start(bf16[96,512]{1,0:T(8,128)(2,1)} %get-tuple-element.33), channel_id=1, source_target_pairs={{0,2},{1,3},{2,0},{3,1},{4,6},{5,7},{6,4},{7,5},{8,10},{9,11},{10,... | collective-permute-start | bytes 294920 | tf_op jit(solution)/shard_map/ppermute | solution.py:317
  8.0 5.4 %collective-permute-start.2 = (bf16[96,512]{1,0:T(8,128)(2,1)}, bf16[96,512]{1,0:T(8,128)(2,1)S(1)}, u32[]{:S(2)}, u32[]{:S(2)}) collective-permute-start(bf16[96,512]{1,0:T(8,128)(2,1)} %get-tuple-element.34), channel_id=1, source_target_pairs={{0,3},{1,0},{2,1},{3,2},{4,7},{5,4},{6,5},{7,6},{8,11},{9,8},{10,9... | collective-permute-start | bytes 294920 | tf_op jit(solution)/shard_map/ppermute | solution.py:317
  9.4 32.7 %copy-start.1 = (bf16[96,4096]{1,0:T(8,128)(2,1)S(1)}, bf16[96,4096]{1,0:T(8,128)(2,1)}, u32[]{:S(2)}) copy-start(bf16[96,4096]{1,0:T(8,128)(2,1)} %do_ref.1) | copy-start | bytes 2359300
  12.7 29.4 %copy-start = (bf16[96,4096]{1,0:T(8,128)(2,1)S(1)}, bf16[96,4096]{1,0:T(8,128)(2,1)}, u32[]{:S(2)}) copy-start(bf16[96,4096]{1,0:T(8,128)(2,1)} %q_ref.1) | copy-start | bytes 2359300
  13.3 0.6 copy-start.11
  13.3 0.7 copy-start.12
  13.3 0.7 copy-start.13
  16.6 23.8 %collective-permute-start.3 = (bf16[400,512]{1,0:T(8,128)(2,1)}, bf16[400,512]{1,0:T(8,128)(2,1)S(1)}, u32[]{:S(2)}, u32[]{:S(2)}) collective-permute-start(bf16[400,512]{1,0:T(8,128)(2,1)} %arrange.1.kv0), channel_id=1, source_target_pairs={{0,8},{4,12},{8,16},{12,20},{16,24},{20,28},{24,32},{28,36},{32,40... | collective-permute-start | bytes 1228808 | tf_op jit(solution)/shard_map/ppermute | solution.py:328
  20.1 13.8 %collective-permute-start.4 = (bf16[96,2048]{1,0:T(8,128)(2,1)}, bf16[96,2048]{1,0:T(8,128)(2,1)S(1)}, u32[]{:S(2)}, u32[]{:S(2)}) collective-permute-start(bf16[96,2048]{1,0:T(8,128)(2,1)} %get-tuple-element.41), channel_id=1, source_target_pairs={{0,1},{1,2},{2,3},{3,0},{4,5},{5,6},{6,7},{7,4},{8,9},{9,10},{10,1... | collective-permute-start | bytes 1179656 | tf_op jit(solution)/shard_map/ppermute | solution.py:317
  20.9 18.9 %collective-permute-start.5 = (bf16[96,2048]{1,0:T(8,128)(2,1)}, bf16[96,2048]{1,0:T(8,128)(2,1)S(1)}, u32[]{:S(2)}, u32[]{:S(2)}) collective-permute-start(bf16[96,2048]{1,0:T(8,128)(2,1)} %get-tuple-element.42), channel_id=1, source_target_pairs={{0,2},{1,3},{2,0},{3,1},{4,6},{5,7},{6,4},{7,5},{8,10},{9,11},{10,... | collective-permute-start | bytes 1179656 | tf_op jit(solution)/shard_map/ppermute | solution.py:317
  23.7 16.7 %collective-permute-start.6 = (bf16[96,2048]{1,0:T(8,128)(2,1)}, bf16[96,2048]{1,0:T(8,128)(2,1)S(1)}, u32[]{:S(2)}, u32[]{:S(2)}) collective-permute-start(bf16[96,2048]{1,0:T(8,128)(2,1)} %get-tuple-element.43), channel_id=1, source_target_pairs={{0,3},{1,0},{2,1},{3,2},{4,7},{5,4},{6,5},{7,6},{8,11},{9,8},{10,9... | collective-permute-start | bytes 1179656 | tf_op jit(solution)/shard_map/ppermute | solution.py:317
  24.9 15.5 %collective-permute-start.7 = (bf16[400,512]{1,0:T(8,128)(2,1)}, bf16[400,512]{1,0:T(8,128)(2,1)S(1)}, u32[]{:S(2)}, u32[]{:S(2)}) collective-permute-start(bf16[400,512]{1,0:T(8,128)(2,1)} %arrange.1.kv0), channel_id=1, source_target_pairs={{0,4},{4,16},{8,12},{12,24},{16,20},{20,32},{24,28},{28,40},{32,36... | collective-permute-start | bytes 1228808 | tf_op jit(solution)/shard_map/ppermute | solution.py:328
  40.3 1.7 %collective-permute-start.8 = (bf16[400,512]{1,0:T(8,128)(2,1)S(1)}, bf16[400,512]{1,0:T(8,128)(2,1)S(1)}, u32[]{:S(2)}, u32[]{:S(2)}) collective-permute-start(bf16[400,512]{1,0:T(8,128)(2,1)S(1)} %collective-permute-done.3.kv_c), channel_id=1, source_target_pairs={{0,4},{4,0},{8,12},{12,8},{16,20},{20,16},{24,28},{28,24},{32,36},... | collective-permute-start | bytes 1228808 | tf_op jit(solution)/shard_map/ppermute | solution.py:328
  42.1 0.6 copy-start.4
  42.7 1.0 %copy-start.2 = (bf16[400,512]{1,0:T(8,128)(2,1)S(1)}, bf16[400,512]{1,0:T(8,128)(2,1)}, u32[]{:S(2)}) copy-start(bf16[400,512]{1,0:T(8,128)(2,1)} %arrange.1.kv0) | copy-start | bytes 1228804
  61.8 4.7 %copy-start.3 = (bf16[96,2048]{1,0:T(8,128)(2,1)}, bf16[96,2048]{1,0:T(8,128)(2,1)S(1)}, u32[]{:S(2)}) copy-start(bf16[96,2048]{1,0:T(8,128)(2,1)S(1)} %get-tuple-element.48.refs_0_) | copy-start | bytes 1179652
  61.8 4.5 %collective-permute-start.13 = (bf16[384,512]{1,0:T(8,128)(2,1)S(1)}, bf16[384,512]{1,0:T(8,128)(2,1)S(1)}, u32[]{:S(2)}, u32[]{:S(2)}) collective-permute-start(bf16[384,512]{1,0:T(8,128)(2,1)S(1)} %get-tuple-element.57), channel_id=1, source_target_pairs={{0,4},{4,0},{8,12},{12,8},{16,20},{20,16},{24,28},{28,24},{32,36},... | collective-permute-start | bytes 1179656 | tf_op jit(solution)/shard_map/ppermute | solution.py:328
  62.0 11.7 %collective-permute-start.12 = (bf16[384,512]{1,0:T(8,128)(2,1)}, bf16[384,512]{1,0:T(8,128)(2,1)}, u32[]{:S(2)}, u32[]{:S(2)}) collective-permute-start(bf16[384,512]{1,0:T(8,128)(2,1)} %get-tuple-element.55), channel_id=1, source_target_pairs={{4,0},{12,8},{20,16},{16,4},{28,24},{24,12},{36,32},{32,20},{44,40... | collective-permute-start | bytes 1179656 | tf_op jit(solution)/shard_map/ppermute | solution.py:328
  66.5 15.4 %collective-permute-start.14 = (bf16[384,512]{1,0:T(8,128)(2,1)S(1)}, bf16[384,512]{1,0:T(8,128)(2,1)}, u32[]{:S(2)}, u32[]{:S(2)}) collective-permute-start(bf16[384,512]{1,0:T(8,128)(2,1)S(1)} %add_convert_fusion.1), channel_id=1, source_target_pairs={{8,0},{12,4},{16,8},{20,12},{24,16},{28,20},{32,24},{36,28},{40,32... | collective-permute-start | bytes 1179656 | tf_op jit(solution)/shard_map/ppermute | solution.py:328
  69.8 18.1 %collective-permute-start.10 = (bf16[96,2048]{1,0:T(8,128)(2,1)S(1)}, bf16[96,2048]{1,0:T(8,128)(2,1)S(1)}, u32[]{:S(2)}, u32[]{:S(2)}) collective-permute-start(bf16[96,2048]{1,0:T(8,128)(2,1)S(1)} %get-tuple-element.50), channel_id=1, source_target_pairs={{0,2},{1,3},{2,0},{3,1},{4,6},{5,7},{6,4},{7,5},{8,10},{9,11},{10,... | collective-permute-start | bytes 1179656 | tf_op jit(solution)/shard_map/ppermute | solution.py:317
  71.7 20.1 %collective-permute-start.11 = (bf16[96,2048]{1,0:T(8,128)(2,1)S(1)}, bf16[96,2048]{1,0:T(8,128)(2,1)S(1)}, u32[]{:S(2)}, u32[]{:S(2)}) collective-permute-start(bf16[96,2048]{1,0:T(8,128)(2,1)S(1)} %get-tuple-element.51), channel_id=1, source_target_pairs={{0,3},{1,0},{2,1},{3,2},{4,7},{5,4},{6,5},{7,6},{8,11},{9,8},{10,9... | collective-permute-start | bytes 1179656 | tf_op jit(solution)/shard_map/ppermute | solution.py:317
  73.7 18.1 %collective-permute-start.9 = (bf16[96,2048]{1,0:T(8,128)(2,1)S(1)}, bf16[96,2048]{1,0:T(8,128)(2,1)S(1)}, u32[]{:S(2)}, u32[]{:S(2)}) collective-permute-start(bf16[96,2048]{1,0:T(8,128)(2,1)S(1)} %get-tuple-element.49), channel_id=1, source_target_pairs={{0,1},{1,2},{2,3},{3,0},{4,5},{5,6},{6,7},{7,4},{8,9},{9,10},{10,1... | collective-permute-start | bytes 1179656 | tf_op jit(solution)/shard_map/ppermute | solution.py:317
  83.9 12.2 %collective-permute-start.15 = (bf16[96,512]{1,0:T(8,128)(2,1)S(1)}, bf16[96,512]{1,0:T(8,128)(2,1)S(1)}, u32[]{:S(2)}, u32[]{:S(2)}) collective-permute-start(bf16[96,512]{1,0:T(8,128)(2,1)S(1)} %get-tuple-element.62), channel_id=1, source_target_pairs={{0,1},{1,2},{2,3},{3,0},{4,5},{5,6},{6,7},{7,4},{8,9},{9,10},{10,1... | collective-permute-start | bytes 294920 | tf_op jit(solution)/shard_map/ppermute | solution.py:317
  85.0 11.1 %collective-permute-start.16 = (bf16[96,512]{1,0:T(8,128)(2,1)S(1)}, bf16[96,512]{1,0:T(8,128)(2,1)S(1)}, u32[]{:S(2)}, u32[]{:S(2)}) collective-permute-start(bf16[96,512]{1,0:T(8,128)(2,1)S(1)} %get-tuple-element.61), channel_id=1, source_target_pairs={{0,2},{1,3},{2,0},{3,1},{4,6},{5,7},{6,4},{7,5},{8,10},{9,11},{10,... | collective-permute-start | bytes 294920 | tf_op jit(solution)/shard_map/ppermute | solution.py:317
  87.9 3.8 %copy-start.5 = (bf16[96,2048]{1,0:T(8,128)(2,1)}, bf16[96,2048]{1,0:T(8,128)(2,1)S(1)}, u32[]{:S(2)}) copy-start(bf16[96,2048]{1,0:T(8,128)(2,1)S(1)} %collective-permute-done.10.refs_2_) | copy-start | bytes 1179652
  88.0 8.2 %collective-permute-start.17 = (bf16[96,512]{1,0:T(8,128)(2,1)S(1)}, bf16[96,512]{1,0:T(8,128)(2,1)S(1)}, u32[]{:S(2)}, u32[]{:S(2)}) collective-permute-start(bf16[96,512]{1,0:T(8,128)(2,1)S(1)} %get-tuple-element.60), channel_id=1, source_target_pairs={{0,3},{1,0},{2,1},{3,2},{4,7},{5,4},{6,5},{7,6},{8,11},{9,8},{10,9... | collective-permute-start | bytes 294920 | tf_op jit(solution)/shard_map/ppermute | solution.py:317
  91.8 0.7 copy-start.6
  91.8 0.9 copy-start.7
  96.1 0.6 copy-start.8
  96.1 0.6 copy-start.9
  96.1 0.7 copy-start.10

commit v3 on v2

--- a/solution.py
+++ b/solution.py
@@ -20,8 +20,10 @@
 MASKED = -1e30
 SCALE = HDIM**-0.5
 EXP_SCALE = SCALE * math.log2(math.e)
+SMALL = pltpu.CompilerParams(vmem_limit_bytes=4 * 1024 * 1024)
 ANY = pl.BlockSpec(memory_space=pl.ANY)
 SMEM = pl.BlockSpec(memory_space=pltpu.SMEM)
+HBM = pl.BlockSpec(memory_space=pltpu.HBM)
 VMEM = pl.BlockSpec(memory_space=pltpu.VMEM)
 BF16, F32 = jnp.bfloat16, jnp.float32
 
@@ -68,8 +70,19 @@
         out_specs=[VMEM] * 3,
         out_shape=[struct((PART, 4 * width), BF16)] * 3,
         scratch_shapes=[pltpu.SemaphoreType.DMA((12,))],
+        compiler_params=SMALL,
         name="pack",
     )(x, a, b)
+
+
+def cut(x, a, b):
+    width = a.shape[1] // 8
+    pieces = []
+    for p in range(1, 4):
+        place = (x + p) % 4 * (2 * width)
+        cuts = [lax.dynamic_slice_in_dim(src, place + g * width, width, 1) for g in range(2) for src in (a, b)]
+        pieces.append(jnp.concatenate(cuts, 1))
+    return pieces
 
 
 def unpack_kernel(width, x_ref, *refs):
@@ -94,6 +107,7 @@
         out_specs=[VMEM] * 2,
         out_shape=[whole] * 2,
         scratch_shapes=[pltpu.SemaphoreType.DMA((16,))],
+        compiler_params=SMALL,
         name="unpack",
     )(x, *parts)
 
@@ -120,6 +134,7 @@
         out_specs=VMEM,
         out_shape=struct((ROWS + 16, KVW), BF16),
         scratch_shapes=[pltpu.SemaphoreType.DMA((8,))],
+        compiler_params=SMALL,
         name="arrange",
     )(x, keys, values, *received, docs)
 
@@ -307,10 +322,44 @@
             pltpu.VMEM((units, 2, HDIM, width), BF16),
             pltpu.SemaphoreType.DMA((20,)),
         ],
-        compiler_params=pltpu.CompilerParams(vmem_limit_bytes=40 * 1024 * 1024),
+        compiler_params=pltpu.CompilerParams(vmem_limit_bytes=28 * 1024 * 1024),
         cost_estimate=pl.CostEstimate(flops=8_000_000_000, bytes_accessed=8_000_000, transcendentals=4_000_000),
         name="attention",
     )(place, queries, out_grad, *received, kv0, kv_b, kv_c, kv_a, docs)
+
+
+def arrived_kernel(docs_ref, *refs):
+    refs[-1][...] = docs_ref[...]
+
+
+def arrived(docs, received, work):
+    return pl.pallas_call(
+        arrived_kernel,
+        in_specs=[VMEM] + [ANY] * len(received),
+        out_specs=VMEM,
+        out_shape=struct(docs.shape, docs.dtype),
+        compiler_params=SMALL,
+        cost_estimate=pl.CostEstimate(flops=work, bytes_accessed=1_000_000, transcendentals=0),
+        name="arrived",
+    )(docs, *received)
+
+
+def total_kernel(x_ref, own_ref, b_ref, c_ref, docs_ref, *outs):
+    del docs_ref
+    for p, out in enumerate(outs):
+        rows = pl.ds(pl.multiple_of(lax.rem(x_ref[0] + p, 4) * PART, PART), PART)
+        out[...] = (own_ref[rows] + b_ref[rows].astype(F32) + c_ref[rows].astype(F32)).astype(BF16)
+
+
+def total(place, own, back_b, back_c, docs):
+    return pl.pallas_call(
+        total_kernel,
+        in_specs=[SMEM] + [VMEM] * 4,
+        out_specs=[VMEM] * 4,
+        out_shape=[struct((PART, KVW), BF16)] * 4,
+        compiler_params=SMALL,
+        name="total",
+    )(place, own, back_b, back_c, docs)
 
 
 def around(block, distance):
@@ -334,27 +383,28 @@
     doc_number = doc_ids + 1
     docs_low = jnp.pad(doc_number.astype(BF16)[None, :], ((0, 15), (0, KVW - ROWS)))
     docs = jnp.broadcast_to(doc_number.astype(F32)[None, :], (8, ROWS))
-    kv_received = [around(piece, p + 1) for p, piece in enumerate(pack(place, keys, values))]
+    kv_received = [around(piece, p + 1) for p, piece in enumerate(cut(x, keys, values))]
     q_pieces = pack(place, queries, out_grad)
     kv_received, q_pieces = lax.optimization_barrier((kv_received, q_pieces))
     q_received = [around(piece, p + 1) for p, piece in enumerate(q_pieces)]
     kv0 = arrange(place, keys, values, kv_received, docs_low)
     kv_c = over_chips(kv0, [(0, 1, 0), (1, 1, 1)])
     kv_b = over_chips(kv0, [(0, 0, 1), (1, 2, 0)])
-    kv_c, q_received = lax.optimization_barrier((kv_c, q_received))
+    kv_c, docs = lax.optimization_barrier((kv_c, arrived(docs, q_received, 40_000_000_000)))
     kv_a = over_chips(kv_c, [(0, 0, 1), (1, 0, 0)])
     o0, o1, o2, o3, own, far, swap, near = attention(
         place, queries, out_grad, q_received, kv0, kv_b, kv_c, kv_a, docs
     )
     back_a = over_chips(swap, [(0, 0, 1), (1, 0, 0)])
     near = (near + back_a.astype(F32)).astype(BF16)
+    near, far = lax.optimization_barrier((near, far))
+    back_b = over_chips(far, [(1, 0, 0), (0, -2, 1)])
     back_c = over_chips(near, [(0, -1, 0), (1, -1, 1)])
-    back_b = over_chips(far, [(1, 0, 0), (0, -2, 1)])
     outs = [o0] + [around(piece, p) for p, piece in ((1, o1), (2, o2), (3, o3))]
+    docs = arrived(docs, outs[1:], 4_000_000_000)
+    parts = total(place, own, back_b, back_c, docs)
+    grads = [parts[0]] + [around(parts[p], p) for p in (1, 2, 3)]
     attention_out, query_grad = unpack(place, outs)
-    total = (own + back_b.astype(F32) + back_c.astype(F32)).astype(BF16)
-    parts = [lax.dynamic_slice_in_dim(total, (x + p) % 4 * PART, PART, 0) for p in range(4)]
-    grads = [parts[0]] + [around(parts[p], p) for p in (1, 2, 3)]
     key_grad, value_grad = unpack(place, grads)
     return attention_out, query_grad, key_grad, value_grad
 

time: 100 us -> 87.7 us (0.88)
  Pallas kernels: 32.2 us -> 23.6 us
  waiting for transfers between devices: 27.1 us -> 31 us
  local copies, waits for them, and re-layouts: 5.13 us -> 2.16 us
  starting transfers between devices: 32 us -> 29.2 us
  other arithmetic: 2.01 us -> 0.25 us
    ppermute x12, waiting for transfers between devices: 17.1 us -> 25.5 us  [around(): lax.ppermute(block, 'head', [(i, (i + distance) % 4) for i in range(4)])]
    pallas_call x2 -> x1, Pallas kernels: 5.65 us -> 0.86 us  [pack(): pl.pallas_call(functools.partial(pack_kernel, width), in_specs=[SMEM, ANY...]
    ppermute x6, waiting for transfers between devices: 9.95 us -> 5.5 us  [over_chips(): return lax.ppermute(block, ('chip', 'core'), pairs)]
    ppermute x6, starting transfers between devices: 13.2 us -> 9.79 us  [over_chips(): return lax.ppermute(block, ('chip', 'core'), pairs)]
    unnamed x30 -> x12, local copies, waits for them, and re-layouts: 3.84 us -> 1.15 us
    pallas_call x2, Pallas kernels: 5.92 us -> 3.68 us  [unpack(): pl.pallas_call(functools.partial(unpack_kernel, width), in_specs=[SMEM] +...]
    pallas_call x1, Pallas kernels: 2.56 us -> 1.07 us  [arrange(): pl.pallas_call(arrange_kernel, in_specs=[SMEM] + [ANY] * 6, out_specs=VME...]
    convert_element_type x1 -> x0, other arithmetic: 1.27 us -> none  [local(): total = (own + back_b.astype(F32) + back_c.astype(F32)).astype(BF16)]
  transfers between devices with their start and end apart: 18 -> 18, of which waited for: 6 -> 10; matrix products, arithmetic and copies ran while one was open for 3% -> 0% of each run, Pallas kernels for 7% -> 5%
where the time goes in v3:
time: 87.7 us; the launch traced here: 87.2 us
  waiting for transfers between devices  31 us (35%)
  starting transfers between devices  29.2 us (33%)
  Pallas kernels  23.6 us (27%)
  local copies, waits for them, and re-layouts  2.16 us (2%)
  between operations  1.03 us (1%)
    ppermute x12, waiting for transfers between devices, around(): lax.ppermute(block, 'head', [(i, (i + distance) % 4) for i in range(4)])  25.5 us
    ppermute x12, starting transfers between devices, around(): lax.ppermute(block, 'head', [(i, (i + distance) % 4) for i in range(4)])  19.4 us
    pallas_call x1, Pallas kernels, attention(): pl.pallas_call(attention_kernel, in_specs=[SMEM] + [ANY] * 9 + [VMEM], ou...  17.3 us
    ppermute x6, starting transfers between devices, over_chips(): return lax.ppermute(block, ('chip', 'core'), pairs)  9.79 us
    ppermute x6, waiting for transfers between devices, over_chips(): return lax.ppermute(block, ('chip', 'core'), pairs)  5.5 us
    pallas_call x2, Pallas kernels, unpack(): pl.pallas_call(functools.partial(unpack_kernel, width), in_specs=[SMEM] +...  3.68 us
  transfers between devices with their start and end apart: 18, of which 10 were waited for; matrix products, arithmetic and copies ran while one was open for 0% of the time, Pallas kernels for 5%

profile of v3, /device:TPU:128, one launch (start us, length us, event | category | flops | bytes accessed | tf_op | source)
XLA Modules:
  0.0 87.2 jit_solution(17442844520351212426)
XLA Ops:
  0.6 0.0 copy-start
  0.7 1.0 %constant_dynamic-slice_fusion.2 = (bf16[96,128]{1,0:T(8,128)(2,1)S(1)}, bf16[96,128]{1,0:T(8,128)(2,1)S(1)}, bf16[96,128]{1,0:T(8,128)(2,1)S(1)}, bf16[96,128]{...) fusion(bf16[96,1024]{1,0:T(8,128)(2,1)} %v_ref.1, ...), kind=kLoop, calls=%fused_computation.6 | loop fusion | bytes 589848 | tf_op jit(solution)/shard_map/dynamic_slice | solution.py:83
  1.7 1.6 %collective-permute-start = (bf16[96,512]{1,0:T(8,128)(2,1)S(1)}, bf16[96,512]{1,0:T(8,128)(2,1)S(1)}, u32[]{:S(2)}, u32[]{:S(2)}) collective-permute-start(bf16[96,512]{1,0:T(8,128)(2,1)S(1)} %pad_maximum_fusion), channel_id=1, source_target_pairs={{0,1},{1,2},{2,3},{3,0},{4,5},{5,6},{6,7},{7,4},{8,9},{9,10},{10,1... | collective-permute-start | bytes 294920 | tf_op jit(solution)/shard_map/ppermute | solution.py:366
  3.3 2.8 %collective-permute-start.1 = (bf16[96,512]{1,0:T(8,128)(2,1)S(1)}, bf16[96,512]{1,0:T(8,128)(2,1)S(1)}, u32[]{:S(2)}, u32[]{:S(2)}) collective-permute-start(bf16[96,512]{1,0:T(8,128)(2,1)S(1)} %pad_maximum_fusion.1), channel_id=1, source_target_pairs={{0,2},{1,3},{2,0},{3,1},{4,6},{5,7},{6,4},{7,5},{8,10},{9,11},{10,... | collective-permute-start | bytes 294920 | tf_op jit(solution)/shard_map/ppermute | solution.py:366
  6.1 1.5 %collective-permute-start.2 = (bf16[96,512]{1,0:T(8,128)(2,1)S(1)}, bf16[96,512]{1,0:T(8,128)(2,1)S(1)}, u32[]{:S(2)}, u32[]{:S(2)}) collective-permute-start(bf16[96,512]{1,0:T(8,128)(2,1)S(1)} %pad_maximum_fusion.2), channel_id=1, source_target_pairs={{0,3},{1,0},{2,1},{3,2},{4,7},{5,4},{6,5},{7,6},{8,11},{9,8},{10,9... | collective-permute-start | bytes 294920 | tf_op jit(solution)/shard_map/ppermute | solution.py:366
  7.6 0.1 pad_add_fusion.x_ref
  7.7 0.0 copy-done
  7.7 1.1 %copy-done.1 = bf16[96,4096]{1,0:T(8,128)(2,1)S(1)} copy-done((bf16[96,4096]{1,0:T(8,128)(2,1)S(1)}, bf16[96,4096]{1,0:T(8,128)(2,1)}, u32[]{:S(2)}) %copy-start.1) | copy-done | bytes 786456
  8.9 0.9 pack.1
  9.7 0.0 collective-permute-done.r1
  9.7 0.9 %collective-permute-done.1.r2 = bf16[96,512]{1,0:T(8,128)(2,1)S(1)} collective-permute-done((bf16[96,512]{1,0:T(8,128)(2,1)S(1)}, bf16[96,512]{1,0:T(8,128)(2,1)S(1)}, u32[]{:S(2)}, u32[]{:S(2)}) %collective-permute-start.1) | collective-permute-done | bytes 98336 | tf_op jit(solution)/shard_map/ppermute | solution.py:366
  10.6 0.2 collective-permute-done.2.r3
  10.8 1.3 %collective-permute-start.3 = (bf16[96,2048]{1,0:T(8,128)(2,1)S(1)}, bf16[96,2048]{1,0:T(8,128)(2,1)S(1)}, u32[]{:S(2)}, u32[]{:S(2)}) collective-permute-start(bf16[96,2048]{1,0:T(8,128)(2,1)S(1)} %get-tuple-element.36), channel_id=1, source_target_pairs={{0,1},{1,2},{2,3},{3,0},{4,5},{5,6},{6,7},{7,4},{8,9},{9,10},{10,1... | collective-permute-start | bytes 1179656 | tf_op jit(solution)/shard_map/ppermute | solution.py:366
  12.2 2.8 %collective-permute-start.4 = (bf16[96,2048]{1,0:T(8,128)(2,1)S(1)}, bf16[96,2048]{1,0:T(8,128)(2,1)S(1)}, u32[]{:S(2)}, u32[]{:S(2)}) collective-permute-start(bf16[96,2048]{1,0:T(8,128)(2,1)S(1)} %get-tuple-element.37), channel_id=1, source_target_pairs={{0,2},{1,3},{2,0},{3,1},{4,6},{5,7},{6,4},{7,5},{8,10},{9,11},{10,... | collective-permute-start | bytes 1179656 | tf_op jit(solution)/shard_map/ppermute | solution.py:366
  14.9 1.1 %collective-permute-start.5 = (bf16[96,2048]{1,0:T(8,128)(2,1)S(1)}, bf16[96,2048]{1,0:T(8,128)(2,1)S(1)}, u32[]{:S(2)}, u32[]{:S(2)}) collective-permute-start(bf16[96,2048]{1,0:T(8,128)(2,1)S(1)} %get-tuple-element.38), channel_id=1, source_target_pairs={{0,3},{1,0},{2,1},{3,2},{4,7},{5,4},{6,5},{7,6},{8,11},{9,8},{10,9... | collective-permute-start | bytes 1179656 | tf_op jit(solution)/shard_map/ppermute | solution.py:366
  16.1 1.1 %arrange.1.kv0 = bf16[400,512]{1,0:T(8,128)(2,1)S(1)} custom-call(s32[2]{0:T(128)S(1)} %pad_add_fusion.x_ref, bf16[96,1024]{1,0:T(8,128)(2,1)S(1)} %copy-done.3, bf16[96,1024]{1,0:T(8,128)(2,1)S(1)} %copy-done.4, bf16[96,512]{1,0:T(8,128)(2,1)S(1)} %collective-permute-done.r1, bf16[96,512]{1,0:T(8,128)(2,1)S(1)} %collective-permute-done.1.r2, ...), custom_call_target="tpu_custom_call" | custom-call | tf_op jit(solution)/shard_map/arrange/pallas_call | solution.py:131
  17.2 3.5 %collective-permute-start.7 = (bf16[400,512]{1,0:T(8,128)(2,1)S(1)}, bf16[400,512]{1,0:T(8,128)(2,1)S(1)}, u32[]{:S(2)}, u32[]{:S(2)}) collective-permute-start(bf16[400,512]{1,0:T(8,128)(2,1)S(1)} %arrange.1.kv0), channel_id=1, source_target_pairs={{0,8},{4,12},{8,16},{12,20},{16,24},{20,28},{24,32},{28,36},{32,40... | collective-permute-start | bytes 1228808 | tf_op jit(solution)/shard_map/ppermute | solution.py:377
  20.7 1.9 %collective-permute-start.6 = (bf16[400,512]{1,0:T(8,128)(2,1)S(1)}, bf16[400,512]{1,0:T(8,128)(2,1)S(1)}, u32[]{:S(2)}, u32[]{:S(2)}) collective-permute-start(bf16[400,512]{1,0:T(8,128)(2,1)S(1)} %arrange.1.kv0), channel_id=1, source_target_pairs={{0,4},{4,16},{8,12},{12,24},{16,20},{20,32},{24,28},{28,40},{32,36... | collective-permute-start | bytes 1228808 | tf_op jit(solution)/shard_map/ppermute | solution.py:377
  22.6 1.2 %collective-permute-done.3.refs_0_.q1 = bf16[96,2048]{1,0:T(8,128)(2,1)S(1)} collective-permute-done((bf16[96,2048]{1,0:T(8,128)(2,1)S(1)}, bf16[96,2048]{1,0:T(8,128)(2,1)S(1)}, u32[]{:S(2)}, u32[]{:S(2)}) %collective-permute-start.3) | collective-permute-done | bytes 393248 | tf_op jit(solution)/shard_map/ppermute | solution.py:366
  23.8 7.3 %collective-permute-done.4.refs_1_.q2 = bf16[96,2048]{1,0:T(8,128)(2,1)S(1)} collective-permute-done((bf16[96,2048]{1,0:T(8,128)(2,1)S(1)}, bf16[96,2048]{1,0:T(8,128)(2,1)S(1)}, u32[]{:S(2)}, u32[]{:S(2)}) %collective-permute-start.4) | collective-permute-done | bytes 393248 | tf_op jit(solution)/shard_map/ppermute | solution.py:366
  31.0 0.0 collective-permute-done.5.refs_2_.q3
  31.0 3.8 %collective-permute-done.7.kv_c = bf16[400,512]{1,0:T(8,128)(2,1)S(1)} collective-permute-done((bf16[400,512]{1,0:T(8,128)(2,1)S(1)}, bf16[400,512]{1,0:T(8,128)(2,1)S(1)}, u32[]{:S(2)}, u32[]{:S(2)}) %collective-permute-start.7) | collective-permute-done | bytes 409632 | tf_op jit(solution)/shard_map/ppermute | solution.py:377
  34.8 0.0 collective-permute-start.8
  34.8 1.2 %collective-permute-done.6.kv_b = bf16[400,512]{1,0:T(8,128)(2,1)S(1)} collective-permute-done((bf16[400,512]{1,0:T(8,128)(2,1)S(1)}, bf16[400,512]{1,0:T(8,128)(2,1)S(1)}, u32[]{:S(2)}, u32[]{:S(2)}) %collective-permute-start.6) | collective-permute-done | bytes 409632 | tf_op jit(solution)/shard_map/ppermute | solution.py:377
  36.0 0.6 collective-permute-done.8.kv_a
  36.5 17.3 %attention.1 = (bf16[96,2048]{1,0:T(8,128)(2,1)S(1)}, bf16[96,2048]{1,0:T(8,128)(2,1)S(1)}, bf16[96,2048]{1,0:T(8,128)(2,1)S(1)}, bf16[96,2048]{1,0:T(8,128)(2,1...) custom-call(s32[2]{0:T(128)S(1)} %pad_add_fusion.x_ref, ...), custom_call_target="tpu_custom_call" | custom-call | flops 8000000000 | bytes 8000000 | tf_op jit(solution)/shard_map/attention/pallas_call | solution.py:306
  53.8 0.2 collective-permute-start.12
  54.1 0.9 collective-permute-start.9
  54.9 1.0 %collective-permute-start.10 = (bf16[96,2048]{1,0:T(8,128)(2,1)S(1)}, bf16[96,2048]{1,0:T(8,128)(2,1)S(1)}, u32[]{:S(2)}, u32[]{:S(2)}) collective-permute-start(bf16[96,2048]{1,0:T(8,128)(2,1)S(1)} %get-tuple-element.46), channel_id=1, source_target_pairs={{0,2},{1,3},{2,0},{3,1},{4,6},{5,7},{6,4},{7,5},{8,10},{9,11},{10,... | collective-permute-start | bytes 1179656 | tf_op jit(solution)/shard_map/ppermute | solution.py:366
  55.9 2.3 %collective-permute-start.11 = (bf16[96,2048]{1,0:T(8,128)(2,1)S(1)}, bf16[96,2048]{1,0:T(8,128)(2,1)S(1)}, u32[]{:S(2)}, u32[]{:S(2)}) collective-permute-start(bf16[96,2048]{1,0:T(8,128)(2,1)S(1)} %get-tuple-element.47), channel_id=1, source_target_pairs={{0,3},{1,0},{2,1},{3,2},{4,7},{5,4},{6,5},{7,6},{8,11},{9,8},{10,9... | collective-permute-start | bytes 1179656 | tf_op jit(solution)/shard_map/ppermute | solution.py:366
  58.2 0.0 collective-permute-done.12
  58.2 0.1 add_convert_fusion
  58.3 1.9 %collective-permute-start.13 = (bf16[384,512]{1,0:T(8,128)(2,1)S(1)}, bf16[384,512]{1,0:T(8,128)(2,1)S(1)}, u32[]{:S(2)}, u32[]{:S(2)}) collective-permute-start(bf16[384,512]{1,0:T(8,128)(2,1)S(1)} %get-tuple-element.54), channel_id=1, source_target_pairs={{4,0},{12,8},{20,16},{16,4},{28,24},{24,12},{36,32},{32,20},{44,40... | collective-permute-start | bytes 1179656 | tf_op jit(solution)/shard_map/ppermute | solution.py:377
  60.2 2.2 %collective-permute-start.14 = (bf16[384,512]{1,0:T(8,128)(2,1)S(1)}, bf16[384,512]{1,0:T(8,128)(2,1)S(1)}, u32[]{:S(2)}, u32[]{:S(2)}) collective-permute-start(bf16[384,512]{1,0:T(8,128)(2,1)S(1)} %add_convert_fusion), channel_id=1, source_target_pairs={{8,0},{12,4},{16,8},{20,12},{24,16},{28,20},{32,24},{36,28},{40,32... | collective-permute-start | bytes 1179656 | tf_op jit(solution)/shard_map/ppermute | solution.py:377
  62.5 12.6 %collective-permute-done.9.refs_1_.refs_0_ = bf16[96,2048]{1,0:T(8,128)(2,1)S(1)} collective-permute-done((bf16[96,2048]{1,0:T(8,128)(2,1)S(1)}, bf16[96,2048]{1,0:T(8,128)(2,1)S(1)}, u32[]{:S(2)}, u32[]{:S(2)}) %collective-permute-start.9) | collective-permute-done | bytes 393248 | tf_op jit(solution)/shard_map/ppermute | solution.py:366
  75.1 0.0 collective-permute-done.10.refs_2_.refs_1_
  75.1 0.6 collective-permute-done.11.refs_3_.refs_2_
  75.7 0.0 collective-permute-done.13.b_ref
  75.7 0.0 collective-permute-done.14.c_ref
  75.7 0.7 total.1
  76.4 1.0 %collective-permute-start.15 = (bf16[96,512]{1,0:T(8,128)(2,1)S(1)}, bf16[96,512]{1,0:T(8,128)(2,1)S(1)}, u32[]{:S(2)}, u32[]{:S(2)}) collective-permute-start(bf16[96,512]{1,0:T(8,128)(2,1)S(1)} %get-tuple-element.57), channel_id=1, source_target_pairs={{0,1},{1,2},{2,3},{3,0},{4,5},{5,6},{6,7},{7,4},{8,9},{9,10},{10,1... | collective-permute-start | bytes 294920 | tf_op jit(solution)/shard_map/ppermute | solution.py:366
  77.4 3.2 %collective-permute-start.16 = (bf16[96,512]{1,0:T(8,128)(2,1)S(1)}, bf16[96,512]{1,0:T(8,128)(2,1)S(1)}, u32[]{:S(2)}, u32[]{:S(2)}) collective-permute-start(bf16[96,512]{1,0:T(8,128)(2,1)S(1)} %get-tuple-element.58), channel_id=1, source_target_pairs={{0,2},{1,3},{2,0},{3,1},{4,6},{5,7},{6,4},{7,5},{8,10},{9,11},{10,... | collective-permute-start | bytes 294920 | tf_op jit(solution)/shard_map/ppermute | solution.py:366
  80.6 0.0 collective-permute-start.17
  80.6 2.1 %unpack.2 = (bf16[96,4096]{1,0:T(8,128)(2,1)}, bf16[96,4096]{1,0:T(8,128)(2,1)}) custom-call(s32[2]{0:T(128)S(1)} %pad_add_fusion.x_ref, bf16[96,2048]{1,0:T(8,128)(2,1)S(1)} %get-tuple-element.44.refs_0_, bf16[96,2048]{1,0:T(8,128)(2,1)S(1)} %collective-permute-done.9.refs_1_.refs_0_, bf16[96,2048]{1,0:T(8,128)(2,1)S(1)} %collective-permute-done.10.refs_2_.refs_1_, ...), custom_call_target="tpu_custom_call" | custom-call | tf_op jit(solution)/shard_map/unpack/pallas_call | solution.py:104
  82.7 0.0 collective-permute-done.15.refs_1_
  82.7 2.7 %collective-permute-done.16.refs_2_ = bf16[96,512]{1,0:T(8,128)(2,1)S(1)} collective-permute-done((bf16[96,512]{1,0:T(8,128)(2,1)S(1)}, bf16[96,512]{1,0:T(8,128)(2,1)S(1)}, u32[]{:S(2)}, u32[]{:S(2)}) %collective-permute-start.16) | collective-permute-done | bytes 98336 | tf_op jit(solution)/shard_map/ppermute | solution.py:366
  85.4 0.0 collective-permute-done.17.refs_3_
  85.4 1.6 %unpack.3 = (bf16[96,1024]{1,0:T(8,128)(2,1)}, bf16[96,1024]{1,0:T(8,128)(2,1)}) custom-call(s32[2]{0:T(128)S(1)} %pad_add_fusion.x_ref, bf16[96,512]{1,0:T(8,128)(2,1)S(1)} %get-tuple-element.56.refs_0_, bf16[96,512]{1,0:T(8,128)(2,1)S(1)} %collective-permute-done.15.refs_1_, bf16[96,512]{1,0:T(8,128)(2,1)S(1)} %collective-permute-done.16.refs_2_, ...), custom_call_target="tpu_custom_call" | custom-call | tf_op jit(solution)/shard_map/unpack/pallas_call | solution.py:104
  (18 shorter events, 0.1 us)
Async XLA Ops:
  0.6 7.1 %copy-start = (bf16[96,4096]{1,0:T(8,128)(2,1)S(1)}, bf16[96,4096]{1,0:T(8,128)(2,1)}, u32[]{:S(2)}) copy-start(bf16[96,4096]{1,0:T(8,128)(2,1)} %q_ref.1) | copy-start | bytes 2359300
  1.7 8.0 %collective-permute-start = (bf16[96,512]{1,0:T(8,128)(2,1)S(1)}, bf16[96,512]{1,0:T(8,128)(2,1)S(1)}, u32[]{:S(2)}, u32[]{:S(2)}) collective-permute-start(bf16[96,512]{1,0:T(8,128)(2,1)S(1)} %pad_maximum_fusion), channel_id=1, source_target_pairs={{0,1},{1,2},{2,3},{3,0},{4,5},{5,6},{6,7},{7,4},{8,9},{9,10},{10,1... | collective-permute-start | bytes 294920 | tf_op jit(solution)/shard_map/ppermute | solution.py:366
  3.3 7.3 %collective-permute-start.1 = (bf16[96,512]{1,0:T(8,128)(2,1)S(1)}, bf16[96,512]{1,0:T(8,128)(2,1)S(1)}, u32[]{:S(2)}, u32[]{:S(2)}) collective-permute-start(bf16[96,512]{1,0:T(8,128)(2,1)S(1)} %pad_maximum_fusion.1), channel_id=1, source_target_pairs={{0,2},{1,3},{2,0},{3,1},{4,6},{5,7},{6,4},{7,5},{8,10},{9,11},{10,... | collective-permute-start | bytes 294920 | tf_op jit(solution)/shard_map/ppermute | solution.py:366
  6.1 4.7 %collective-permute-start.2 = (bf16[96,512]{1,0:T(8,128)(2,1)S(1)}, bf16[96,512]{1,0:T(8,128)(2,1)S(1)}, u32[]{:S(2)}, u32[]{:S(2)}) collective-permute-start(bf16[96,512]{1,0:T(8,128)(2,1)S(1)} %pad_maximum_fusion.2), channel_id=1, source_target_pairs={{0,3},{1,0},{2,1},{3,2},{4,7},{5,4},{6,5},{7,6},{8,11},{9,8},{10,9... | collective-permute-start | bytes 294920 | tf_op jit(solution)/shard_map/ppermute | solution.py:366
  7.7 1.1 %copy-start.1 = (bf16[96,4096]{1,0:T(8,128)(2,1)S(1)}, bf16[96,4096]{1,0:T(8,128)(2,1)}, u32[]{:S(2)}) copy-start(bf16[96,4096]{1,0:T(8,128)(2,1)} %do_ref.1) | copy-start | bytes 2359300
  8.9 7.2 %copy-start.3 = (bf16[96,1024]{1,0:T(8,128)(2,1)S(1)}, bf16[96,1024]{1,0:T(8,128)(2,1)}, u32[]{:S(2)}) copy-start(bf16[96,1024]{1,0:T(8,128)(2,1)} %k_ref.1) | copy-start | bytes 589828
  8.9 7.2 %copy-start.4 = (bf16[96,1024]{1,0:T(8,128)(2,1)S(1)}, bf16[96,1024]{1,0:T(8,128)(2,1)}, u32[]{:S(2)}) copy-start(bf16[96,1024]{1,0:T(8,128)(2,1)} %v_ref.1) | copy-start | bytes 589828
  10.8 5.2 %copy-start.5 = (s32[384]{0:T(512)S(1)}, s32[384]{0:T(512)}, u32[]{:S(2)}) copy-start(s32[384]{0:T(512)} %param.9) | copy-start | bytes 4612
  10.8 12.9 %collective-permute-start.3 = (bf16[96,2048]{1,0:T(8,128)(2,1)S(1)}, bf16[96,2048]{1,0:T(8,128)(2,1)S(1)}, u32[]{:S(2)}, u32[]{:S(2)}) collective-permute-start(bf16[96,2048]{1,0:T(8,128)(2,1)S(1)} %get-tuple-element.36), channel_id=1, source_target_pairs={{0,1},{1,2},{2,3},{3,0},{4,5},{5,6},{6,7},{7,4},{8,9},{9,10},{10,1... | collective-permute-start | bytes 1179656 | tf_op jit(solution)/shard_map/ppermute | solution.py:366
  12.2 18.8 %collective-permute-start.4 = (bf16[96,2048]{1,0:T(8,128)(2,1)S(1)}, bf16[96,2048]{1,0:T(8,128)(2,1)S(1)}, u32[]{:S(2)}, u32[]{:S(2)}) collective-permute-start(bf16[96,2048]{1,0:T(8,128)(2,1)S(1)} %get-tuple-element.37), channel_id=1, source_target_pairs={{0,2},{1,3},{2,0},{3,1},{4,6},{5,7},{6,4},{7,5},{8,10},{9,11},{10,... | collective-permute-start | bytes 1179656 | tf_op jit(solution)/shard_map/ppermute | solution.py:366
  14.9 16.1 %collective-permute-start.5 = (bf16[96,2048]{1,0:T(8,128)(2,1)S(1)}, bf16[96,2048]{1,0:T(8,128)(2,1)S(1)}, u32[]{:S(2)}, u32[]{:S(2)}) collective-permute-start(bf16[96,2048]{1,0:T(8,128)(2,1)S(1)} %get-tuple-element.38), channel_id=1, source_target_pairs={{0,3},{1,0},{2,1},{3,2},{4,7},{5,4},{6,5},{7,6},{8,11},{9,8},{10,9... | collective-permute-start | bytes 1179656 | tf_op jit(solution)/shard_map/ppermute | solution.py:366
  17.2 17.6 %collective-permute-start.7 = (bf16[400,512]{1,0:T(8,128)(2,1)S(1)}, bf16[400,512]{1,0:T(8,128)(2,1)S(1)}, u32[]{:S(2)}, u32[]{:S(2)}) collective-permute-start(bf16[400,512]{1,0:T(8,128)(2,1)S(1)} %arrange.1.kv0), channel_id=1, source_target_pairs={{0,8},{4,12},{8,16},{12,20},{16,24},{20,28},{24,32},{28,36},{32,40... | collective-permute-start | bytes 1228808 | tf_op jit(solution)/shard_map/ppermute | solution.py:377
  20.7 15.3 %collective-permute-start.6 = (bf16[400,512]{1,0:T(8,128)(2,1)S(1)}, bf16[400,512]{1,0:T(8,128)(2,1)S(1)}, u32[]{:S(2)}, u32[]{:S(2)}) collective-permute-start(bf16[400,512]{1,0:T(8,128)(2,1)S(1)} %arrange.1.kv0), channel_id=1, source_target_pairs={{0,4},{4,16},{8,12},{12,24},{16,20},{20,32},{24,28},{28,40},{32,36... | collective-permute-start | bytes 1228808 | tf_op jit(solution)/shard_map/ppermute | solution.py:377
  31.0 5.5 %copy-start.2 = (bf16[96,4096]{1,0:T(8,128)(2,1)S(1)}, bf16[96,4096]{1,0:T(8,128)(2,1)}, u32[]{:S(2)}) copy-start(bf16[96,4096]{1,0:T(8,128)(2,1)} %do_ref.1) | copy-start | bytes 2359300
  34.8 1.7 %collective-permute-start.8 = (bf16[400,512]{1,0:T(8,128)(2,1)S(1)}, bf16[400,512]{1,0:T(8,128)(2,1)S(1)}, u32[]{:S(2)}, u32[]{:S(2)}) collective-permute-start(bf16[400,512]{1,0:T(8,128)(2,1)S(1)} %collective-permute-done.7.kv_c), channel_id=1, source_target_pairs={{0,4},{4,0},{8,12},{12,8},{16,20},{20,16},{24,28},{28,24},{32,36},... | collective-permute-start | bytes 1228808 | tf_op jit(solution)/shard_map/ppermute | solution.py:377
  53.8 4.3 %collective-permute-start.12 = (bf16[384,512]{1,0:T(8,128)(2,1)S(1)}, bf16[384,512]{1,0:T(8,128)(2,1)S(1)}, u32[]{:S(2)}, u32[]{:S(2)}) collective-permute-start(bf16[384,512]{1,0:T(8,128)(2,1)S(1)} %get-tuple-element.52), channel_id=1, source_target_pairs={{0,4},{4,0},{8,12},{12,8},{16,20},{20,16},{24,28},{28,24},{32,36},... | collective-permute-start | bytes 1179656 | tf_op jit(solution)/shard_map/ppermute | solution.py:377
  54.1 21.0 %collective-permute-start.9 = (bf16[96,2048]{1,0:T(8,128)(2,1)S(1)}, bf16[96,2048]{1,0:T(8,128)(2,1)S(1)}, u32[]{:S(2)}, u32[]{:S(2)}) collective-permute-start(bf16[96,2048]{1,0:T(8,128)(2,1)S(1)} %get-tuple-element.45), channel_id=1, source_target_pairs={{0,1},{1,2},{2,3},{3,0},{4,5},{5,6},{6,7},{7,4},{8,9},{9,10},{10,1... | collective-permute-start | bytes 1179656 | tf_op jit(solution)/shard_map/ppermute | solution.py:366
  54.9 20.2 %collective-permute-start.10 = (bf16[96,2048]{1,0:T(8,128)(2,1)S(1)}, bf16[96,2048]{1,0:T(8,128)(2,1)S(1)}, u32[]{:S(2)}, u32[]{:S(2)}) collective-permute-start(bf16[96,2048]{1,0:T(8,128)(2,1)S(1)} %get-tuple-element.46), channel_id=1, source_target_pairs={{0,2},{1,3},{2,0},{3,1},{4,6},{5,7},{6,4},{7,5},{8,10},{9,11},{10,... | collective-permute-start | bytes 1179656 | tf_op jit(solution)/shard_map/ppermute | solution.py:366
  55.9 19.8 %collective-permute-start.11 = (bf16[96,2048]{1,0:T(8,128)(2,1)S(1)}, bf16[96,2048]{1,0:T(8,128)(2,1)S(1)}, u32[]{:S(2)}, u32[]{:S(2)}) collective-permute-start(bf16[96,2048]{1,0:T(8,128)(2,1)S(1)} %get-tuple-element.47), channel_id=1, source_target_pairs={{0,3},{1,0},{2,1},{3,2},{4,7},{5,4},{6,5},{7,6},{8,11},{9,8},{10,9... | collective-permute-start | bytes 1179656 | tf_op jit(solution)/shard_map/ppermute | solution.py:366
  58.3 17.4 %collective-permute-start.13 = (bf16[384,512]{1,0:T(8,128)(2,1)S(1)}, bf16[384,512]{1,0:T(8,128)(2,1)S(1)}, u32[]{:S(2)}, u32[]{:S(2)}) collective-permute-start(bf16[384,512]{1,0:T(8,128)(2,1)S(1)} %get-tuple-element.54), channel_id=1, source_target_pairs={{4,0},{12,8},{20,16},{16,4},{28,24},{24,12},{36,32},{32,20},{44,40... | collective-permute-start | bytes 1179656 | tf_op jit(solution)/shard_map/ppermute | solution.py:377
  60.2 15.5 %collective-permute-start.14 = (bf16[384,512]{1,0:T(8,128)(2,1)S(1)}, bf16[384,512]{1,0:T(8,128)(2,1)S(1)}, u32[]{:S(2)}, u32[]{:S(2)}) collective-permute-start(bf16[384,512]{1,0:T(8,128)(2,1)S(1)} %add_convert_fusion), channel_id=1, source_target_pairs={{8,0},{12,4},{16,8},{20,12},{24,16},{28,20},{32,24},{36,28},{40,32... | collective-permute-start | bytes 1179656 | tf_op jit(solution)/shard_map/ppermute | solution.py:377
  76.4 6.3 %collective-permute-start.15 = (bf16[96,512]{1,0:T(8,128)(2,1)S(1)}, bf16[96,512]{1,0:T(8,128)(2,1)S(1)}, u32[]{:S(2)}, u32[]{:S(2)}) collective-permute-start(bf16[96,512]{1,0:T(8,128)(2,1)S(1)} %get-tuple-element.57), channel_id=1, source_target_pairs={{0,1},{1,2},{2,3},{3,0},{4,5},{5,6},{6,7},{7,4},{8,9},{9,10},{10,1... | collective-permute-start | bytes 294920 | tf_op jit(solution)/shard_map/ppermute | solution.py:366
  77.4 8.0 %collective-permute-start.16 = (bf16[96,512]{1,0:T(8,128)(2,1)S(1)}, bf16[96,512]{1,0:T(8,128)(2,1)S(1)}, u32[]{:S(2)}, u32[]{:S(2)}) collective-permute-start(bf16[96,512]{1,0:T(8,128)(2,1)S(1)} %get-tuple-element.58), channel_id=1, source_target_pairs={{0,2},{1,3},{2,0},{3,1},{4,6},{5,7},{6,4},{7,5},{8,10},{9,11},{10,... | collective-permute-start | bytes 294920 | tf_op jit(solution)/shard_map/ppermute | solution.py:366
  80.6 4.8 %collective-permute-start.17 = (bf16[96,512]{1,0:T(8,128)(2,1)S(1)}, bf16[96,512]{1,0:T(8,128)(2,1)S(1)}, u32[]{:S(2)}, u32[]{:S(2)}) collective-permute-start(bf16[96,512]{1,0:T(8,128)(2,1)S(1)} %get-tuple-element.59), channel_id=1, source_target_pairs={{0,3},{1,0},{2,1},{3,2},{4,7},{5,4},{6,5},{7,6},{8,11},{9,8},{10,9... | collective-permute-start | bytes 294920 | tf_op jit(solution)/shard_map/ppermute | solution.py:366

commit v4 on v3

--- a/solution.py
+++ b/solution.py
@@ -78,7 +78,7 @@
 def cut(x, a, b):
     width = a.shape[1] // 8
     pieces = []
-    for p in range(1, 4):
+    for p in range(4):
         place = (x + p) % 4 * (2 * width)
         cuts = [lax.dynamic_slice_in_dim(src, place + g * width, width, 1) for g in range(2) for src in (a, b)]
         pieces.append(jnp.concatenate(cuts, 1))
@@ -110,33 +110,6 @@
         compiler_params=SMALL,
         name="unpack",
     )(x, *parts)
-
-
-def arrange_kernel(x_ref, k_ref, v_ref, r1, r2, r3, doc_ref, out_ref, sems):
-    make = copier(sems)
-    x = x_ref[0]
-    rows = pl.ds(pl.multiple_of(x * PART, PART), PART)
-    copies = [make(doc_ref, out_ref.at[pl.ds(ROWS, 16)])]
-    for g in range(2):
-        own = pl.multiple_of(x * (2 * HDIM) + g * HDIM, HDIM)
-        for n, ref in enumerate((k_ref, v_ref)):
-            copies.append(make(ref.at[:, pl.ds(own, HDIM)], out_ref.at[rows, pl.ds((2 * g + n) * HDIM, HDIM)]))
-    for p, ref in enumerate((r1, r2, r3)):
-        place = pl.multiple_of(lax.rem(x + 3 - p, 4) * PART, PART)
-        copies.append(make(ref, out_ref.at[pl.ds(place, PART)]))
-    run_copies(copies)
-
-
-def arrange(x, keys, values, received, docs):
-    return pl.pallas_call(
-        arrange_kernel,
-        in_specs=[SMEM] + [ANY] * 6,
-        out_specs=VMEM,
-        out_shape=struct((ROWS + 16, KVW), BF16),
-        scratch_shapes=[pltpu.SemaphoreType.DMA((8,))],
-        compiler_params=SMALL,
-        name="arrange",
-    )(x, keys, values, *received, docs)
 
 
 def dot(a, b, contract):
@@ -383,11 +356,15 @@
     doc_number = doc_ids + 1
     docs_low = jnp.pad(doc_number.astype(BF16)[None, :], ((0, 15), (0, KVW - ROWS)))
     docs = jnp.broadcast_to(doc_number.astype(F32)[None, :], (8, ROWS))
-    kv_received = [around(piece, p + 1) for p, piece in enumerate(cut(x, keys, values))]
+    kv_pieces = cut(x, keys, values)
+    kv_received = [around(kv_pieces[p], p) for p in (1, 2, 3)]
     q_pieces = pack(place, queries, out_grad)
     kv_received, q_pieces = lax.optimization_barrier((kv_received, q_pieces))
     q_received = [around(piece, p + 1) for p, piece in enumerate(q_pieces)]
-    kv0 = arrange(place, keys, values, kv_received, docs_low)
+    turn = [kv_received[2], kv_received[1], kv_received[0], kv_pieces[0]]
+    rows = jnp.stack(turn + turn[:3])
+    rows = lax.dynamic_slice_in_dim(rows, 3 - x, 4, 0).reshape(ROWS, KVW)
+    kv0 = jnp.concatenate([rows, docs_low], 0)
     kv_c = over_chips(kv0, [(0, 1, 0), (1, 1, 1)])
     kv_b = over_chips(kv0, [(0, 0, 1), (1, 2, 0)])
     kv_c, docs = lax.optimization_barrier((kv_c, arrived(docs, q_received, 40_000_000_000)))
@@ -397,7 +374,6 @@
     )
     back_a = over_chips(swap, [(0, 0, 1), (1, 0, 0)])
     near = (near + back_a.astype(F32)).astype(BF16)
-    near, far = lax.optimization_barrier((near, far))
     back_b = over_chips(far, [(1, 0, 0), (0, -2, 1)])
     back_c = over_chips(near, [(0, -1, 0), (1, -1, 1)])
     outs = [o0] + [around(piece, p) for p, piece in ((1, o1), (2, o2), (3, o3))]

time: 87.7 us -> 87 us (level)
  Pallas kernels: 23.6 us -> 22.5 us
  local copies, waits for them, and re-layouts: 2.16 us -> 1.18 us
  waiting for transfers between devices: 31 us -> 31.9 us
    ppermute x12, waiting for transfers between devices: 25.5 us -> 26.8 us  [around(): lax.ppermute(block, 'head', [(i, (i + distance) % 4) for i in range(4)])]
    unnamed x12 -> x11, local copies, waits for them, and re-layouts: 1.15 us -> 0.05 us
    pallas_call x1 -> x0, Pallas kernels: 1.07 us -> none  [arrange(): pl.pallas_call(arrange_kernel, in_specs=[SMEM] + [ANY] * 6, out_specs=VME...]
  transfers between devices with their start and end apart: 18 -> 18, of which waited for: 10 -> 13; matrix products, arithmetic and copies ran while one was open for 0% -> 0% of each run, Pallas kernels for 5% -> 3%
where the time goes in v4:
time: 87 us; the launch traced here: 86.8 us
  waiting for transfers between devices  31.9 us (37%)
  starting transfers between devices  29.7 us (34%)
  Pallas kernels  22.5 us (26%)
  local copies, waits for them, and re-layouts  1.18 us (1%)
  between operations  1.09 us (1%)
    ppermute x12, waiting for transfers between devices, around(): lax.ppermute(block, 'head', [(i, (i + distance) % 4) for i in range(4)])  26.8 us
    ppermute x12, starting transfers between devices, around(): lax.ppermute(block, 'head', [(i, (i + distance) % 4) for i in range(4)])  19.2 us
    pallas_call x1, Pallas kernels, attention(): pl.pallas_call(attention_kernel, in_specs=[SMEM] + [ANY] * 9 + [VMEM], ou...  17.3 us
    ppermute x6, starting transfers between devices, over_chips(): return lax.ppermute(block, ('chip', 'core'), pairs)  10.5 us
    ppermute x6, waiting for transfers between devices, over_chips(): return lax.ppermute(block, ('chip', 'core'), pairs)  5.11 us
    pallas_call x2, Pallas kernels, unpack(): pl.pallas_call(functools.partial(unpack_kernel, width), in_specs=[SMEM] +...  3.68 us
  transfers between devices with their start and end apart: 18, of which 13 were waited for; matrix products, arithmetic and copies ran while one was open for 0% of the time, Pallas kernels for 3%

profile of v4, /device:TPU:128, one launch (start us, length us, event | category | flops | bytes accessed | tf_op | source)
XLA Modules:
  0.0 86.8 jit_solution(4035887315875305901)
XLA Ops:
  0.6 0.0 copy-start.2
  0.6 0.0 copy-start.1
  0.7 0.0 copy-start
  0.7 1.1 %constant_dynamic-slice_fusion.3 = (bf16[96,128]{1,0:T(8,128)(2,1)S(1)}, bf16[96,128]{1,0:T(8,128)(2,1)S(1)}, bf16[96,128]{1,0:T(8,128)(2,1)S(1)}, bf16[96,128]{...) fusion(bf16[96,1024]{1,0:T(8,128)(2,1)} %param.7, ...), kind=kLoop, calls=%fused_computation.18 | loop fusion | bytes 786464 | tf_op jit(solution)/shard_map/dynamic_slice | solution.py:83
  1.8 1.6 %collective-permute-start = (bf16[96,512]{1,0:T(8,128)(2,1)S(1)}, bf16[96,512]{1,0:T(8,128)(2,1)S(1)}, u32[]{:S(2)}, u32[]{:S(2)}) collective-permute-start(bf16[96,512]{1,0:T(8,128)(2,1)S(1)} %pad_maximum_fusion), channel_id=1, source_target_pairs={{0,1},{1,2},{2,3},{3,0},{4,5},{5,6},{6,7},{7,4},{8,9},{9,10},{10,1... | collective-permute-start | bytes 294920 | tf_op jit(solution)/shard_map/ppermute | solution.py:339
  3.4 2.8 %collective-permute-start.1 = (bf16[96,512]{1,0:T(8,128)(2,1)S(1)}, bf16[96,512]{1,0:T(8,128)(2,1)S(1)}, u32[]{:S(2)}, u32[]{:S(2)}) collective-permute-start(bf16[96,512]{1,0:T(8,128)(2,1)S(1)} %pad_maximum_fusion.1), channel_id=1, source_target_pairs={{0,2},{1,3},{2,0},{3,1},{4,6},{5,7},{6,4},{7,5},{8,10},{9,11},{10,... | collective-permute-start | bytes 294920 | tf_op jit(solution)/shard_map/ppermute | solution.py:339
  6.3 1.5 %collective-permute-start.2 = (bf16[96,512]{1,0:T(8,128)(2,1)S(1)}, bf16[96,512]{1,0:T(8,128)(2,1)S(1)}, u32[]{:S(2)}, u32[]{:S(2)}) collective-permute-start(bf16[96,512]{1,0:T(8,128)(2,1)S(1)} %pad_maximum_fusion.2), channel_id=1, source_target_pairs={{0,3},{1,0},{2,1},{3,2},{4,7},{5,4},{6,5},{7,6},{8,11},{9,8},{10,9... | collective-permute-start | bytes 294920 | tf_op jit(solution)/shard_map/ppermute | solution.py:339
  7.8 0.0 copy-done.2
  7.8 0.1 pad_add_fusion.x_ref
  7.9 0.9 pack.1
  8.7 0.0 collective-permute-done
  8.7 2.0 %collective-permute-done.1 = bf16[96,512]{1,0:T(8,128)(2,1)S(1)} collective-permute-done((bf16[96,512]{1,0:T(8,128)(2,1)S(1)}, bf16[96,512]{1,0:T(8,128)(2,1)S(1)}, u32[]{:S(2)}, u32[]{:S(2)}) %collective-permute-start.1) | collective-permute-done | bytes 98336 | tf_op jit(solution)/shard_map/ppermute | solution.py:339
  10.8 0.2 collective-permute-done.2
  11.0 1.3 %collective-permute-start.3 = (bf16[96,2048]{1,0:T(8,128)(2,1)S(1)}, bf16[96,2048]{1,0:T(8,128)(2,1)S(1)}, u32[]{:S(2)}, u32[]{:S(2)}) collective-permute-start(bf16[96,2048]{1,0:T(8,128)(2,1)S(1)} %get-tuple-element.34), channel_id=1, source_target_pairs={{0,1},{1,2},{2,3},{3,0},{4,5},{5,6},{6,7},{7,4},{8,9},{9,10},{10,1... | collective-permute-start | bytes 1179656 | tf_op jit(solution)/shard_map/ppermute | solution.py:339
  12.3 2.8 %collective-permute-start.4 = (bf16[96,2048]{1,0:T(8,128)(2,1)S(1)}, bf16[96,2048]{1,0:T(8,128)(2,1)S(1)}, u32[]{:S(2)}, u32[]{:S(2)}) collective-permute-start(bf16[96,2048]{1,0:T(8,128)(2,1)S(1)} %get-tuple-element.35), channel_id=1, source_target_pairs={{0,2},{1,3},{2,0},{3,1},{4,6},{5,7},{6,4},{7,5},{8,10},{9,11},{10,... | collective-permute-start | bytes 1179656 | tf_op jit(solution)/shard_map/ppermute | solution.py:339
  15.1 1.1 %collective-permute-start.5 = (bf16[96,2048]{1,0:T(8,128)(2,1)S(1)}, bf16[96,2048]{1,0:T(8,128)(2,1)S(1)}, u32[]{:S(2)}, u32[]{:S(2)}) collective-permute-start(bf16[96,2048]{1,0:T(8,128)(2,1)S(1)} %get-tuple-element.36), channel_id=1, source_target_pairs={{0,3},{1,0},{2,1},{3,2},{4,7},{5,4},{6,5},{7,6},{8,11},{9,8},{10,9... | collective-permute-start | bytes 1179656 | tf_op jit(solution)/shard_map/ppermute | solution.py:339
  16.3 3.5 %collective-permute-start.7 = (bf16[400,512]{1,0:T(8,128)(2,1)S(1)}, bf16[400,512]{1,0:T(8,128)(2,1)S(1)}, u32[]{:S(2)}, u32[]{:S(2)}) collective-permute-start(bf16[400,512]{1,0:T(8,128)(2,1)S(1)} %fusion.1.kv0), channel_id=1, source_target_pairs={{0,8},{4,12},{8,16},{12,20},{16,24},{20,28},{24,32},{28,36},{32,40... | collective-permute-start | bytes 1228808 | tf_op jit(solution)/shard_map/ppermute | solution.py:350
  19.8 1.9 %collective-permute-start.6 = (bf16[400,512]{1,0:T(8,128)(2,1)S(1)}, bf16[400,512]{1,0:T(8,128)(2,1)S(1)}, u32[]{:S(2)}, u32[]{:S(2)}) collective-permute-start(bf16[400,512]{1,0:T(8,128)(2,1)S(1)} %fusion.1.kv0), channel_id=1, source_target_pairs={{0,4},{4,16},{8,12},{12,24},{16,20},{20,32},{24,28},{28,40},{32,36... | collective-permute-start | bytes 1228808 | tf_op jit(solution)/shard_map/ppermute | solution.py:350
  21.8 2.1 %collective-permute-done.3.refs_0_.q1 = bf16[96,2048]{1,0:T(8,128)(2,1)S(1)} collective-permute-done((bf16[96,2048]{1,0:T(8,128)(2,1)S(1)}, bf16[96,2048]{1,0:T(8,128)(2,1)S(1)}, u32[]{:S(2)}, u32[]{:S(2)}) %collective-permute-start.3) | collective-permute-done | bytes 393248 | tf_op jit(solution)/shard_map/ppermute | solution.py:339
  23.9 7.3 %collective-permute-done.4.refs_1_.q2 = bf16[96,2048]{1,0:T(8,128)(2,1)S(1)} collective-permute-done((bf16[96,2048]{1,0:T(8,128)(2,1)S(1)}, bf16[96,2048]{1,0:T(8,128)(2,1)S(1)}, u32[]{:S(2)}, u32[]{:S(2)}) %collective-permute-start.4) | collective-permute-done | bytes 393248 | tf_op jit(solution)/shard_map/ppermute | solution.py:339
  31.1 0.0 collective-permute-done.5.refs_2_.q3
  31.2 2.8 %collective-permute-done.7.kv_c = bf16[400,512]{1,0:T(8,128)(2,1)S(1)} collective-permute-done((bf16[400,512]{1,0:T(8,128)(2,1)S(1)}, bf16[400,512]{1,0:T(8,128)(2,1)S(1)}, u32[]{:S(2)}, u32[]{:S(2)}) %collective-permute-start.7) | collective-permute-done | bytes 409632 | tf_op jit(solution)/shard_map/ppermute | solution.py:350
  34.0 0.0 collective-permute-start.8
  34.0 1.2 %collective-permute-done.6.kv_b = bf16[400,512]{1,0:T(8,128)(2,1)S(1)} collective-permute-done((bf16[400,512]{1,0:T(8,128)(2,1)S(1)}, bf16[400,512]{1,0:T(8,128)(2,1)S(1)}, u32[]{:S(2)}, u32[]{:S(2)}) %collective-permute-start.6) | collective-permute-done | bytes 409632 | tf_op jit(solution)/shard_map/ppermute | solution.py:350
  35.2 0.6 collective-permute-done.8.kv_a
  35.7 17.3 %attention.1 = (bf16[96,2048]{1,0:T(8,128)(2,1)S(1)}, bf16[96,2048]{1,0:T(8,128)(2,1)S(1)}, bf16[96,2048]{1,0:T(8,128)(2,1)S(1)}, bf16[96,2048]{1,0:T(8,128)(2,1...) custom-call(s32[2]{0:T(128)S(1)} %pad_add_fusion.x_ref, ...), custom_call_target="tpu_custom_call" | custom-call | flops 8000000000 | bytes 8000000 | tf_op jit(solution)/shard_map/attention/pallas_call | solution.py:279
  53.0 0.2 collective-permute-start.13
  53.2 0.9 collective-permute-start.9
  54.1 1.0 %collective-permute-start.10 = (bf16[96,2048]{1,0:T(8,128)(2,1)S(1)}, bf16[96,2048]{1,0:T(8,128)(2,1)S(1)}, u32[]{:S(2)}, u32[]{:S(2)}) collective-permute-start(bf16[96,2048]{1,0:T(8,128)(2,1)S(1)} %get-tuple-element.44), channel_id=1, source_target_pairs={{0,2},{1,3},{2,0},{3,1},{4,6},{5,7},{6,4},{7,5},{8,10},{9,11},{10,... | collective-permute-start | bytes 1179656 | tf_op jit(solution)/shard_map/ppermute | solution.py:339
  55.1 2.3 %collective-permute-start.11 = (bf16[96,2048]{1,0:T(8,128)(2,1)S(1)}, bf16[96,2048]{1,0:T(8,128)(2,1)S(1)}, u32[]{:S(2)}, u32[]{:S(2)}) collective-permute-start(bf16[96,2048]{1,0:T(8,128)(2,1)S(1)} %get-tuple-element.45), channel_id=1, source_target_pairs={{0,3},{1,0},{2,1},{3,2},{4,7},{5,4},{6,5},{7,6},{8,11},{9,8},{10,9... | collective-permute-start | bytes 1179656 | tf_op jit(solution)/shard_map/ppermute | solution.py:339
  57.4 1.9 %collective-permute-start.12 = (bf16[384,512]{1,0:T(8,128)(2,1)S(1)}, bf16[384,512]{1,0:T(8,128)(2,1)S(1)}, u32[]{:S(2)}, u32[]{:S(2)}) collective-permute-start(bf16[384,512]{1,0:T(8,128)(2,1)S(1)} %get-tuple-element.49), channel_id=1, source_target_pairs={{4,0},{12,8},{20,16},{16,4},{28,24},{24,12},{36,32},{32,20},{44,40... | collective-permute-start | bytes 1179656 | tf_op jit(solution)/shard_map/ppermute | solution.py:350
  59.3 0.0 collective-permute-done.13
  59.3 0.1 add_convert_fusion
  59.4 3.0 %collective-permute-start.14 = (bf16[384,512]{1,0:T(8,128)(2,1)S(1)}, bf16[384,512]{1,0:T(8,128)(2,1)S(1)}, u32[]{:S(2)}, u32[]{:S(2)}) collective-permute-start(bf16[384,512]{1,0:T(8,128)(2,1)S(1)} %add_convert_fusion), channel_id=1, source_target_pairs={{8,0},{12,4},{16,8},{20,12},{24,16},{28,20},{32,24},{36,28},{40,32... | collective-permute-start | bytes 1179656 | tf_op jit(solution)/shard_map/ppermute | solution.py:350
  62.4 11.9 %collective-permute-done.9.refs_1_.refs_0_ = bf16[96,2048]{1,0:T(8,128)(2,1)S(1)} collective-permute-done((bf16[96,2048]{1,0:T(8,128)(2,1)S(1)}, bf16[96,2048]{1,0:T(8,128)(2,1)S(1)}, u32[]{:S(2)}, u32[]{:S(2)}) %collective-permute-start.9) | collective-permute-done | bytes 393248 | tf_op jit(solution)/shard_map/ppermute | solution.py:339
  74.3 0.0 collective-permute-done.10.refs_2_.refs_1_
  74.3 0.6 collective-permute-done.11.refs_3_.refs_2_
  74.9 0.0 collective-permute-done.12.b_ref
  74.9 0.5 collective-permute-done.14.c_ref
  75.5 0.7 total.1
  76.2 1.2 %collective-permute-start.15 = (bf16[96,512]{1,0:T(8,128)(2,1)S(1)}, bf16[96,512]{1,0:T(8,128)(2,1)S(1)}, u32[]{:S(2)}, u32[]{:S(2)}) collective-permute-start(bf16[96,512]{1,0:T(8,128)(2,1)S(1)} %get-tuple-element.53), channel_id=1, source_target_pairs={{0,1},{1,2},{2,3},{3,0},{4,5},{5,6},{6,7},{7,4},{8,9},{9,10},{10,1... | collective-permute-start | bytes 294920 | tf_op jit(solution)/shard_map/ppermute | solution.py:339
  77.4 2.4 %collective-permute-start.16 = (bf16[96,512]{1,0:T(8,128)(2,1)S(1)}, bf16[96,512]{1,0:T(8,128)(2,1)S(1)}, u32[]{:S(2)}, u32[]{:S(2)}) collective-permute-start(bf16[96,512]{1,0:T(8,128)(2,1)S(1)} %get-tuple-element.54), channel_id=1, source_target_pairs={{0,2},{1,3},{2,0},{3,1},{4,6},{5,7},{6,4},{7,5},{8,10},{9,11},{10,... | collective-permute-start | bytes 294920 | tf_op jit(solution)/shard_map/ppermute | solution.py:339
  79.8 0.4 collective-permute-start.17
  80.2 2.1 %unpack.2 = (bf16[96,4096]{1,0:T(8,128)(2,1)}, bf16[96,4096]{1,0:T(8,128)(2,1)}) custom-call(s32[2]{0:T(128)S(1)} %pad_add_fusion.x_ref, bf16[96,2048]{1,0:T(8,128)(2,1)S(1)} %get-tuple-element.42.refs_0_, bf16[96,2048]{1,0:T(8,128)(2,1)S(1)} %collective-permute-done.9.refs_1_.refs_0_, bf16[96,2048]{1,0:T(8,128)(2,1)S(1)} %collective-permute-done.10.refs_2_.refs_1_, ...), custom_call_target="tpu_custom_call" | custom-call | tf_op jit(solution)/shard_map/unpack/pallas_call | solution.py:104
  82.3 0.6 collective-permute-done.15.refs_1_
  82.9 1.7 %collective-permute-done.16.refs_2_ = bf16[96,512]{1,0:T(8,128)(2,1)S(1)} collective-permute-done((bf16[96,512]{1,0:T(8,128)(2,1)S(1)}, bf16[96,512]{1,0:T(8,128)(2,1)S(1)}, u32[]{:S(2)}, u32[]{:S(2)}) %collective-permute-start.16) | collective-permute-done | bytes 98336 | tf_op jit(solution)/shard_map/ppermute | solution.py:339
  84.6 0.4 collective-permute-done.17.refs_3_
  85.0 1.6 %unpack.3 = (bf16[96,1024]{1,0:T(8,128)(2,1)}, bf16[96,1024]{1,0:T(8,128)(2,1)}) custom-call(s32[2]{0:T(128)S(1)} %pad_add_fusion.x_ref, bf16[96,512]{1,0:T(8,128)(2,1)S(1)} %get-tuple-element.52.refs_0_, bf16[96,512]{1,0:T(8,128)(2,1)S(1)} %collective-permute-done.15.refs_1_, bf16[96,512]{1,0:T(8,128)(2,1)S(1)} %collective-permute-done.16.refs_2_, ...), custom_call_target="tpu_custom_call" | custom-call | tf_op jit(solution)/shard_map/unpack/pallas_call | solution.py:104
  (19 shorter events, 0.2 us)
Async XLA Ops:
  0.6 7.1 %copy-start.2 = (s32[384]{0:T(512)S(1)}, s32[384]{0:T(512)}, u32[]{:S(2)}) copy-start(s32[384]{0:T(512)} %param.9) | copy-start | bytes 4612
  0.6 7.2 %copy-start.1 = (bf16[96,4096]{1,0:T(8,128)(2,1)S(1)}, bf16[96,4096]{1,0:T(8,128)(2,1)}, u32[]{:S(2)}) copy-start(bf16[96,4096]{1,0:T(8,128)(2,1)} %do_ref.1) | copy-start | bytes 2359300
  0.7 7.2 %copy-start = (bf16[96,4096]{1,0:T(8,128)(2,1)S(1)}, bf16[96,4096]{1,0:T(8,128)(2,1)}, u32[]{:S(2)}) copy-start(bf16[96,4096]{1,0:T(8,128)(2,1)} %q_ref.1) | copy-start | bytes 2359300
  1.8 6.9 %collective-permute-start = (bf16[96,512]{1,0:T(8,128)(2,1)S(1)}, bf16[96,512]{1,0:T(8,128)(2,1)S(1)}, u32[]{:S(2)}, u32[]{:S(2)}) collective-permute-start(bf16[96,512]{1,0:T(8,128)(2,1)S(1)} %pad_maximum_fusion), channel_id=1, source_target_pairs={{0,1},{1,2},{2,3},{3,0},{4,5},{5,6},{6,7},{7,4},{8,9},{9,10},{10,1... | collective-permute-start | bytes 294920 | tf_op jit(solution)/shard_map/ppermute | solution.py:339
  3.4 7.3 %collective-permute-start.1 = (bf16[96,512]{1,0:T(8,128)(2,1)S(1)}, bf16[96,512]{1,0:T(8,128)(2,1)S(1)}, u32[]{:S(2)}, u32[]{:S(2)}) collective-permute-start(bf16[96,512]{1,0:T(8,128)(2,1)S(1)} %pad_maximum_fusion.1), channel_id=1, source_target_pairs={{0,2},{1,3},{2,0},{3,1},{4,6},{5,7},{6,4},{7,5},{8,10},{9,11},{10,... | collective-permute-start | bytes 294920 | tf_op jit(solution)/shard_map/ppermute | solution.py:339
  6.3 4.7 %collective-permute-start.2 = (bf16[96,512]{1,0:T(8,128)(2,1)S(1)}, bf16[96,512]{1,0:T(8,128)(2,1)S(1)}, u32[]{:S(2)}, u32[]{:S(2)}) collective-permute-start(bf16[96,512]{1,0:T(8,128)(2,1)S(1)} %pad_maximum_fusion.2), channel_id=1, source_target_pairs={{0,3},{1,0},{2,1},{3,2},{4,7},{5,4},{6,5},{7,6},{8,11},{9,8},{10,9... | collective-permute-start | bytes 294920 | tf_op jit(solution)/shard_map/ppermute | solution.py:339
  11.0 12.9 %collective-permute-start.3 = (bf16[96,2048]{1,0:T(8,128)(2,1)S(1)}, bf16[96,2048]{1,0:T(8,128)(2,1)S(1)}, u32[]{:S(2)}, u32[]{:S(2)}) collective-permute-start(bf16[96,2048]{1,0:T(8,128)(2,1)S(1)} %get-tuple-element.34), channel_id=1, source_target_pairs={{0,1},{1,2},{2,3},{3,0},{4,5},{5,6},{6,7},{7,4},{8,9},{9,10},{10,1... | collective-permute-start | bytes 1179656 | tf_op jit(solution)/shard_map/ppermute | solution.py:339
  12.3 18.8 %collective-permute-start.4 = (bf16[96,2048]{1,0:T(8,128)(2,1)S(1)}, bf16[96,2048]{1,0:T(8,128)(2,1)S(1)}, u32[]{:S(2)}, u32[]{:S(2)}) collective-permute-start(bf16[96,2048]{1,0:T(8,128)(2,1)S(1)} %get-tuple-element.35), channel_id=1, source_target_pairs={{0,2},{1,3},{2,0},{3,1},{4,6},{5,7},{6,4},{7,5},{8,10},{9,11},{10,... | collective-permute-start | bytes 1179656 | tf_op jit(solution)/shard_map/ppermute | solution.py:339
  15.1 16.1 %collective-permute-start.5 = (bf16[96,2048]{1,0:T(8,128)(2,1)S(1)}, bf16[96,2048]{1,0:T(8,128)(2,1)S(1)}, u32[]{:S(2)}, u32[]{:S(2)}) collective-permute-start(bf16[96,2048]{1,0:T(8,128)(2,1)S(1)} %get-tuple-element.36), channel_id=1, source_target_pairs={{0,3},{1,0},{2,1},{3,2},{4,7},{5,4},{6,5},{7,6},{8,11},{9,8},{10,9... | collective-permute-start | bytes 1179656 | tf_op jit(solution)/shard_map/ppermute | solution.py:339
  16.3 17.6 %collective-permute-start.7 = (bf16[400,512]{1,0:T(8,128)(2,1)S(1)}, bf16[400,512]{1,0:T(8,128)(2,1)S(1)}, u32[]{:S(2)}, u32[]{:S(2)}) collective-permute-start(bf16[400,512]{1,0:T(8,128)(2,1)S(1)} %fusion.1.kv0), channel_id=1, source_target_pairs={{0,8},{4,12},{8,16},{12,20},{16,24},{20,28},{24,32},{28,36},{32,40... | collective-permute-start | bytes 1228808 | tf_op jit(solution)/shard_map/ppermute | solution.py:350
  19.8 15.3 %collective-permute-start.6 = (bf16[400,512]{1,0:T(8,128)(2,1)S(1)}, bf16[400,512]{1,0:T(8,128)(2,1)S(1)}, u32[]{:S(2)}, u32[]{:S(2)}) collective-permute-start(bf16[400,512]{1,0:T(8,128)(2,1)S(1)} %fusion.1.kv0), channel_id=1, source_target_pairs={{0,4},{4,16},{8,12},{12,24},{16,20},{20,32},{24,28},{28,40},{32,36... | collective-permute-start | bytes 1228808 | tf_op jit(solution)/shard_map/ppermute | solution.py:350
  34.0 1.7 %collective-permute-start.8 = (bf16[400,512]{1,0:T(8,128)(2,1)S(1)}, bf16[400,512]{1,0:T(8,128)(2,1)S(1)}, u32[]{:S(2)}, u32[]{:S(2)}) collective-permute-start(bf16[400,512]{1,0:T(8,128)(2,1)S(1)} %collective-permute-done.7.kv_c), channel_id=1, source_target_pairs={{0,4},{4,0},{8,12},{12,8},{16,20},{20,16},{24,28},{28,24},{32,36},... | collective-permute-start | bytes 1228808 | tf_op jit(solution)/shard_map/ppermute | solution.py:350
  53.0 6.2 %collective-permute-start.13 = (bf16[384,512]{1,0:T(8,128)(2,1)S(1)}, bf16[384,512]{1,0:T(8,128)(2,1)S(1)}, u32[]{:S(2)}, u32[]{:S(2)}) collective-permute-start(bf16[384,512]{1,0:T(8,128)(2,1)S(1)} %get-tuple-element.51), channel_id=1, source_target_pairs={{0,4},{4,0},{8,12},{12,8},{16,20},{20,16},{24,28},{28,24},{32,36},... | collective-permute-start | bytes 1179656 | tf_op jit(solution)/shard_map/ppermute | solution.py:350
  53.2 21.0 %collective-permute-start.9 = (bf16[96,2048]{1,0:T(8,128)(2,1)S(1)}, bf16[96,2048]{1,0:T(8,128)(2,1)S(1)}, u32[]{:S(2)}, u32[]{:S(2)}) collective-permute-start(bf16[96,2048]{1,0:T(8,128)(2,1)S(1)} %get-tuple-element.43), channel_id=1, source_target_pairs={{0,1},{1,2},{2,3},{3,0},{4,5},{5,6},{6,7},{7,4},{8,9},{9,10},{10,1... | collective-permute-start | bytes 1179656 | tf_op jit(solution)/shard_map/ppermute | solution.py:339
  54.1 20.2 %collective-permute-start.10 = (bf16[96,2048]{1,0:T(8,128)(2,1)S(1)}, bf16[96,2048]{1,0:T(8,128)(2,1)S(1)}, u32[]{:S(2)}, u32[]{:S(2)}) collective-permute-start(bf16[96,2048]{1,0:T(8,128)(2,1)S(1)} %get-tuple-element.44), channel_id=1, source_target_pairs={{0,2},{1,3},{2,0},{3,1},{4,6},{5,7},{6,4},{7,5},{8,10},{9,11},{10,... | collective-permute-start | bytes 1179656 | tf_op jit(solution)/shard_map/ppermute | solution.py:339
  55.1 19.8 %collective-permute-start.11 = (bf16[96,2048]{1,0:T(8,128)(2,1)S(1)}, bf16[96,2048]{1,0:T(8,128)(2,1)S(1)}, u32[]{:S(2)}, u32[]{:S(2)}) collective-permute-start(bf16[96,2048]{1,0:T(8,128)(2,1)S(1)} %get-tuple-element.45), channel_id=1, source_target_pairs={{0,3},{1,0},{2,1},{3,2},{4,7},{5,4},{6,5},{7,6},{8,11},{9,8},{10,9... | collective-permute-start | bytes 1179656 | tf_op jit(solution)/shard_map/ppermute | solution.py:339
  57.4 17.6 %collective-permute-start.12 = (bf16[384,512]{1,0:T(8,128)(2,1)S(1)}, bf16[384,512]{1,0:T(8,128)(2,1)S(1)}, u32[]{:S(2)}, u32[]{:S(2)}) collective-permute-start(bf16[384,512]{1,0:T(8,128)(2,1)S(1)} %get-tuple-element.49), channel_id=1, source_target_pairs={{4,0},{12,8},{20,16},{16,4},{28,24},{24,12},{36,32},{32,20},{44,40... | collective-permute-start | bytes 1179656 | tf_op jit(solution)/shard_map/ppermute | solution.py:350
  59.4 16.0 %collective-permute-start.14 = (bf16[384,512]{1,0:T(8,128)(2,1)S(1)}, bf16[384,512]{1,0:T(8,128)(2,1)S(1)}, u32[]{:S(2)}, u32[]{:S(2)}) collective-permute-start(bf16[384,512]{1,0:T(8,128)(2,1)S(1)} %add_convert_fusion), channel_id=1, source_target_pairs={{8,0},{12,4},{16,8},{20,12},{24,16},{28,20},{32,24},{36,28},{40,32... | collective-permute-start | bytes 1179656 | tf_op jit(solution)/shard_map/ppermute | solution.py:350
  76.2 6.7 %collective-permute-start.15 = (bf16[96,512]{1,0:T(8,128)(2,1)S(1)}, bf16[96,512]{1,0:T(8,128)(2,1)S(1)}, u32[]{:S(2)}, u32[]{:S(2)}) collective-permute-start(bf16[96,512]{1,0:T(8,128)(2,1)S(1)} %get-tuple-element.53), channel_id=1, source_target_pairs={{0,1},{1,2},{2,3},{3,0},{4,5},{5,6},{6,7},{7,4},{8,9},{9,10},{10,1... | collective-permute-start | bytes 294920 | tf_op jit(solution)/shard_map/ppermute | solution.py:339
  77.4 7.2 %collective-permute-start.16 = (bf16[96,512]{1,0:T(8,128)(2,1)S(1)}, bf16[96,512]{1,0:T(8,128)(2,1)S(1)}, u32[]{:S(2)}, u32[]{:S(2)}) collective-permute-start(bf16[96,512]{1,0:T(8,128)(2,1)S(1)} %get-tuple-element.54), channel_id=1, source_target_pairs={{0,2},{1,3},{2,0},{3,1},{4,6},{5,7},{6,4},{7,5},{8,10},{9,11},{10,... | collective-permute-start | bytes 294920 | tf_op jit(solution)/shard_map/ppermute | solution.py:339
  79.8 5.2 %collective-permute-start.17 = (bf16[96,512]{1,0:T(8,128)(2,1)S(1)}, bf16[96,512]{1,0:T(8,128)(2,1)S(1)}, u32[]{:S(2)}, u32[]{:S(2)}) collective-permute-start(bf16[96,512]{1,0:T(8,128)(2,1)S(1)} %get-tuple-element.55), channel_id=1, source_target_pairs={{0,3},{1,0},{2,1},{3,2},{4,7},{5,4},{6,5},{7,6},{8,11},{9,8},{10,9... | collective-permute-start | bytes 294920 | tf_op jit(solution)/shard_map/ppermute | solution.py:339

commit v5 on v4

--- a/solution.py
+++ b/solution.py
@@ -264,8 +264,8 @@
         scales = (SCALE, 1.0, SCALE, 1.0)
         return jnp.concatenate([part[:, n * HDIM : (n + 1) * HDIM] * scales[n] for n in range(4)], 1)
 
-    own_ref[...] = gradient(3)
-    next_ref[...] = gradient(1)
+    own_ref[...] = gradient(3).astype(BF16)
+    next_ref[...] = gradient(1).astype(BF16)
     far_ref[...] = gradient(slot_b).astype(BF16)
     swap_ref[...] = gradient(slot_a).astype(BF16)
     for copy in copies:
@@ -274,13 +274,13 @@
 
 def attention(place, queries, out_grad, received, kv0, kv_b, kv_c, kv_a, docs):
     piece = struct((PART, 4 * QW), BF16)
-    grad, low_grad = struct((ROWS, KVW), F32), struct((ROWS, KVW), BF16)
+    low_grad = struct((ROWS, KVW), BF16)
     units, chunks, width = 2 * (ROWS // TILE), SPAN // KT, 4 * TILE
     return pl.pallas_call(
         attention_kernel,
         in_specs=[SMEM] + [ANY] * 9 + [VMEM],
         out_specs=[ANY] * 4 + [VMEM] * 4,
-        out_shape=[piece] * 4 + [grad, low_grad, low_grad, grad],
+        out_shape=[piece] * 4 + [low_grad] * 4,
         scratch_shapes=[
             pltpu.VMEM((WINDOW, KVW), BF16),
             pltpu.VMEM((4, 16, KVW), BF16),
@@ -321,7 +321,7 @@
     del docs_ref
     for p, out in enumerate(outs):
         rows = pl.ds(pl.multiple_of(lax.rem(x_ref[0] + p, 4) * PART, PART), PART)
-        out[...] = (own_ref[rows] + b_ref[rows].astype(F32) + c_ref[rows].astype(F32)).astype(BF16)
+        out[...] = (own_ref[rows].astype(F32) + b_ref[rows].astype(F32) + c_ref[rows].astype(F32)).astype(BF16)
 
 
 def total(place, own, back_b, back_c, docs):
@@ -373,7 +373,7 @@
         place, queries, out_grad, q_received, kv0, kv_b, kv_c, kv_a, docs
     )
     back_a = over_chips(swap, [(0, 0, 1), (1, 0, 0)])
-    near = (near + back_a.astype(F32)).astype(BF16)
+    near = (near.astype(F32) + back_a.astype(F32)).astype(BF16)
     back_b = over_chips(far, [(1, 0, 0), (0, -2, 1)])
     back_c = over_chips(near, [(0, -1, 0), (1, -1, 1)])
     outs = [o0] + [around(piece, p) for p, piece in ((1, o1), (2, o2), (3, o3))]

time: 87 us -> 86.9 us (level)
  no operation moved by 1% of the time
where the time goes in v5:
time: 86.9 us; the launch traced here: 86.7 us
  waiting for transfers between devices  32 us (37%)
  starting transfers between devices  29.7 us (34%)
  Pallas kernels  22.5 us (26%)
  local copies, waits for them, and re-layouts  1.18 us (1%)
  between operations  1.1 us (1%)
    ppermute x12, waiting for transfers between devices, around(): lax.ppermute(block, 'head', [(i, (i + distance) % 4) for i in range(4)])  26.9 us
    ppermute x12, starting transfers between devices, around(): lax.ppermute(block, 'head', [(i, (i + distance) % 4) for i in range(4)])  19.2 us
    pallas_call x1, Pallas kernels, attention(): pl.pallas_call(attention_kernel, in_specs=[SMEM] + [ANY] * 9 + [VMEM], ou...  17.3 us
    ppermute x6, starting transfers between devices, over_chips(): return lax.ppermute(block, ('chip', 'core'), pairs)  10.5 us
    ppermute x6, waiting for transfers between devices, over_chips(): return lax.ppermute(block, ('chip', 'core'), pairs)  5.11 us
    pallas_call x2, Pallas kernels, unpack(): pl.pallas_call(functools.partial(unpack_kernel, width), in_specs=[SMEM] +...  3.68 us
  transfers between devices with their start and end apart: 18, of which 13 were waited for; matrix products, arithmetic and copies ran while one was open for 0% of the time, Pallas kernels for 3%

profile of v5, /device:TPU:128, one launch (start us, length us, event | category | flops | bytes accessed | tf_op | source)
XLA Modules:
  0.0 86.7 jit_solution(3565004558778851763)
XLA Ops:
  0.6 0.0 copy-start.2
  0.6 0.0 copy-start.1
  0.7 0.0 copy-start
  0.7 1.1 %constant_dynamic-slice_fusion.3 = (bf16[96,128]{1,0:T(8,128)(2,1)S(1)}, bf16[96,128]{1,0:T(8,128)(2,1)S(1)}, bf16[96,128]{1,0:T(8,128)(2,1)S(1)}, bf16[96,128]{...) fusion(bf16[96,1024]{1,0:T(8,128)(2,1)} %param.7, ...), kind=kLoop, calls=%fused_computation.18 | loop fusion | bytes 786464 | tf_op jit(solution)/shard_map/dynamic_slice | solution.py:83
  1.8 1.6 %collective-permute-start = (bf16[96,512]{1,0:T(8,128)(2,1)S(1)}, bf16[96,512]{1,0:T(8,128)(2,1)S(1)}, u32[]{:S(2)}, u32[]{:S(2)}) collective-permute-start(bf16[96,512]{1,0:T(8,128)(2,1)S(1)} %pad_maximum_fusion), channel_id=1, source_target_pairs={{0,1},{1,2},{2,3},{3,0},{4,5},{5,6},{6,7},{7,4},{8,9},{9,10},{10,1... | collective-permute-start | bytes 294920 | tf_op jit(solution)/shard_map/ppermute | solution.py:339
  3.4 2.8 %collective-permute-start.1 = (bf16[96,512]{1,0:T(8,128)(2,1)S(1)}, bf16[96,512]{1,0:T(8,128)(2,1)S(1)}, u32[]{:S(2)}, u32[]{:S(2)}) collective-permute-start(bf16[96,512]{1,0:T(8,128)(2,1)S(1)} %pad_maximum_fusion.1), channel_id=1, source_target_pairs={{0,2},{1,3},{2,0},{3,1},{4,6},{5,7},{6,4},{7,5},{8,10},{9,11},{10,... | collective-permute-start | bytes 294920 | tf_op jit(solution)/shard_map/ppermute | solution.py:339
  6.3 1.5 %collective-permute-start.2 = (bf16[96,512]{1,0:T(8,128)(2,1)S(1)}, bf16[96,512]{1,0:T(8,128)(2,1)S(1)}, u32[]{:S(2)}, u32[]{:S(2)}) collective-permute-start(bf16[96,512]{1,0:T(8,128)(2,1)S(1)} %pad_maximum_fusion.2), channel_id=1, source_target_pairs={{0,3},{1,0},{2,1},{3,2},{4,7},{5,4},{6,5},{7,6},{8,11},{9,8},{10,9... | collective-permute-start | bytes 294920 | tf_op jit(solution)/shard_map/ppermute | solution.py:339
  7.8 0.0 copy-done.2
  7.8 0.1 pad_add_fusion.x_ref
  7.9 0.9 pack.1
  8.7 0.0 collective-permute-done
  8.7 2.0 %collective-permute-done.1 = bf16[96,512]{1,0:T(8,128)(2,1)S(1)} collective-permute-done((bf16[96,512]{1,0:T(8,128)(2,1)S(1)}, bf16[96,512]{1,0:T(8,128)(2,1)S(1)}, u32[]{:S(2)}, u32[]{:S(2)}) %collective-permute-start.1) | collective-permute-done | bytes 98336 | tf_op jit(solution)/shard_map/ppermute | solution.py:339
  10.8 0.2 collective-permute-done.2
  11.0 1.3 %collective-permute-start.3 = (bf16[96,2048]{1,0:T(8,128)(2,1)S(1)}, bf16[96,2048]{1,0:T(8,128)(2,1)S(1)}, u32[]{:S(2)}, u32[]{:S(2)}) collective-permute-start(bf16[96,2048]{1,0:T(8,128)(2,1)S(1)} %get-tuple-element.34), channel_id=1, source_target_pairs={{0,1},{1,2},{2,3},{3,0},{4,5},{5,6},{6,7},{7,4},{8,9},{9,10},{10,1... | collective-permute-start | bytes 1179656 | tf_op jit(solution)/shard_map/ppermute | solution.py:339
  12.3 2.8 %collective-permute-start.4 = (bf16[96,2048]{1,0:T(8,128)(2,1)S(1)}, bf16[96,2048]{1,0:T(8,128)(2,1)S(1)}, u32[]{:S(2)}, u32[]{:S(2)}) collective-permute-start(bf16[96,2048]{1,0:T(8,128)(2,1)S(1)} %get-tuple-element.35), channel_id=1, source_target_pairs={{0,2},{1,3},{2,0},{3,1},{4,6},{5,7},{6,4},{7,5},{8,10},{9,11},{10,... | collective-permute-start | bytes 1179656 | tf_op jit(solution)/shard_map/ppermute | solution.py:339
  15.1 1.1 %collective-permute-start.5 = (bf16[96,2048]{1,0:T(8,128)(2,1)S(1)}, bf16[96,2048]{1,0:T(8,128)(2,1)S(1)}, u32[]{:S(2)}, u32[]{:S(2)}) collective-permute-start(bf16[96,2048]{1,0:T(8,128)(2,1)S(1)} %get-tuple-element.36), channel_id=1, source_target_pairs={{0,3},{1,0},{2,1},{3,2},{4,7},{5,4},{6,5},{7,6},{8,11},{9,8},{10,9... | collective-permute-start | bytes 1179656 | tf_op jit(solution)/shard_map/ppermute | solution.py:339
  16.3 3.5 %collective-permute-start.7 = (bf16[400,512]{1,0:T(8,128)(2,1)S(1)}, bf16[400,512]{1,0:T(8,128)(2,1)S(1)}, u32[]{:S(2)}, u32[]{:S(2)}) collective-permute-start(bf16[400,512]{1,0:T(8,128)(2,1)S(1)} %fusion.1.kv0), channel_id=1, source_target_pairs={{0,8},{4,12},{8,16},{12,20},{16,24},{20,28},{24,32},{28,36},{32,40... | collective-permute-start | bytes 1228808 | tf_op jit(solution)/shard_map/ppermute | solution.py:350
  19.8 1.9 %collective-permute-start.6 = (bf16[400,512]{1,0:T(8,128)(2,1)S(1)}, bf16[400,512]{1,0:T(8,128)(2,1)S(1)}, u32[]{:S(2)}, u32[]{:S(2)}) collective-permute-start(bf16[400,512]{1,0:T(8,128)(2,1)S(1)} %fusion.1.kv0), channel_id=1, source_target_pairs={{0,4},{4,16},{8,12},{12,24},{16,20},{20,32},{24,28},{28,40},{32,36... | collective-permute-start | bytes 1228808 | tf_op jit(solution)/shard_map/ppermute | solution.py:350
  21.8 2.1 %collective-permute-done.3.refs_0_.q1 = bf16[96,2048]{1,0:T(8,128)(2,1)S(1)} collective-permute-done((bf16[96,2048]{1,0:T(8,128)(2,1)S(1)}, bf16[96,2048]{1,0:T(8,128)(2,1)S(1)}, u32[]{:S(2)}, u32[]{:S(2)}) %collective-permute-start.3) | collective-permute-done | bytes 393248 | tf_op jit(solution)/shard_map/ppermute | solution.py:339
  23.9 7.3 %collective-permute-done.4.refs_1_.q2 = bf16[96,2048]{1,0:T(8,128)(2,1)S(1)} collective-permute-done((bf16[96,2048]{1,0:T(8,128)(2,1)S(1)}, bf16[96,2048]{1,0:T(8,128)(2,1)S(1)}, u32[]{:S(2)}, u32[]{:S(2)}) %collective-permute-start.4) | collective-permute-done | bytes 393248 | tf_op jit(solution)/shard_map/ppermute | solution.py:339
  31.1 0.0 collective-permute-done.5.refs_2_.q3
  31.2 2.8 %collective-permute-done.7.kv_c = bf16[400,512]{1,0:T(8,128)(2,1)S(1)} collective-permute-done((bf16[400,512]{1,0:T(8,128)(2,1)S(1)}, bf16[400,512]{1,0:T(8,128)(2,1)S(1)}, u32[]{:S(2)}, u32[]{:S(2)}) %collective-permute-start.7) | collective-permute-done | bytes 409632 | tf_op jit(solution)/shard_map/ppermute | solution.py:350
  34.0 0.0 collective-permute-start.8
  34.0 1.2 %collective-permute-done.6.kv_b = bf16[400,512]{1,0:T(8,128)(2,1)S(1)} collective-permute-done((bf16[400,512]{1,0:T(8,128)(2,1)S(1)}, bf16[400,512]{1,0:T(8,128)(2,1)S(1)}, u32[]{:S(2)}, u32[]{:S(2)}) %collective-permute-start.6) | collective-permute-done | bytes 409632 | tf_op jit(solution)/shard_map/ppermute | solution.py:350
  35.2 0.6 collective-permute-done.8.kv_a
  35.7 17.3 %attention.1 = (bf16[96,2048]{1,0:T(8,128)(2,1)S(1)}, bf16[96,2048]{1,0:T(8,128)(2,1)S(1)}, bf16[96,2048]{1,0:T(8,128)(2,1)S(1)}, bf16[96,2048]{1,0:T(8,128)(2,1...) custom-call(s32[2]{0:T(128)S(1)} %pad_add_fusion.x_ref, ...), custom_call_target="tpu_custom_call" | custom-call | flops 8000000000 | bytes 8000000 | tf_op jit(solution)/shard_map/attention/pallas_call | solution.py:279
  53.0 0.2 collective-permute-start.13
  53.2 0.9 %collective-permute-start.9 = (bf16[96,2048]{1,0:T(8,128)(2,1)S(1)}, bf16[96,2048]{1,0:T(8,128)(2,1)S(1)}, u32[]{:S(2)}, u32[]{:S(2)}) collective-permute-start(bf16[96,2048]{1,0:T(8,128)(2,1)S(1)} %get-tuple-element.43), channel_id=1, source_target_pairs={{0,1},{1,2},{2,3},{3,0},{4,5},{5,6},{6,7},{7,4},{8,9},{9,10},{10,1... | collective-permute-start | bytes 1179656 | tf_op jit(solution)/shard_map/ppermute | solution.py:339
  54.1 1.0 %collective-permute-start.10 = (bf16[96,2048]{1,0:T(8,128)(2,1)S(1)}, bf16[96,2048]{1,0:T(8,128)(2,1)S(1)}, u32[]{:S(2)}, u32[]{:S(2)}) collective-permute-start(bf16[96,2048]{1,0:T(8,128)(2,1)S(1)} %get-tuple-element.44), channel_id=1, source_target_pairs={{0,2},{1,3},{2,0},{3,1},{4,6},{5,7},{6,4},{7,5},{8,10},{9,11},{10,... | collective-permute-start | bytes 1179656 | tf_op jit(solution)/shard_map/ppermute | solution.py:339
  55.1 2.3 %collective-permute-start.11 = (bf16[96,2048]{1,0:T(8,128)(2,1)S(1)}, bf16[96,2048]{1,0:T(8,128)(2,1)S(1)}, u32[]{:S(2)}, u32[]{:S(2)}) collective-permute-start(bf16[96,2048]{1,0:T(8,128)(2,1)S(1)} %get-tuple-element.45), channel_id=1, source_target_pairs={{0,3},{1,0},{2,1},{3,2},{4,7},{5,4},{6,5},{7,6},{8,11},{9,8},{10,9... | collective-permute-start | bytes 1179656 | tf_op jit(solution)/shard_map/ppermute | solution.py:339
  57.3 1.9 %collective-permute-start.12 = (bf16[384,512]{1,0:T(8,128)(2,1)S(1)}, bf16[384,512]{1,0:T(8,128)(2,1)S(1)}, u32[]{:S(2)}, u32[]{:S(2)}) collective-permute-start(bf16[384,512]{1,0:T(8,128)(2,1)S(1)} %get-tuple-element.49), channel_id=1, source_target_pairs={{4,0},{12,8},{20,16},{16,4},{28,24},{24,12},{36,32},{32,20},{44,40... | collective-permute-start | bytes 1179656 | tf_op jit(solution)/shard_map/ppermute | solution.py:350
  59.3 0.0 collective-permute-done.13
  59.3 0.1 add_convert_fusion
  59.4 3.0 %collective-permute-start.14 = (bf16[384,512]{1,0:T(8,128)(2,1)S(1)}, bf16[384,512]{1,0:T(8,128)(2,1)S(1)}, u32[]{:S(2)}, u32[]{:S(2)}) collective-permute-start(bf16[384,512]{1,0:T(8,128)(2,1)S(1)} %add_convert_fusion), channel_id=1, source_target_pairs={{8,0},{12,4},{16,8},{20,12},{24,16},{28,20},{32,24},{36,28},{40,32... | collective-permute-start | bytes 1179656 | tf_op jit(solution)/shard_map/ppermute | solution.py:350
  62.3 11.9 %collective-permute-done.9.refs_1_.refs_0_ = bf16[96,2048]{1,0:T(8,128)(2,1)S(1)} collective-permute-done((bf16[96,2048]{1,0:T(8,128)(2,1)S(1)}, bf16[96,2048]{1,0:T(8,128)(2,1)S(1)}, u32[]{:S(2)}, u32[]{:S(2)}) %collective-permute-start.9) | collective-permute-done | bytes 393248 | tf_op jit(solution)/shard_map/ppermute | solution.py:339
  74.3 0.0 collective-permute-done.10.refs_2_.refs_1_
  74.3 0.6 collective-permute-done.11.refs_3_.refs_2_
  74.9 0.0 collective-permute-done.12.b_ref
  74.9 0.5 collective-permute-done.14.c_ref
  75.4 0.7 total.1
  76.1 1.2 %collective-permute-start.15 = (bf16[96,512]{1,0:T(8,128)(2,1)S(1)}, bf16[96,512]{1,0:T(8,128)(2,1)S(1)}, u32[]{:S(2)}, u32[]{:S(2)}) collective-permute-start(bf16[96,512]{1,0:T(8,128)(2,1)S(1)} %get-tuple-element.53), channel_id=1, source_target_pairs={{0,1},{1,2},{2,3},{3,0},{4,5},{5,6},{6,7},{7,4},{8,9},{9,10},{10,1... | collective-permute-start | bytes 294920 | tf_op jit(solution)/shard_map/ppermute | solution.py:339
  77.4 2.4 %collective-permute-start.16 = (bf16[96,512]{1,0:T(8,128)(2,1)S(1)}, bf16[96,512]{1,0:T(8,128)(2,1)S(1)}, u32[]{:S(2)}, u32[]{:S(2)}) collective-permute-start(bf16[96,512]{1,0:T(8,128)(2,1)S(1)} %get-tuple-element.54), channel_id=1, source_target_pairs={{0,2},{1,3},{2,0},{3,1},{4,6},{5,7},{6,4},{7,5},{8,10},{9,11},{10,... | collective-permute-start | bytes 294920 | tf_op jit(solution)/shard_map/ppermute | solution.py:339
  79.8 0.4 collective-permute-start.17
  80.1 2.1 %unpack.2 = (bf16[96,4096]{1,0:T(8,128)(2,1)}, bf16[96,4096]{1,0:T(8,128)(2,1)}) custom-call(s32[2]{0:T(128)S(1)} %pad_add_fusion.x_ref, bf16[96,2048]{1,0:T(8,128)(2,1)S(1)} %get-tuple-element.42.refs_0_, bf16[96,2048]{1,0:T(8,128)(2,1)S(1)} %collective-permute-done.9.refs_1_.refs_0_, bf16[96,2048]{1,0:T(8,128)(2,1)S(1)} %collective-permute-done.10.refs_2_.refs_1_, ...), custom_call_target="tpu_custom_call" | custom-call | tf_op jit(solution)/shard_map/unpack/pallas_call | solution.py:104
  82.3 0.6 collective-permute-done.15.refs_1_
  82.9 1.7 %collective-permute-done.16.refs_2_ = bf16[96,512]{1,0:T(8,128)(2,1)S(1)} collective-permute-done((bf16[96,512]{1,0:T(8,128)(2,1)S(1)}, bf16[96,512]{1,0:T(8,128)(2,1)S(1)}, u32[]{:S(2)}, u32[]{:S(2)}) %collective-permute-start.16) | collective-permute-done | bytes 98336 | tf_op jit(solution)/shard_map/ppermute | solution.py:339
  84.6 0.4 collective-permute-done.17.refs_3_
  85.0 1.6 %unpack.3 = (bf16[96,1024]{1,0:T(8,128)(2,1)}, bf16[96,1024]{1,0:T(8,128)(2,1)}) custom-call(s32[2]{0:T(128)S(1)} %pad_add_fusion.x_ref, bf16[96,512]{1,0:T(8,128)(2,1)S(1)} %get-tuple-element.52.refs_0_, bf16[96,512]{1,0:T(8,128)(2,1)S(1)} %collective-permute-done.15.refs_1_, bf16[96,512]{1,0:T(8,128)(2,1)S(1)} %collective-permute-done.16.refs_2_, ...), custom_call_target="tpu_custom_call" | custom-call | tf_op jit(solution)/shard_map/unpack/pallas_call | solution.py:104
  (19 shorter events, 0.2 us)
Async XLA Ops:
  0.6 7.1 %copy-start.2 = (s32[384]{0:T(512)S(1)}, s32[384]{0:T(512)}, u32[]{:S(2)}) copy-start(s32[384]{0:T(512)} %param.9) | copy-start | bytes 4612
  0.6 7.2 %copy-start.1 = (bf16[96,4096]{1,0:T(8,128)(2,1)S(1)}, bf16[96,4096]{1,0:T(8,128)(2,1)}, u32[]{:S(2)}) copy-start(bf16[96,4096]{1,0:T(8,128)(2,1)} %do_ref.1) | copy-start | bytes 2359300
  0.7 7.2 %copy-start = (bf16[96,4096]{1,0:T(8,128)(2,1)S(1)}, bf16[96,4096]{1,0:T(8,128)(2,1)}, u32[]{:S(2)}) copy-start(bf16[96,4096]{1,0:T(8,128)(2,1)} %q_ref.1) | copy-start | bytes 2359300
  1.8 6.9 %collective-permute-start = (bf16[96,512]{1,0:T(8,128)(2,1)S(1)}, bf16[96,512]{1,0:T(8,128)(2,1)S(1)}, u32[]{:S(2)}, u32[]{:S(2)}) collective-permute-start(bf16[96,512]{1,0:T(8,128)(2,1)S(1)} %pad_maximum_fusion), channel_id=1, source_target_pairs={{0,1},{1,2},{2,3},{3,0},{4,5},{5,6},{6,7},{7,4},{8,9},{9,10},{10,1... | collective-permute-start | bytes 294920 | tf_op jit(solution)/shard_map/ppermute | solution.py:339
  3.4 7.3 %collective-permute-start.1 = (bf16[96,512]{1,0:T(8,128)(2,1)S(1)}, bf16[96,512]{1,0:T(8,128)(2,1)S(1)}, u32[]{:S(2)}, u32[]{:S(2)}) collective-permute-start(bf16[96,512]{1,0:T(8,128)(2,1)S(1)} %pad_maximum_fusion.1), channel_id=1, source_target_pairs={{0,2},{1,3},{2,0},{3,1},{4,6},{5,7},{6,4},{7,5},{8,10},{9,11},{10,... | collective-permute-start | bytes 294920 | tf_op jit(solution)/shard_map/ppermute | solution.py:339
  6.3 4.7 %collective-permute-start.2 = (bf16[96,512]{1,0:T(8,128)(2,1)S(1)}, bf16[96,512]{1,0:T(8,128)(2,1)S(1)}, u32[]{:S(2)}, u32[]{:S(2)}) collective-permute-start(bf16[96,512]{1,0:T(8,128)(2,1)S(1)} %pad_maximum_fusion.2), channel_id=1, source_target_pairs={{0,3},{1,0},{2,1},{3,2},{4,7},{5,4},{6,5},{7,6},{8,11},{9,8},{10,9... | collective-permute-start | bytes 294920 | tf_op jit(solution)/shard_map/ppermute | solution.py:339
  11.0 12.9 %collective-permute-start.3 = (bf16[96,2048]{1,0:T(8,128)(2,1)S(1)}, bf16[96,2048]{1,0:T(8,128)(2,1)S(1)}, u32[]{:S(2)}, u32[]{:S(2)}) collective-permute-start(bf16[96,2048]{1,0:T(8,128)(2,1)S(1)} %get-tuple-element.34), channel_id=1, source_target_pairs={{0,1},{1,2},{2,3},{3,0},{4,5},{5,6},{6,7},{7,4},{8,9},{9,10},{10,1... | collective-permute-start | bytes 1179656 | tf_op jit(solution)/shard_map/ppermute | solution.py:339
  12.3 18.8 %collective-permute-start.4 = (bf16[96,2048]{1,0:T(8,128)(2,1)S(1)}, bf16[96,2048]{1,0:T(8,128)(2,1)S(1)}, u32[]{:S(2)}, u32[]{:S(2)}) collective-permute-start(bf16[96,2048]{1,0:T(8,128)(2,1)S(1)} %get-tuple-element.35), channel_id=1, source_target_pairs={{0,2},{1,3},{2,0},{3,1},{4,6},{5,7},{6,4},{7,5},{8,10},{9,11},{10,... | collective-permute-start | bytes 1179656 | tf_op jit(solution)/shard_map/ppermute | solution.py:339
  15.1 16.1 %collective-permute-start.5 = (bf16[96,2048]{1,0:T(8,128)(2,1)S(1)}, bf16[96,2048]{1,0:T(8,128)(2,1)S(1)}, u32[]{:S(2)}, u32[]{:S(2)}) collective-permute-start(bf16[96,2048]{1,0:T(8,128)(2,1)S(1)} %get-tuple-element.36), channel_id=1, source_target_pairs={{0,3},{1,0},{2,1},{3,2},{4,7},{5,4},{6,5},{7,6},{8,11},{9,8},{10,9... | collective-permute-start | bytes 1179656 | tf_op jit(solution)/shard_map/ppermute | solution.py:339
  16.3 17.6 %collective-permute-start.7 = (bf16[400,512]{1,0:T(8,128)(2,1)S(1)}, bf16[400,512]{1,0:T(8,128)(2,1)S(1)}, u32[]{:S(2)}, u32[]{:S(2)}) collective-permute-start(bf16[400,512]{1,0:T(8,128)(2,1)S(1)} %fusion.1.kv0), channel_id=1, source_target_pairs={{0,8},{4,12},{8,16},{12,20},{16,24},{20,28},{24,32},{28,36},{32,40... | collective-permute-start | bytes 1228808 | tf_op jit(solution)/shard_map/ppermute | solution.py:350
  19.8 15.3 %collective-permute-start.6 = (bf16[400,512]{1,0:T(8,128)(2,1)S(1)}, bf16[400,512]{1,0:T(8,128)(2,1)S(1)}, u32[]{:S(2)}, u32[]{:S(2)}) collective-permute-start(bf16[400,512]{1,0:T(8,128)(2,1)S(1)} %fusion.1.kv0), channel_id=1, source_target_pairs={{0,4},{4,16},{8,12},{12,24},{16,20},{20,32},{24,28},{28,40},{32,36... | collective-permute-start | bytes 1228808 | tf_op jit(solution)/shard_map/ppermute | solution.py:350
  34.0 1.7 %collective-permute-start.8 = (bf16[400,512]{1,0:T(8,128)(2,1)S(1)}, bf16[400,512]{1,0:T(8,128)(2,1)S(1)}, u32[]{:S(2)}, u32[]{:S(2)}) collective-permute-start(bf16[400,512]{1,0:T(8,128)(2,1)S(1)} %collective-permute-done.7.kv_c), channel_id=1, source_target_pairs={{0,4},{4,0},{8,12},{12,8},{16,20},{20,16},{24,28},{28,24},{32,36},... | collective-permute-start | bytes 1228808 | tf_op jit(solution)/shard_map/ppermute | solution.py:350
  53.0 6.2 %collective-permute-start.13 = (bf16[384,512]{1,0:T(8,128)(2,1)S(1)}, bf16[384,512]{1,0:T(8,128)(2,1)S(1)}, u32[]{:S(2)}, u32[]{:S(2)}) collective-permute-start(bf16[384,512]{1,0:T(8,128)(2,1)S(1)} %get-tuple-element.51), channel_id=1, source_target_pairs={{0,4},{4,0},{8,12},{12,8},{16,20},{20,16},{24,28},{28,24},{32,36},... | collective-permute-start | bytes 1179656 | tf_op jit(solution)/shard_map/ppermute | solution.py:350
  53.2 21.0 %collective-permute-start.9 = (bf16[96,2048]{1,0:T(8,128)(2,1)S(1)}, bf16[96,2048]{1,0:T(8,128)(2,1)S(1)}, u32[]{:S(2)}, u32[]{:S(2)}) collective-permute-start(bf16[96,2048]{1,0:T(8,128)(2,1)S(1)} %get-tuple-element.43), channel_id=1, source_target_pairs={{0,1},{1,2},{2,3},{3,0},{4,5},{5,6},{6,7},{7,4},{8,9},{9,10},{10,1... | collective-permute-start | bytes 1179656 | tf_op jit(solution)/shard_map/ppermute | solution.py:339
  54.1 20.2 %collective-permute-start.10 = (bf16[96,2048]{1,0:T(8,128)(2,1)S(1)}, bf16[96,2048]{1,0:T(8,128)(2,1)S(1)}, u32[]{:S(2)}, u32[]{:S(2)}) collective-permute-start(bf16[96,2048]{1,0:T(8,128)(2,1)S(1)} %get-tuple-element.44), channel_id=1, source_target_pairs={{0,2},{1,3},{2,0},{3,1},{4,6},{5,7},{6,4},{7,5},{8,10},{9,11},{10,... | collective-permute-start | bytes 1179656 | tf_op jit(solution)/shard_map/ppermute | solution.py:339
  55.1 19.8 %collective-permute-start.11 = (bf16[96,2048]{1,0:T(8,128)(2,1)S(1)}, bf16[96,2048]{1,0:T(8,128)(2,1)S(1)}, u32[]{:S(2)}, u32[]{:S(2)}) collective-permute-start(bf16[96,2048]{1,0:T(8,128)(2,1)S(1)} %get-tuple-element.45), channel_id=1, source_target_pairs={{0,3},{1,0},{2,1},{3,2},{4,7},{5,4},{6,5},{7,6},{8,11},{9,8},{10,9... | collective-permute-start | bytes 1179656 | tf_op jit(solution)/shard_map/ppermute | solution.py:339
  57.3 17.6 %collective-permute-start.12 = (bf16[384,512]{1,0:T(8,128)(2,1)S(1)}, bf16[384,512]{1,0:T(8,128)(2,1)S(1)}, u32[]{:S(2)}, u32[]{:S(2)}) collective-permute-start(bf16[384,512]{1,0:T(8,128)(2,1)S(1)} %get-tuple-element.49), channel_id=1, source_target_pairs={{4,0},{12,8},{20,16},{16,4},{28,24},{24,12},{36,32},{32,20},{44,40... | collective-permute-start | bytes 1179656 | tf_op jit(solution)/shard_map/ppermute | solution.py:350
  59.4 16.1 %collective-permute-start.14 = (bf16[384,512]{1,0:T(8,128)(2,1)S(1)}, bf16[384,512]{1,0:T(8,128)(2,1)S(1)}, u32[]{:S(2)}, u32[]{:S(2)}) collective-permute-start(bf16[384,512]{1,0:T(8,128)(2,1)S(1)} %add_convert_fusion), channel_id=1, source_target_pairs={{8,0},{12,4},{16,8},{20,12},{24,16},{28,20},{32,24},{36,28},{40,32... | collective-permute-start | bytes 1179656 | tf_op jit(solution)/shard_map/ppermute | solution.py:350
  76.1 6.7 %collective-permute-start.15 = (bf16[96,512]{1,0:T(8,128)(2,1)S(1)}, bf16[96,512]{1,0:T(8,128)(2,1)S(1)}, u32[]{:S(2)}, u32[]{:S(2)}) collective-permute-start(bf16[96,512]{1,0:T(8,128)(2,1)S(1)} %get-tuple-element.53), channel_id=1, source_target_pairs={{0,1},{1,2},{2,3},{3,0},{4,5},{5,6},{6,7},{7,4},{8,9},{9,10},{10,1... | collective-permute-start | bytes 294920 | tf_op jit(solution)/shard_map/ppermute | solution.py:339
  77.4 7.2 %collective-permute-start.16 = (bf16[96,512]{1,0:T(8,128)(2,1)S(1)}, bf16[96,512]{1,0:T(8,128)(2,1)S(1)}, u32[]{:S(2)}, u32[]{:S(2)}) collective-permute-start(bf16[96,512]{1,0:T(8,128)(2,1)S(1)} %get-tuple-element.54), channel_id=1, source_target_pairs={{0,2},{1,3},{2,0},{3,1},{4,6},{5,7},{6,4},{7,5},{8,10},{9,11},{10,... | collective-permute-start | bytes 294920 | tf_op jit(solution)/shard_map/ppermute | solution.py:339
  79.8 5.2 %collective-permute-start.17 = (bf16[96,512]{1,0:T(8,128)(2,1)S(1)}, bf16[96,512]{1,0:T(8,128)(2,1)S(1)}, u32[]{:S(2)}, u32[]{:S(2)}) collective-permute-start(bf16[96,512]{1,0:T(8,128)(2,1)S(1)} %get-tuple-element.55), channel_id=1, source_target_pairs={{0,3},{1,0},{2,1},{3,2},{4,7},{5,4},{6,5},{7,6},{8,11},{9,8},{10,9... | collective-permute-start | bytes 294920 | tf_op jit(solution)/shard_map/ppermute | solution.py:339
